TPU v7x, 32 devices: a whole 2x2x4 slice. The times are simulated.
32 devices in a mesh: rep: 2 (over x), grp: 4 (over z), tp: 4 (over y, core).
Axes of the slice: x: 2, y: 2, z: 4, core: 2. Of those that a mesh axis runs over, the one named last changes fastest.
Arguments:
- x_in: bfloat16 [4, 8, 128, 1280], P(None, ('rep', 'grp'), None, 'tp'), parts along dimension 1, may hold values from -6 to 6
- taps: bfloat16 [4, 8, 128, 6400], P(None, ('rep', 'grp'), None, 'tp'), parts along dimension 1, may hold values from -6 to 6
- ln_gain: float32 [1280], replicated, may hold values from 0.1 to 1.9
- ln_bias: float32 [1280], replicated, may hold values from -3 to 3
- w_up: bfloat16 [1280, 5120], P(None, 'tp'), may hold values from -0.15625 to 0.15625
- b_up: float32 [5120], P('tp'), may hold values from -3 to 3
- w_down: bfloat16 [5120, 1280], P('tp'), may hold values from -0.078125 to 0.078125
- b_down: float32 [1280], P('tp'), may hold values from -3 to 3
- kv_w_out: bfloat16 [1280, 2048], P('tp'), may hold values from -0.0625 to 0.0625
- kv_w_taps: bfloat16 [6400, 2048], P('tp'), may hold values from -0.09375 to 0.09375
- k_gain: float32 [128], replicated, may hold values from 1 to 2.5
- q_gain: float32 [128], replicated, may hold values from 1 to 2.5
- queries: bfloat16 [4096, 8192], P(('rep', 'grp'), 'tp'), parts along dimension 0, may hold values from -6 to 6
- tiles_per_request: int32 [16], P('rep'), parts along dimension 0, may hold values from 1 to 4, as said below
- owner: int32 [16], P('rep'), parts along dimension 0, may hold values from 0 to 3, as said below
- text_per_request: int32 [16], P('rep'), parts along dimension 0, may hold values from 64 to 256, as said below
Outputs:
- attended: bfloat16 [4096, 8192], P(('rep', 'grp'), 'tp'), parts along dimension 0
There are 2 independent parts, one for each index of `rep`. A program takes and returns all parts, laid end to end along the dimension named above; an argument that names none is the same for every part. Nothing has to cross between parts.
Inputs may be any that keep to these rules, and one draw needn't show every extreme that they name: `owner`: each group owns exactly 2 requests. `tiles_per_request`: the tiles of all requests sum to 16; the tiles of one group's requests sum to at most 8, and some group has exactly 8. `text_per_request`: the text tokens of one group's requests sum to at most 512, and some group has exactly 512.
All inputs are finite; a program needn't handle non-finite values.
Results may differ from a plain program's by a relative error of at most 0.04.
Values may be sent and summed in bfloat16 or wider, within the bound.
No kernel may reach another device: no remote copies, remote signals or barrier semaphores. Data moves between devices by JAX's collectives and lax.ppermute only.
A program may use at most 128 MiB of HBM per device.

v0:
```python
import jax
import jax.numpy as jnp
from jax import lax
from jax.sharding import PartitionSpec as P

KVH = 8
HD = 128
MAXT = 4
REQ_G = 2


epsilon = 1e-05


def layer_norm(row_block, ln_gain, ln_bias):
    values = row_block.astype(jnp.float32)
    average = jnp.mean(values, axis=-1, keepdims=True)
    centered = values - average
    variance = jnp.mean(centered * centered, axis=-1, keepdims=True)
    return (centered * lax.rsqrt(variance + epsilon) * ln_gain + ln_bias).astype(jnp.bfloat16)


def head_norm(values, head_gain):
    square = jnp.mean(values * values, axis=-1, keepdims=True)
    return values * lax.rsqrt(square + epsilon) * head_gain


def group_layout(tiles_per_request, owner, text_per_request, group_count):
    request_count = owner.shape[0]
    request_ids = jnp.arange(request_count, dtype=jnp.int32)
    group_ids = jnp.arange(group_count, dtype=jnp.int32)
    member = owner[None, :] == group_ids[:, None]
    first_req = jnp.min(jnp.where(member, request_ids[None, :], request_count), axis=1)
    second_req = jnp.max(jnp.where(member, request_ids[None, :], -1), axis=1)
    pick_first = request_ids[None, :] == first_req[:, None]
    pick_second = request_ids[None, :] == second_req[:, None]
    tiles_first = jnp.sum(jnp.where(pick_first, tiles_per_request[None, :], 0), axis=1)
    tiles_second = jnp.sum(jnp.where(pick_second, tiles_per_request[None, :], 0), axis=1)
    text_first = jnp.sum(jnp.where(pick_first, text_per_request[None, :], 0), axis=1)
    text_second = jnp.sum(jnp.where(pick_second, text_per_request[None, :], 0), axis=1)
    tiles_both = tiles_first + tiles_second
    text_both = text_first + text_second
    offsets = jnp.cumsum(tiles_both) - tiles_both
    return (tiles_first, tiles_both, offsets, text_first, text_both)


def slot_label(position, first_count, both_count):
    return jnp.where(position < first_count, 0, jnp.where(position < both_count, 1, -1)).astype(
        jnp.int32
    )


def reduce_heads(partial_value, tp_count, tp_index):
    own_width = max(1, KVH // tp_count) * 2 * HD
    summed = lax.psum(partial_value.astype(jnp.bfloat16), "tp").astype(jnp.float32)
    start = tp_index * KVH // tp_count * (2 * HD)
    own_part = lax.dynamic_slice_in_dim(summed, start, own_width, 1)
    return own_part


def finish_heads(own_part, k_gain):
    row_count = own_part.shape[0]
    shaped = own_part.reshape(row_count, -1, 2, HD)
    key_rows = head_norm(shaped[:, :, 0, :], k_gain).astype(jnp.bfloat16)
    value_rows = shaped[:, :, 1, :].astype(jnp.bfloat16)
    return (key_rows, value_rows)


def local(
    x_in,
    taps,
    ln_gain,
    ln_bias,
    w_up,
    b_up,
    w_down,
    b_down,
    kv_w_out,
    kv_w_taps,
    k_gain,
    q_gain,
    queries,
    tiles_per_request,
    owner,
    text_per_request,
):
    group_count = lax.axis_size("grp")
    tp_count = lax.axis_size("tp")
    group_index = lax.axis_index("grp")
    tp_index = lax.axis_index("tp")
    tiles_local, _, tile_rows, channel_share = x_in.shape
    tap_share = taps.shape[3]
    local_rows = tiles_local * tile_rows
    token_rows = x_in.reshape(local_rows, channel_share)
    tap_rows = taps.reshape(local_rows, tap_share)
    full_rows = lax.all_gather(token_rows, "tp", axis=1, tiled=True)
    normed = layer_norm(full_rows, ln_gain, ln_bias)
    hidden = jax.nn.gelu(
        jnp.dot(normed, w_up, preferred_element_type=jnp.float32) + b_up, approximate=False
    ).astype(jnp.bfloat16)
    mlp_terms = jnp.dot(hidden, w_down, preferred_element_type=jnp.float32)
    mlp_share = lax.psum_scatter(
        mlp_terms.astype(jnp.bfloat16), "tp", scatter_dimension=1, tiled=True
    ).astype(jnp.float32)
    encoded = (token_rows.astype(jnp.float32) + mlp_share + b_down).astype(jnp.bfloat16)
    tiles_first, tiles_both, offsets, text_first, text_both = group_layout(
        tiles_per_request, owner, text_per_request, group_count
    )
    slot_count = (REQ_G * MAXT + group_count - 1) // group_count
    slot_ids = jnp.arange(slot_count, dtype=jnp.int32)
    lane = (group_index - offsets) % group_count
    position = slot_ids[:, None] * group_count + lane[None, :]
    send_live = (position < tiles_both[None, :]).reshape(-1)
    local_slot = jnp.clip((offsets[None, :] + position) // group_count, 0, tiles_local - 1).reshape(
        -1
    )
    my_offset = offsets[group_index]

    def pack(payload):
        picked = jnp.take(payload, local_slot, axis=0)
        live_shape = (send_live.shape[0],) + (1,) * (picked.ndim - 1)
        picked = jnp.where(send_live.reshape(live_shape), picked, jnp.zeros((), picked.dtype))
        return picked.reshape((slot_count, group_count) + payload.shape[1:])

    def unpack(received):
        rolled = jnp.roll(received, -my_offset, axis=1)
        return rolled.reshape((slot_count * group_count * tile_rows,) + received.shape[3:])

    partial_value = jnp.dot(encoded, kv_w_out, preferred_element_type=jnp.float32) + jnp.dot(
        tap_rows, kv_w_taps, preferred_element_type=jnp.float32
    )
    local_keys, local_values = finish_heads(reduce_heads(partial_value, tp_count, tp_index), k_gain)
    head_count = local_keys.shape[1]
    sent_keys = pack(local_keys.reshape(tiles_local, tile_rows, head_count, HD))
    sent_values = pack(local_values.reshape(tiles_local, tile_rows, head_count, HD))
    got_keys, got_values = (
        lax.all_to_all(sent_keys, "grp", split_axis=1, concat_axis=1, tiled=True),
        lax.all_to_all(sent_values, "grp", split_axis=1, concat_axis=1, tiled=True),
    )
    key_rows = unpack(got_keys)
    value_rows = unpack(got_values)
    key_slots = jnp.arange(slot_count * group_count, dtype=jnp.int32)
    key_label = jnp.repeat(
        slot_label(key_slots, tiles_first[group_index], tiles_both[group_index]), tile_rows
    )
    text_rows, query_width = queries.shape
    text_label = slot_label(
        jnp.arange(text_rows, dtype=jnp.int32), text_first[group_index], text_both[group_index]
    )
    head_count = key_rows.shape[1]
    query_heads = query_width // HD
    query_view = queries.reshape(text_rows, head_count, query_heads // head_count, HD).astype(
        jnp.float32
    )
    query_rows = head_norm(query_view, q_gain).astype(jnp.bfloat16)
    block_rows = min(512, text_rows)
    block_count = text_rows // block_rows
    scale = 1.0 / float(HD) ** 0.5

    def attend(item):
        query_block, label_block = item
        scores = (
            jnp.einsum("tkgd,skd->tkgs", query_block, key_rows, preferred_element_type=jnp.float32)
            * scale
        )
        allowed = (label_block[:, None] == key_label[None, :]) & (label_block[:, None] >= 0)
        weights = jnp.where(allowed[:, None, None, :], jnp.exp(scores), 0.0)
        total = jnp.sum(weights, axis=-1, keepdims=True)
        live_rows = (label_block >= 0)[:, None, None, None]
        probs = jnp.where(live_rows, weights / jnp.where(live_rows, total, 1.0), 0.0).astype(
            jnp.bfloat16
        )
        result = jnp.einsum("tkgs,skd->tkgd", probs, value_rows, preferred_element_type=jnp.float32)
        return result.astype(jnp.bfloat16).reshape(block_rows, query_width)

    blocks_out = lax.map(
        attend,
        (
            query_rows.reshape(block_count, block_rows, head_count, query_heads // head_count, HD),
            text_label.reshape(block_count, block_rows),
        ),
    )
    return blocks_out.reshape(text_rows, query_width)


def solution(mesh):
    in_specs = (
        P(None, ("rep", "grp"), None, "tp"),
        P(None, ("rep", "grp"), None, "tp"),
        P(),
        P(),
        P(None, "tp"),
        P("tp"),
        P("tp", None),
        P("tp"),
        P("tp", None),
        P("tp", None),
        P(),
        P(),
        P(("rep", "grp"), "tp"),
        P("rep"),
        P("rep"),
        P("rep"),
    )
    out_specs = P(("rep", "grp"), "tp")
    return jax.shard_map(local, mesh=mesh, in_specs=in_specs, out_specs=out_specs, check_vma=False)
```

profile of v0, /device:TPU:0, one launch (start us, length us, event | category | flops | bytes accessed | tf_op | source)
XLA Modules:
  0.0 216.8 jit_solution(9267755241361213123)
XLA Ops:
  6.6 1.4 copy.72
  9.5 21.0 %all-gather.2.cloned.1.call-done = bf16[512,1280]{0,1:T(8,128)(2,1)} async-done(((bf16[512,320]{0,1:T(8,128)(2,1)}), bf16[512,1280]{0,1:T(8,128)(2,1)}) %all-gather.2.cloned.1.call-update) | async-done | bytes 1310736 | tf_op jit(solution)/shard_map/all_gather | solution.py:96
  30.5 1.6 convert_reduce_fusion
  32.1 1.7 fusion.4
  33.9 12.8 %convolution_convert_fusion = bf16[512,1280]{0,1:T(8,128)(2,1)} fusion(bf16[1280,1280]{1,0:T(8,128)(2,1)S(1)} %copy-done, bf16[1280,1280]{1,0:T(8,128)(2,1)} %param.24, bf16[512,1280]{0,1:T(8,128)(2,1)} %all-gather.2.cloned.1.call-done, f32[1280]{0:T(1024)S(1)} %copy-done.13, f32[1280]{0:T(1024)S(1)} %copy-done.14, f32[1280]{0:T(1024)S(1)} %copy-done.15, ...), kind=kOutput, calls=%fused_computation.16 | convolution fusion | flops 3403284480 | bytes 9194496 | tf_op jit(solution)/shard_map/dot_general | solution.py:101
  51.7 2.8 %copy.73 = bf16[4,1,128,1600]{3,2,0,1:T(8,128)(2,1)S(1)} copy(bf16[4,1,128,1600]{2,3,1,0:T(8,128)(2,1)} %param.21) | data formatting | bytes 3276800 | tf_op args[1]
  54.5 8.5 %fusion.101 = f32[512,2048]{1,0:T(8,128)} fusion(bf16[512,1600]{1,0:T(8,128)(2,1)S(1)} %bitcast.71, bf16[1600,2048]{1,0:T(8,128)(2,1)} %param.29), kind=kOutput, calls=%fused_computation.164 | convolution fusion | flops 3355443200 | bytes 12386304 | tf_op jit(solution)/shard_map/dot_general | solution.py:129
  63.0 10.4 %reduce-scatter.2.cloned.1.call-done = bf16[512,320]{0,1:T(8,128)(2,1)} async-done(((bf16[512,1280]{0,1:T(8,128)(2,1)}), bf16[512,320]{0,1:T(8,128)(2,1)}) %reduce-scatter.2.cloned.1.call-update) | async-done | bytes 327696 | tf_op jit(solution)/shard_map/reduce_scatter | solution.py:102
  73.4 5.4 %add_convert_fusion = bf16[512,2048]{1,0:T(8,128)(2,1)} fusion(f32[512,2048]{1,0:T(8,128)} %fusion.101, bf16[320,2048]{1,0:T(8,128)(2,1)} %param.28, bf16[512,320]{0,1:T(8,128)(2,1)} %reduce-scatter.2.cloned.1.call-done, f32[320]{0:T(512)S(1)} %copy-done.8, bf16[40,8,4,128]{3,2,1,0:T(4,128)(2,1)S(1)} %bitcast.66), kind=kOutput, calls=%fused_computation.9 | convolution fusion | flops 674004992 | bytes 8258816 | tf_op jit(solution)/shard_map/dot_general | solution.py:129
  78.8 1.6 copy-done.5
  81.8 1.9 copy-done.2
  83.7 1.7 multiply_reduce_fusion
  86.7 43.7 %all-reduce.2.cloned.1.call-done = bf16[512,2048]{1,0:T(8,128)(2,1)} async-done(((bf16[512,2048]{1,0:T(8,128)(2,1)}), bf16[512,2048]{1,0:T(8,128)(2,1)}) %all-reduce.2.cloned.1.call-update) | async-done | bytes 2097168 | tf_op jit(solution)/shard_map/psum | solution.py:55
  135.0 4.6 %all-to-all-start.1 = ((bf16[2,4,128,2,128]{4,2,0,3,1:T(8,128)(2,1)}), bf16[2,4,128,2,128]{4,2,0,3,1:T(8,128)(2,1)S(1)}, u32[]{:S(2)}, u32[]{:S(2)}) async-start(bf16[2,4,128,2,128]{4,2,0,3,1:T(8,128)(2,1)} %copy.82), calls=%async_computation.2 | async-start | bytes 1048576 | tf_op jit(solution)/shard_map/all_to_all | solution.py:137
  139.6 1.2 compare_select_fusion.4
  140.8 1.3 broadcast_compare_fusion
  145.8 8.2 %all-to-all-done.1 = bf16[2,4,128,2,128]{4,2,0,3,1:T(8,128)(2,1)S(1)} async-done(((bf16[2,4,128,2,128]{4,2,0,3,1:T(8,128)(2,1)}), bf16[2,4,128,2,128]{4,2,0,3,1:T(8,128)(2,1)S(1)}, u32[]{:S(2)}, u32[]{:S(2)}) %all-to-all-start.1) | async-done | bytes 524320 | tf_op jit(solution)/shard_map/all_to_all | solution.py:137
  154.0 3.7 %all-to-all-start = ((bf16[2,4,128,2,128]{2,0,4,3,1:T(2,128)(2,1)}), bf16[2,4,128,2,128]{2,0,4,3,1:T(2,128)(2,1)S(1)}, u32[]{:S(2)}, u32[]{:S(2)}) async-start(bf16[2,4,128,2,128]{2,0,4,3,1:T(2,128)(2,1)} %copy.77), calls=%async_computation.1 | async-start | bytes 1048576 | tf_op jit(solution)/shard_map/all_to_all | solution.py:138
  157.7 2.9 %multiply_convert_fusion = bf16[512,2,8,128]{3,2,1,0:T(8,128)(2,1)S(1)} fusion(f32[512,2,8,128]{3,2,1,0:T(8,128)} %bitcast.62, f32[128]{0:T(128)S(1)} %copy-done.9, f32[512,2,8]{2,1,0:T(2,128)} %copy.85), kind=kLoop, calls=%fused_computation.7 | loop fusion | flops 3145728 | bytes 6324736 | tf_op jit(solution)/shard_map/convert_element_type | solution.py:155
  161.7 9.7 %all-to-all-done = bf16[2,4,128,2,128]{2,0,4,3,1:T(2,128)(2,1)S(1)} async-done(((bf16[2,4,128,2,128]{2,0,4,3,1:T(2,128)(2,1)}), bf16[2,4,128,2,128]{2,0,4,3,1:T(2,128)(2,1)S(1)}, u32[]{:S(2)}, u32[]{:S(2)}) %all-to-all-start) | async-done | bytes 524320 | tf_op jit(solution)/shard_map/all_to_all | solution.py:138
  171.4 1.3 fusion.62
  174.6 15.9 %fusion = (f32[512,2,8]{0,2,1:T(8,128)S(1)}, f32[2,1024,512,8]{2,1,3,0:T(8,128)}) fusion(pred[512,1024]{0,1:T(8,128)(4,1)} %compare_and_fusion, bf16[1024,2,128,1]{2,0,3,1:T(8,128)(2,1)} %bitcast.74, bf16[512,2,8,128]{3,2,1,0:T(8,128)(2,1)S(1)} %multiply_convert_fusion), kind=kOutput, calls=%fused_computation.4 | convolution fusion | flops 2172641280 | bytes 36732928 | tf_op jit(solution)/shard_map/while/body/eval_jaxpr/tkgd,skd->tkgs/dot_general | solution.py:163
  190.5 15.8 %fusion.20 = bf16[2,128,512,8]{2,1,3,0:T(8,128)(2,1)} fusion(f32[2,1024,512,8]{2,1,3,0:T(8,128)} %get-tuple-element.43, f32[512,2,8]{0,2,1:T(8,128)S(1)} %broadcast_select_fusion, pred[512,1024]{0,1:T(8,128)(4,1)S(1)} %copy-done.6, pred[512]{0:T(512)(128)(4,1)S(1)} %broadcast_compare_fusion, bf16[1024,2,128,1]{0,2,1,3:T(8,128)(2,1)S(1)} %copy-done.7), kind=kOutput, calls=%fused_computation.42 | convolution fusion | flops 2190475264 | bytes 36733440 | tf_op jit(solution)/shard_map/while/body/eval_jaxpr/tkgs,skd->tkgd/dot_general | solution.py:173
  206.3 3.9 %copy.88 = bf16[512,2048]{1,0:T(8,128)(2,1)} copy(bf16[512,2048]{0,1:T(8,128)(2,1)} %bitcast.67) | data formatting | bytes 4194304 | tf_op jit(solution)/shard_map/reshape | solution.py:183
  (86 shorter events, 19.7 us)
Async XLA Ops:
  6.5 27.3 %copy-start = (bf16[1280,1280]{1,0:T(8,128)(2,1)S(1)}, bf16[1280,1280]{1,0:T(8,128)(2,1)}, u32[]{:S(2)}) copy-start(bf16[1280,1280]{1,0:T(8,128)(2,1)} %param.26) | copy-start | bytes 9830404
  6.5 27.3 %copy-start.13 = (f32[1280]{0:T(1024)S(1)}, f32[1280]{0:T(1024)}, u32[]{:S(2)}) copy-start(f32[1280]{0:T(1024)} %param.25) | copy-start | bytes 15364
  6.5 27.3 %copy-start.14 = (f32[1280]{0:T(1024)S(1)}, f32[1280]{0:T(1024)}, u32[]{:S(2)}) copy-start(f32[1280]{0:T(1024)} %param.23) | copy-start | bytes 15364
  6.5 27.3 %copy-start.15 = (f32[1280]{0:T(1024)S(1)}, f32[1280]{0:T(1024)}, u32[]{:S(2)}) copy-start(f32[1280]{0:T(1024)} %param.22) | copy-start | bytes 15364
  6.5 24.0 %all-gather.2.cloned.1.call-start = ((), (), s32[]{:S(2)}) async-start(), calls=%async_computation.3 | async-start | bytes 1638400 | tf_op jit(solution)/shard_map/all_gather | solution.py:96
  8.0 0.7 copy-start.3
  9.5 63.9 %reduce-scatter.2.cloned.1.call-start = ((), (), s32[]{:S(2)}) async-start(), calls=%async_computation.4 | async-start | bytes 1638400 | tf_op jit(solution)/shard_map/reduce_scatter | solution.py:102
  33.9 13.1 %copy-start.16 = (s32[8]{0:T(128)S(1)}, s32[8]{0:T(128)}, u32[]{:S(2)}) copy-start(s32[8]{0:T(128)} %param.34) | copy-start | bytes 100
  33.9 13.2 %copy-start.10 = (s32[8]{0:T(128)S(1)}, s32[8]{0:T(128)}, u32[]{:S(2)}) copy-start(s32[8]{0:T(128)} %param.35) | copy-start | bytes 100
  33.9 13.2 %copy-start.11 = (s32[8]{0:T(128)S(1)}, s32[8]{0:T(128)}, u32[]{:S(2)}) copy-start(s32[8]{0:T(128)} %param.33) | copy-start | bytes 100
  46.7 83.7 %all-reduce.2.cloned.1.call-start = ((), (), s32[]{:S(2)}) async-start(), calls=%async_computation.5 | async-start | bytes 4194304 | tf_op jit(solution)/shard_map/psum | solution.py:55
  54.5 18.9 %copy-start.4 = (bf16[4,1,128,320]{2,0,3,1:T(4,128)(2,1)S(1)}, bf16[4,1,128,320]{2,0,3,1:T(4,128)(2,1)}, u32[]{:S(2)}) copy-start(bf16[4,1,128,320]{2,0,3,1:T(4,128)(2,1)} %copy-done.3) | copy-start | bytes 983044
  54.5 18.9 %copy-start.8 = (f32[320]{0:T(512)S(1)}, f32[320]{0:T(512)}, u32[]{:S(2)}) copy-start(f32[320]{0:T(512)} %param.27) | copy-start | bytes 3844
  78.8 1.6 copy-start.5
  81.8 1.9 copy-start.2
  131.9 1.2 copy-start.12
  134.1 23.6 %copy-start.9 = (f32[128]{0:T(128)S(1)}, f32[128]{0:T(128)}, u32[]{:S(2)}) copy-start(f32[128]{0:T(128)} %param.31) | copy-start | bytes 1540
  135.0 19.0 %all-to-all-start.1 = ((bf16[2,4,128,2,128]{4,2,0,3,1:T(8,128)(2,1)}), bf16[2,4,128,2,128]{4,2,0,3,1:T(8,128)(2,1)S(1)}, u32[]{:S(2)}, u32[]{:S(2)}) async-start(bf16[2,4,128,2,128]{4,2,0,3,1:T(8,128)(2,1)} %copy.82), calls=%async_computation.2 | async-start | bytes 1048576 | tf_op jit(solution)/shard_map/all_to_all | solution.py:137
  154.0 17.4 %all-to-all-start = ((bf16[2,4,128,2,128]{2,0,4,3,1:T(2,128)(2,1)}), bf16[2,4,128,2,128]{2,0,4,3,1:T(2,128)(2,1)S(1)}, u32[]{:S(2)}, u32[]{:S(2)}) async-start(bf16[2,4,128,2,128]{2,0,4,3,1:T(2,128)(2,1)} %copy.77), calls=%async_computation.1 | async-start | bytes 1048576 | tf_op jit(solution)/shard_map/all_to_all | solution.py:138
  174.6 15.9 %copy-start.6 = (pred[512,1024]{0,1:T(8,128)(4,1)S(1)}, pred[512,1024]{0,1:T(8,128)(4,1)}, u32[]{:S(2)}) copy-start(pred[512,1024]{0,1:T(8,128)(4,1)} %compare_and_fusion) | copy-start | bytes 1572868
  174.6 15.9 %copy-start.7 = (bf16[1024,2,128,1]{0,2,1,3:T(8,128)(2,1)S(1)}, bf16[1024,2,128,1]{0,2,1,3:T(8,128)(2,1)}, u32[]{:S(2)}) copy-start(bf16[1024,2,128,1]{0,2,1,3:T(8,128)(2,1)} %reshape.274) | copy-start | bytes 1572868
  190.5 19.8 %copy-start.1 = (bf16[1280,1280]{1,0:T(8,128)(2,1)S(1)}, bf16[1280,1280]{1,0:T(8,128)(2,1)}, u32[]{:S(2)}) copy-start(bf16[1280,1280]{1,0:T(8,128)(2,1)} %param.26) | copy-start | bytes 9830404
Sparse Core Ops, SparseCore 0:
  9.6 20.8 all-gather.1
  46.8 26.5 reduce-scatter.1
  78.9 51.3 all-reduce.1
where the time goes:
time: 217 us
  waiting for transfers between devices  93.1 us (43%)
  matrix products  58.3 us (27%)
  local copies, waits for them, and re-layouts  25.3 us (12%)
  other arithmetic  17.3 us (8%)
  between operations  14.2 us (7%)
  starting transfers between devices  8.59 us (4%)
    psum x1, waiting for transfers between devices, reduce_heads(): lax.psum(partial_value.astype(jnp.bfloat16), 'tp').astype(jnp.float32)  43.7 us
    all_gather x1, waiting for transfers between devices, local(): full_rows = lax.all_gather(token_rows, 'tp', axis=1, tiled=True)  21 us
    dot_general x1, matrix products, attend(): jnp.einsum('tkgd,skd->tkgs', query_block, key_rows, preferred_element_typ...  15.9 us
    dot_general x1, matrix products, attend(): jnp.einsum('tkgs,skd->tkgd', probs, value_rows, preferred_element_type=jn...  15.8 us
    dot_general x1, matrix products, local(): mlp_terms = jnp.dot(hidden, w_down, preferred_element_type=jnp.float32)  12.8 us
    reduce_scatter x1, waiting for transfers between devices, local(): lax.psum_scatter(mlp_terms.astype(jnp.bfloat16), 'tp', scatter_dimension=...  10.4 us
    unnamed x38, local copies, waits for them, and re-layouts  10.1 us
    all_to_all x1, waiting for transfers between devices, local(): lax.all_to_all(sent_values, 'grp', split_axis=1, concat_axis=1, tiled=True)  9.71 us
  transfers between devices with their start and end apart: 5, of which 5 were waited for; matrix products, arithmetic and copies ran while one was open for 14% of the time, Pallas kernels for 0%

commit v1 on v0

v1 whole, which is shorter than its diff:
```python
import functools
import math

import jax
import jax.numpy as jnp
from jax import lax
from jax.experimental import pallas as pl
from jax.experimental.pallas import tpu as pltpu
from jax.sharding import PartitionSpec as P

KVH = 8
HD = 128
MAXT = 4
REQ_G = 2
LANES = 128
ROW_BLOCK = 128
HIDDEN_BLOCK = 256
VALUE_SHIFT = 2.0**-24
epsilon = 1e-05

F32 = jnp.float32
BF16 = jnp.bfloat16
VMEM = pl.BlockSpec(memory_space=pltpu.VMEM)
SMEM = pl.BlockSpec(memory_space=pltpu.SMEM)
MIB = 1024 * 1024


def bits_of(count):
    bits = count.bit_length() - 1
    assert 1 << bits == count
    return bits


def xor_order(blocks, index):
    blocks = list(blocks)
    for b in range(bits_of(len(blocks))):
        swap = ((index >> b) & 1) == 1
        for k in range(len(blocks)):
            if not (k >> b) & 1:
                low, high = blocks[k], blocks[k | (1 << b)]
                blocks[k] = lax.select(swap, high, low)
                blocks[k | (1 << b)] = lax.select(swap, low, high)
    return blocks


def xor_pairs(count, mask):
    return [(i, i ^ mask) for i in range(count)]


def tail_plan(rows, width):
    whole = width // LANES * LANES
    tail = width - whole
    packed = tail > 0 and rows // ROW_BLOCK * tail == whole
    return whole, tail, packed


def layout_kernel(group_count, tiles_local, where_ref, tiles_ref, owner_ref, text_ref, meta_ref):
    group = where_ref[0]
    zero = jnp.int32(0)
    firsts, counts, offsets, texts_first, texts_both = [], [], [], [], []
    offset = zero
    for p in range(group_count):
        first, count, text_first, text_both, seen = zero, zero, zero, zero, zero
        for r in range(owner_ref.shape[0]):
            mine = owner_ref[r] == p
            tiles = jnp.where(mine, tiles_ref[r], 0)
            text = jnp.where(mine, text_ref[r], 0)
            first = first + jnp.where(seen == 0, tiles, 0)
            text_first = text_first + jnp.where(seen == 0, text, 0)
            count = count + tiles
            text_both = text_both + text
            seen = seen + jnp.where(mine, 1, 0)
        firsts.append(first)
        counts.append(count)
        offsets.append(offset)
        texts_first.append(text_first)
        texts_both.append(text_both)
        offset = offset + count

    def pick(values, index):
        out = values[0]
        for p in range(1, group_count):
            out = jnp.where(index == p, values[p], out)
        return out

    slots = slot_count_of(group_count)
    star, most = zero, counts[0]
    for p in range(1, group_count):
        larger = counts[p] > most
        star = jnp.where(larger, p, star)
        most = jnp.where(larger, counts[p], most)

    def local_tile(offset, slot):
        lane = lax.rem(group - offset + group_count * REQ_G * MAXT * group_count, group_count)
        tile = lax.div(offset + slot * group_count + lane, group_count)
        return jnp.minimum(tile, tiles_local - 1)

    my_first, my_count = pick(firsts, group), pick(counts, group)
    my_offset = pick(offsets, group)
    place = meta_places(group_count)
    meta_ref[place["first"]] = my_first
    meta_ref[place["second"]] = my_count - my_first
    meta_ref[place["text_first"]] = pick(texts_first, group)
    meta_ref[place["text_both"]] = pick(texts_both, group)
    meta_ref[place["star"]] = local_tile(pick(offsets, star), 1)
    for slot in range(slots):
        for d in range(group_count):
            other = group ^ d
            meta_ref[place["send"] + slot * group_count + d] = local_tile(pick(offsets, other), slot)
            lane = lax.rem(other - my_offset + group_count * REQ_G * MAXT * group_count, group_count)
            position = slot * group_count + lane
            goes = jnp.where(
                position < my_first,
                position,
                jnp.where(position < my_count, MAXT + position - my_first, -1),
            )
            meta_ref[place["goes"] + slot * group_count + d] = goes


def slot_count_of(group_count):
    return (REQ_G * MAXT + group_count - 1) // group_count


def meta_places(group_count):
    table = slot_count_of(group_count) * group_count
    return {
        "first": 0,
        "second": 1,
        "text_first": 2,
        "text_both": 3,
        "star": 4,
        "send": 8,
        "goes": 8 + table,
        "size": 8 + 2 * table,
    }


def request_layout(group_count, tiles_local, where, tiles_per_request, owner, text_per_request):
    size = meta_places(group_count)["size"]
    return pl.pallas_call(
        functools.partial(layout_kernel, group_count, tiles_local),
        out_shape=jax.ShapeDtypeStruct((size,), jnp.int32),
        in_specs=[SMEM] * 4,
        out_specs=SMEM,
        cost_estimate=pl.CostEstimate(flops=1000, bytes_accessed=4000, transcendentals=0),
        name="request_layout",
    )(where, tiles_per_request, owner, text_per_request)


def mlp_kernel(piece_count, where_ref, *refs):
    pieces = refs[:piece_count]
    gain_ref, bias_ref, up_ref, up_bias_ref, down_ref = refs[piece_count : piece_count + 5]
    outs = refs[piece_count + 5 : 2 * piece_count + 5]
    normed_ref, hidden_ref, total_ref = refs[2 * piece_count + 5 :]
    index = where_ref[1]
    rows, width = pieces[0].shape
    channels = width * piece_count
    for row in range(0, rows, ROW_BLOCK):
        take = pl.ds(row, ROW_BLOCK)
        blocks = xor_order([piece[take, :].astype(F32) for piece in pieces], index)
        values = jnp.concatenate(blocks, axis=1)
        average = jnp.sum(values, axis=1, keepdims=True) * (1.0 / channels)
        centered = values - average
        variance = jnp.sum(centered * centered, axis=1, keepdims=True) * (1.0 / channels)
        normed = centered * lax.rsqrt(variance + epsilon) * gain_ref[...] + bias_ref[...]
        normed_ref[take, :] = normed.astype(BF16)
    hidden_width = up_ref.shape[1]
    step = math.gcd(hidden_width, HIDDEN_BLOCK)
    for col in range(0, hidden_width, step):
        take = pl.ds(col, step)
        value = jnp.dot(normed_ref[...], up_ref[:, take], preferred_element_type=F32)
        value = value + up_bias_ref[:, take]
        value = 0.5 * value * (1.0 + lax.erf(value * (1.0 / math.sqrt(2.0))))
        hidden_ref[:, take] = value.astype(BF16)
    step = math.gcd(channels, HIDDEN_BLOCK)
    for col in range(0, channels, step):
        take = pl.ds(col, step)
        total_ref[:, take] = jnp.dot(
            hidden_ref[...], down_ref[:, take], preferred_element_type=F32
        )
    whole, tail, packed = tail_plan(rows, width)
    for row in range(0, rows, ROW_BLOCK):
        take = pl.ds(row, ROW_BLOCK)
        blocks = [total_ref[take, j * width : (j + 1) * width] for j in range(piece_count)]
        for out, block in zip(outs, xor_order(blocks, index)):
            block = block.astype(BF16)
            if packed:
                out[take, :] = block[:, :whole]
                out[rows : rows + ROW_BLOCK, row // ROW_BLOCK * tail : (row // ROW_BLOCK + 1) * tail] = block[:, whole:]
            else:
                out[take, :] = block


def encoder_mlp(where, pieces, ln_gain, ln_bias, w_up, b_up, w_down):
    rows, width = pieces[0].shape
    count = len(pieces)
    channels, hidden_width = w_up.shape
    whole, _, packed = tail_plan(rows, width)
    shape = (rows + ROW_BLOCK, whole) if packed else (rows, width)
    return pl.pallas_call(
        functools.partial(mlp_kernel, count),
        out_shape=[jax.ShapeDtypeStruct(shape, BF16)] * count,
        in_specs=[SMEM] + [VMEM] * (count + 5),
        out_specs=[VMEM] * count,
        scratch_shapes=[
            pltpu.VMEM((rows, channels), BF16),
            pltpu.VMEM((rows, hidden_width), BF16),
            pltpu.VMEM((rows, channels), F32),
        ],
        compiler_params=pltpu.CompilerParams(vmem_limit_bytes=32 * MIB),
        cost_estimate=pl.CostEstimate(
            flops=4 * rows * channels * hidden_width,
            bytes_accessed=4 * channels * hidden_width + 4 * rows * channels,
            transcendentals=rows * hidden_width,
        ),
        name="encoder_mlp",
    )(
        where,
        *pieces,
        ln_gain.reshape(1, channels),
        ln_bias.reshape(1, channels),
        w_up,
        b_up.reshape(1, hidden_width),
        w_down,
    )


def tap_kernel(where_ref, tap_ref, weight_ref, out_ref):
    out_ref[...] = jnp.dot(
        tap_ref[...], weight_ref[...], preferred_element_type=F32
    ).astype(BF16)[None, None]


def tap_projection(where, tap_rows, weights, head_count, dest_count, dup):
    rows, depth = tap_rows.shape
    block = 2 * HD

    def head_of(n, where_ref):
        dest = lax.div(where_ref[1], jnp.int32(dup)) ^ lax.rem(n, dest_count)
        return dest * head_count + lax.div(n, dest_count)

    return pl.pallas_call(
        tap_kernel,
        out_shape=jax.ShapeDtypeStruct((head_count, dest_count, rows, block), BF16),
        grid_spec=pltpu.PrefetchScalarGridSpec(
            num_scalar_prefetch=1,
            grid=(head_count * dest_count,),
            in_specs=[
                pl.BlockSpec((rows, depth), lambda n, w: (0, 0)),
                pl.BlockSpec((depth, block), lambda n, w: (0, head_of(n, w))),
            ],
            out_specs=pl.BlockSpec(
                (1, 1, rows, block),
                lambda n, w: (lax.div(n, dest_count), lax.rem(n, dest_count), 0, 0),
            ),
        ),
        compiler_params=pltpu.CompilerParams(vmem_limit_bytes=16 * MIB),
        cost_estimate=pl.CostEstimate(
            flops=2 * rows * depth * weights.shape[1],
            bytes_accessed=2 * depth * weights.shape[1],
            transcendentals=0,
        ),
        name="tap_projection",
    )(where, tap_rows, weights)


def kv_kernel(head_count, dest_count, dup, term_count, where_ref, *refs):
    x_ref, bias_ref, weight_ref, tap_ref = refs[:4]
    terms = refs[4 : 4 + term_count]
    outs = refs[4 + term_count : -1]
    encoded_ref = refs[-1]
    rows, width = x_ref.shape
    whole, tail, packed = tail_plan(rows, width)
    for row in range(0, rows, ROW_BLOCK):
        take = pl.ds(row, ROW_BLOCK)

        def summed(part, lanes):
            out = terms[0][part, lanes].astype(F32)
            for term in terms[1:]:
                out = out + term[part, lanes].astype(F32)
            return out

        if packed:
            start = row // ROW_BLOCK * tail
            main = summed(take, slice(None))
            rest = summed(pl.ds(rows, ROW_BLOCK), slice(start, start + tail))
            total = jnp.concatenate([main, rest], axis=1)
        else:
            total = summed(take, slice(None))
        encoded_ref[take, :] = (x_ref[take, :].astype(F32) + total + bias_ref[...]).astype(BF16)
    block = 2 * HD
    mine = lax.div(where_ref[1], jnp.int32(dup))
    for head in range(head_count):
        for k in range(dest_count):
            column = ((mine ^ k) * head_count + head) * block
            weights = weight_ref[:, pl.ds(pl.multiple_of(column, block), block)]
            value = jnp.dot(encoded_ref[...], weights, preferred_element_type=F32)
            value = value + tap_ref[head, k].astype(F32)
            outs[head * dest_count + k][...] = value.astype(BF16)


def kv_projection(where, x_rows, b_down, weights, tap_part, terms, dup):
    rows, width = x_rows.shape
    head_count, dest_count = tap_part.shape[:2]
    block = 2 * HD
    outs = pl.pallas_call(
        functools.partial(kv_kernel, head_count, dest_count, dup, len(terms)),
        out_shape=[jax.ShapeDtypeStruct((rows, block), BF16)] * (head_count * dest_count),
        in_specs=[SMEM] + [VMEM] * (4 + len(terms)),
        out_specs=[VMEM] * (head_count * dest_count),
        scratch_shapes=[pltpu.VMEM((rows, width), BF16)],
        compiler_params=pltpu.CompilerParams(vmem_limit_bytes=24 * MIB),
        cost_estimate=pl.CostEstimate(
            flops=2 * rows * width * weights.shape[1],
            bytes_accessed=2 * width * weights.shape[1] + 4 * rows * weights.shape[1],
            transcendentals=0,
        ),
        name="kv_projection",
    )(where, x_rows, b_down.reshape(1, width), weights, tap_part, *terms)
    return [outs[h * dest_count : (h + 1) * dest_count] for h in range(head_count)]


def finish_kernel(term_count, picks, meta_ref, gain_ref, *refs):
    terms = refs[:term_count]
    outs = refs[term_count : term_count + len(picks)]
    done_ref = refs[-1]
    rows = terms[0].shape[0]
    for row in range(0, rows, ROW_BLOCK):
        take = pl.ds(row, ROW_BLOCK)
        total = terms[0][take, :].astype(F32)
        for term in terms[1:]:
            total = total + term[take, :].astype(F32)
        keys = total[:, :HD]
        square = jnp.sum(keys * keys, axis=1, keepdims=True) * (1.0 / HD)
        keys = keys * lax.rsqrt(square + epsilon) * gain_ref[...]
        done_ref[take, :HD] = keys.astype(BF16)
        done_ref[take, HD:] = (total[:, HD:] * VALUE_SHIFT).astype(BF16)
    for out, places in zip(outs, picks):
        for n, place in enumerate(places):
            start = pl.multiple_of(meta_ref[place] * ROW_BLOCK, ROW_BLOCK)
            out[n] = done_ref[pl.ds(start, ROW_BLOCK), :]


def finish_tiles(meta, k_gain, terms, picks):
    rows, block = terms[0].shape
    return pl.pallas_call(
        functools.partial(finish_kernel, len(terms), picks),
        out_shape=[jax.ShapeDtypeStruct((len(p), ROW_BLOCK, block), BF16) for p in picks],
        in_specs=[SMEM] + [VMEM] * (1 + len(terms)),
        out_specs=[VMEM] * len(picks),
        scratch_shapes=[pltpu.VMEM((rows, block), BF16)],
        compiler_params=pltpu.CompilerParams(vmem_limit_bytes=8 * MIB),
        cost_estimate=pl.CostEstimate(
            flops=10 * rows * block, bytes_accessed=10 * rows * block, transcendentals=rows
        ),
        name="finish_tiles",
    )(meta, k_gain.reshape(1, HD), *terms)


def query_kernel(gain_ref, query_ref, out_ref):
    gain = gain_ref[...] * (math.log2(math.e) / math.sqrt(HD))
    for col in range(0, query_ref.shape[1], HD):
        values = query_ref[:, col : col + HD].astype(F32)
        square = jnp.sum(values * values, axis=1, keepdims=True) * (1.0 / HD)
        out_ref[:, col : col + HD] = (values * lax.rsqrt(square + epsilon) * gain).astype(BF16)


def query_norm(queries, q_gain):
    rows, width = queries.shape
    step = math.gcd(rows, 128)
    return pl.pallas_call(
        query_kernel,
        out_shape=jax.ShapeDtypeStruct((rows, width), BF16),
        grid=(rows // step,),
        in_specs=[
            pl.BlockSpec((1, HD), lambda i: (0, 0)),
            pl.BlockSpec((step, width), lambda i: (i, 0)),
        ],
        out_specs=pl.BlockSpec((step, width), lambda i: (i, 0)),
        compiler_params=pltpu.CompilerParams(vmem_limit_bytes=16 * MIB),
        cost_estimate=pl.CostEstimate(
            flops=8 * rows * width, bytes_accessed=4 * rows * width, transcendentals=rows * width // HD
        ),
        name="query_norm",
    )(q_gain.reshape(1, HD), queries)


def attend_kernel(group_count, sources, has_base, meta_ref, query_ref, *refs):
    tile_refs = refs[: len(sources)]
    out_ref, key_ref, value_ref = refs[len(sources) + has_base :]
    place = meta_places(group_count)
    counts = (meta_ref[place["first"]], meta_ref[place["second"]])
    text_first, text_both = meta_ref[place["text_first"]], meta_ref[place["text_both"]]
    span = MAXT * ROW_BLOCK
    key_ref[...] = jnp.zeros_like(key_ref)
    value_ref[...] = jnp.zeros_like(value_ref)
    out_ref[...] = jnp.zeros_like(out_ref)
    for tile_ref, places in zip(tile_refs, sources):
        for n, slot in enumerate(places):
            goes = meta_ref[place["goes"] + slot]

            @pl.when(goes >= 0)
            def _(tile_ref=tile_ref, n=n, goes=goes):
                take = pl.ds(pl.multiple_of(goes * ROW_BLOCK, ROW_BLOCK), ROW_BLOCK)
                key_ref[take, :] = tile_ref[n, :, :HD]
                value_ref[take, :HD] = tile_ref[n, :, HD:]
                value_ref[take, HD:] = jnp.ones((ROW_BLOCK, HD), BF16)

    text_rows, width = query_ref.shape
    heads = width // HD
    for block in range(text_rows // ROW_BLOCK):
        start = block * ROW_BLOCK
        take = pl.ds(start, ROW_BLOCK)
        for label, (low, high) in enumerate(((0, text_first), (text_first, text_both))):
            meets = jnp.maximum(low, start) < jnp.minimum(high, start + ROW_BLOCK)

            def attend(key_rows, label=label, start=start, take=take, low=low, high=high):
                part = pl.ds(label * span, key_rows)
                slots = start + lax.broadcasted_iota(jnp.int32, (ROW_BLOCK, HD), 0)
                owned = (slots >= low) & (slots < high)
                for head in range(heads):
                    lanes = slice(head * HD, (head + 1) * HD)
                    scores = lax.dot_general(
                        query_ref[take, lanes],
                        key_ref[part, :],
                        (((1,), (1,)), ((), ())),
                        preferred_element_type=F32,
                    )
                    weights = jnp.exp2(scores).astype(BF16)
                    sums = jnp.dot(weights, value_ref[part, :], preferred_element_type=F32)
                    result = sums[:, :HD] / sums[:, HD:] * (1.0 / VALUE_SHIFT)
                    kept = out_ref[take, lanes].astype(F32)
                    out_ref[take, lanes] = jnp.where(owned, result, kept).astype(BF16)

            half = span // 2
            few = counts[label] * ROW_BLOCK <= half

            @pl.when(meets & few)
            def _(attend=attend):
                attend(half)

            @pl.when(meets & jnp.logical_not(few))
            def _(attend=attend):
                attend(span)


def attend_head(group_count, meta, queries, tiles, sources, base, head, head_count):
    rows, width = queries.shape
    head_width = width // head_count
    group_rows = REQ_G * MAXT * ROW_BLOCK
    whole_tile = pl.BlockSpec(memory_space=pltpu.VMEM)
    extra = [] if base is None else [base]
    return pl.pallas_call(
        functools.partial(attend_kernel, group_count, sources, len(extra)),
        out_shape=jax.ShapeDtypeStruct((rows, width), BF16),
        grid=(1,),
        in_specs=[
            SMEM,
            pl.BlockSpec((rows, head_width), lambda i: (0, head)),
        ]
        + [whole_tile] * len(tiles)
        + [pl.BlockSpec(memory_space=pl.ANY)] * len(extra),
        out_specs=pl.BlockSpec((rows, head_width), lambda i: (0, head)),
        scratch_shapes=[
            pltpu.VMEM((group_rows, HD), BF16),
            pltpu.VMEM((group_rows, 2 * HD), BF16),
        ],
        input_output_aliases={2 + len(tiles): 0} if extra else {},
        compiler_params=pltpu.CompilerParams(vmem_limit_bytes=24 * MIB),
        cost_estimate=pl.CostEstimate(
            flops=4 * rows * head_width * group_rows,
            bytes_accessed=4 * rows * head_width,
            transcendentals=rows * head_width // HD * group_rows // 2,
        ),
        name="attend_head",
    )(meta, queries, *tiles, *extra)


def add_rounded(a, b):
    return (a.astype(F32) + b.astype(F32)).astype(BF16)


def scatter_sum(blocks, count, first_bit):
    blocks = dict(enumerate(blocks))
    bits = bits_of(len(blocks))
    for b in range(bits):
        pairs = xor_pairs(count, 1 << (b + first_bit))
        got = {}
        for k in sorted((k for k in blocks if (k >> b) & 1), reverse=True):
            got[k ^ (1 << b)] = lax.ppermute(blocks[k], "tp", pairs)
        if b == bits - 1:
            return [blocks[0], got[0]]
        blocks = {
            k: add_rounded(blocks[k], got[k]) for k in got
        }
    return [blocks[0]]


def gather_pieces(own, count):
    pieces = {0: own}
    for b in reversed(range(bits_of(count))):
        pairs = xor_pairs(count, 1 << b)
        for k in list(pieces):
            pieces[k | (1 << b)] = lax.ppermute(pieces[k], "tp", pairs)
    return [pieces[k] for k in range(count)]


def local(
    x_in,
    taps,
    ln_gain,
    ln_bias,
    w_up,
    b_up,
    w_down,
    b_down,
    kv_w_out,
    kv_w_taps,
    k_gain,
    q_gain,
    queries,
    tiles_per_request,
    owner,
    text_per_request,
):
    group_count = lax.axis_size("grp")
    tp_count = lax.axis_size("tp")
    where = jnp.stack([lax.axis_index("grp"), lax.axis_index("tp")]).astype(jnp.int32)
    tiles_local, _, tile_rows, channel_share = x_in.shape
    local_rows = tiles_local * tile_rows
    x_rows = x_in.reshape(local_rows, channel_share)
    tap_rows = taps.reshape(local_rows, taps.shape[3])

    head_count = max(1, KVH // tp_count)
    dup = max(1, tp_count // KVH)
    dest_count = tp_count // dup

    pieces = gather_pieces(x_rows, tp_count)
    tap_part = tap_projection(where, tap_rows, kv_w_taps, head_count, dest_count, dup)
    query_rows = query_norm(queries, q_gain)
    meta = request_layout(
        group_count, tiles_local, where, tiles_per_request, owner, text_per_request
    )

    mlp_blocks = encoder_mlp(where, pieces, ln_gain, ln_bias, w_up, b_up, w_down)
    mlp_terms = scatter_sum(mlp_blocks, tp_count, 0)
    kv_blocks = kv_projection(where, x_rows, b_down, kv_w_out, tap_part, mlp_terms, dup)

    place = meta_places(group_count)
    slots = slot_count_of(group_count)
    total_tiles = group_count * tiles_local
    most_other = total_tiles - REQ_G * MAXT - REQ_G * (group_count - 2)
    one_large = group_count == 4 and slots == 2 and most_other <= group_count
    out = None
    for head in range(head_count):
        blocks = kv_blocks[head]
        for b in range(bits_of(dup)):
            pairs = xor_pairs(tp_count, 1 << b)
            blocks = [add_rounded(v, lax.ppermute(v, "tp", pairs)) for v in blocks]
        terms = scatter_sum(blocks, tp_count, bits_of(dup))
        send = place["send"]

        def move(value, mask):
            return lax.ppermute(value, "grp", xor_pairs(group_count, mask))

        if one_large:
            star = place["star"]
            picks = ((send, star), (send + 1, star), (send + 2,), (send + 3, star))
            own, near, middle, far = finish_tiles(meta, k_gain, terms, picks)
            far_got = move(far, 3)
            middle_got = move(middle, 2)
            near_got = move(near, 1)
            passed = move(far_got[1:], 1)
            tiles = (own, near_got, middle_got, far_got, passed)
            sources = ((0, 4), (1, 5), (2,), (3, 7), (6,))
        else:
            picks = tuple(
                tuple(send + s * group_count + d for s in range(slots)) for d in range(group_count)
            )
            made = finish_tiles(meta, k_gain, terms, picks)
            tiles = tuple(made[:1]) + tuple(move(made[d], d) for d in range(1, group_count))
            sources = tuple(
                tuple(s * group_count + d for s in range(slots)) for d in range(group_count)
            )
        out = attend_head(
            group_count, meta, query_rows, tiles, sources, out, head, head_count
        )
    return out


def solution(mesh):
    in_specs = (
        P(None, ("rep", "grp"), None, "tp"),
        P(None, ("rep", "grp"), None, "tp"),
        P(),
        P(),
        P(None, "tp"),
        P("tp"),
        P("tp", None),
        P("tp"),
        P("tp", None),
        P("tp", None),
        P(),
        P(),
        P(("rep", "grp"), "tp"),
        P("rep"),
        P("rep"),
        P("rep"),
    )
    out_specs = P(("rep", "grp"), "tp")
    return jax.shard_map(local, mesh=mesh, in_specs=in_specs, out_specs=out_specs, check_vma=False)
```

time: 217 us -> 85.7 us (0.39)
  waiting for transfers between devices: 93.1 us -> 20.2 us
  matrix products: 58.3 us -> 0 us
  Pallas kernels: 0 us -> 27.4 us
  other arithmetic: 17.3 us -> 1.48 us
  between operations: 14.2 us -> 0.19 us
  starting transfers between devices: 8.59 us -> 22 us
  local copies, waits for them, and re-layouts: 25.3 us -> 12.8 us
    dot_general x5 -> x0, matrix products: 58.3 us -> none  [the longest x1 15.9 us: attend(): jnp.einsum('tkgd,skd->tkgs', query_block, key_rows, preferred_element_typ...]
    psum x1 -> x0, waiting for transfers between devices: 43.7 us -> none  [reduce_heads(): lax.psum(partial_value.astype(jnp.bfloat16), 'tp').astype(jnp.float32)]
    pallas_call x0 -> x9, Pallas kernels: none -> 27.4 us  [the longest x2 8.43 us: attend_head(): pl.pallas_call(functools.partial(attend_kernel, group_count, sources, len...]
    ppermute x0 -> x20, starting transfers between devices: none -> 22 us  [the longest x8 13.2 us: move(): return lax.ppermute(value, 'grp', xor_pairs(group_count, mask))]
    all_gather x1 -> x0, waiting for transfers between devices: 21 us -> none  [local(): full_rows = lax.all_gather(token_rows, 'tp', axis=1, tiled=True)]
    ppermute x0 -> x20, waiting for transfers between devices: none -> 20.2 us  [the longest x3 9.12 us: gather_pieces(): pieces[k | 1 << b] = lax.ppermute(pieces[k], 'tp', pairs)]
    all_to_all x2 -> x0, waiting for transfers between devices: 18 us -> none  [the longest x1 9.71 us: local(): lax.all_to_all(sent_values, 'grp', split_axis=1, concat_axis=1, tiled=True)]
    reduce_scatter x1 -> x0, waiting for transfers between devices: 10.4 us -> none  [local(): lax.psum_scatter(mlp_terms.astype(jnp.bfloat16), 'tp', scatter_dimension=...]
  transfers between devices with their start and end apart: 5 -> 20, of which waited for: 5 -> 5; matrix products, arithmetic and copies ran while one was open for 14% -> 8% of each run, Pallas kernels for 0% -> 18%
where the time goes in v1:
time: 85.7 us; the launch traced here: 84.1 us
  Pallas kernels  27.4 us (32%)
  starting transfers between devices  22 us (26%)
  waiting for transfers between devices  20.2 us (24%)
  local copies, waits for them, and re-layouts  12.8 us (15%)
  other arithmetic  1.48 us (2%)
    ppermute x8, starting transfers between devices, move(): return lax.ppermute(value, 'grp', xor_pairs(group_count, mask))  13.2 us
    unnamed x22, local copies, waits for them, and re-layouts  10.6 us
    ppermute x3, waiting for transfers between devices, gather_pieces(): pieces[k | 1 << b] = lax.ppermute(pieces[k], 'tp', pairs)  9.12 us
    pallas_call x2, Pallas kernels, attend_head(): pl.pallas_call(functools.partial(attend_kernel, group_count, sources, len...  8.43 us
    ppermute x9, waiting for transfers between devices, scatter_sum(): got[k ^ 1 << b] = lax.ppermute(blocks[k], 'tp', pairs)  7.32 us
    pallas_call x1, Pallas kernels, tap_projection(): pl.pallas_call(tap_kernel, out_shape=jax.ShapeDtypeStruct((head_count, de...  6.8 us
    pallas_call x1, Pallas kernels, encoder_mlp(): pl.pallas_call(functools.partial(mlp_kernel, count), out_shape=[jax.Shape...  5.94 us
    ppermute x9, starting transfers between devices, scatter_sum(): got[k ^ 1 << b] = lax.ppermute(blocks[k], 'tp', pairs)  5.77 us
  transfers between devices with their start and end apart: 20, of which 5 were waited for; matrix products, arithmetic and copies ran while one was open for 8% of the time, Pallas kernels for 18%

profile of v1, /device:TPU:0, one launch (start us, length us, event | category | flops | bytes accessed | tf_op | source)
XLA Modules:
  0.0 84.1 jit_solution(1531395851754910887)
XLA Ops:
  0.0 1.2 %copy.18 = bf16[4,1,128,320]{3,2,0,1:T(8,128)(2,1)S(1)} copy(bf16[4,1,128,320]{2,3,1,0:T(8,128)(2,1)} %param.16) | data formatting | bytes 655360 | tf_op args[0]
  1.2 3.0 %collective-permute-start.1 = (bf16[512,320]{1,0:T(8,128)(2,1)S(1)}, bf16[512,320]{1,0:T(8,128)(2,1)S(1)}, u32[]{:S(2)}, u32[]{:S(2)}) collective-permute-start(bf16[512,320]{1,0:T(8,128)(2,1)S(1)} %bitcast.7), channel_id=1, source_target_pairs={{0,2},{1,3},{2,0},{3,1},{4,6},{5,7},{6,4},{7,5},{8,10},{9,11},{10,... | collective-permute-start | bytes 983048 | tf_op jit(solution)/shard_map/ppermute | solution.py:504
  4.2 9.1 %collective-permute-done.1.refs_2_ = bf16[512,320]{1,0:T(8,128)(2,1)S(1)} collective-permute-done((bf16[512,320]{1,0:T(8,128)(2,1)S(1)}, bf16[512,320]{1,0:T(8,128)(2,1)S(1)}, u32[]{:S(2)}, u32[]{:S(2)}) %collective-permute-start.1) | collective-permute-done | bytes 327712 | tf_op jit(solution)/shard_map/ppermute | solution.py:504
  15.5 1.9 %copy-done.7 = bf16[1280,1280]{1,0:T(8,128)(2,1)S(1)} copy-done((bf16[1280,1280]{1,0:T(8,128)(2,1)S(1)}, bf16[1280,1280]{1,0:T(8,128)(2,1)}, u32[]{:S(2)}) %copy-start.7) | copy-done | bytes 3276824
  17.5 1.9 %copy-done.8 = bf16[1280,1280]{1,0:T(8,128)(2,1)S(1)} copy-done((bf16[1280,1280]{1,0:T(8,128)(2,1)S(1)}, bf16[1280,1280]{1,0:T(8,128)(2,1)}, u32[]{:S(2)}) %copy-start.8) | copy-done | bytes 3276824
  19.4 5.9 %encoder_mlp.1 = (bf16[640,256]{1,0:T(8,128)(2,1)S(1)}, bf16[640,256]{1,0:T(8,128)(2,1)S(1)}, bf16[640,256]{1,0:T(8,128)(2,1)S(1)}, bf16[640,256]{1,0:T(8,128)(2,1)S(1)}) custom-call(s32[2]{0:T(128)S(1)} %pad_add_fusion.where_ref, bf16[512,320]{1,0:T(8,128)(2,1)S(1)} %bitcast.9, bf16[512,320]{1,0:T(8,128)(2,1)S(1)} %collective-permute-done.refs_1_, ...), custom_call_target="tpu_custom_call" | custom-call | flops 3355443200 | bytes 9175040 | tf_op jit(solution)/shard_map/encoder_mlp/pallas_call | solution.py:200
  25.9 2.7 %copy.19 = bf16[4,1,128,1600]{3,2,0,1:T(8,128)(2,1)S(1)} copy(bf16[4,1,128,1600]{2,3,1,0:T(8,128)(2,1)} %param.17) | data formatting | bytes 3276800 | tf_op args[1]
  28.7 1.1 %add_convert_fusion = bf16[640,256]{1,0:T(8,128)(2,1)S(1)} fusion(bf16[640,256]{1,0:T(8,128)(2,1)} %collective-permute-done.4, bf16[640,256]{1,0:T(8,128)(2,1)S(1)} %get-tuple-element.27), kind=kLoop, calls=%fused_computation | loop fusion | flops 655360 | bytes 983040 | tf_op jit(solution)/shard_map/convert_element_type | solution.py:480
  29.8 1.8 %collective-permute-start.5 = (bf16[640,256]{1,0:T(8,128)(2,1)S(1)}, bf16[640,256]{1,0:T(8,128)(2,1)S(1)}, u32[]{:S(2)}, u32[]{:S(2)}) collective-permute-start(bf16[640,256]{1,0:T(8,128)(2,1)S(1)} %add_convert_fusion), channel_id=1, source_target_pairs={{0,2},{1,3},{2,0},{3,1},{4,6},{5,7},{6,4},{7,5},{8,10},{9,11},{10,... | collective-permute-start | bytes 983048 | tf_op jit(solution)/shard_map/ppermute | solution.py:490
  31.6 2.9 %copy-done.6 = bf16[1600,2048]{1,0:T(8,128)(2,1)S(1)} copy-done((bf16[1600,2048]{1,0:T(8,128)(2,1)S(1)}, bf16[1600,2048]{1,0:T(8,128)(2,1)}, u32[]{:S(2)}) %copy-start.6) | copy-done | bytes 6553624
  34.4 6.8 %tap_projection.1.refs_3_ = bf16[2,4,512,256]{3,2,1,0:T(8,128)(2,1)S(1)} custom-call(s32[2]{0:T(128)S(1)} %pad_add_fusion.where_ref, bf16[512,1600]{1,0:T(8,128)(2,1)S(1)} %bitcast.6, bf16[1600,2048]{1,0:T(8,128)(2,1)S(1)} %copy-done.6), custom_call_target="tpu_custom_call" | custom-call | flops 3355443200 | bytes 6553600 | tf_op jit(solution)/shard_map/tap_projection/pallas_call | solution.py:242
  41.4 1.9 %kv_projection.1 = (bf16[512,256]{1,0:T(8,128)(2,1)S(1)}, bf16[512,256]{1,0:T(8,128)(2,1)S(1)}, bf16[512,256]{1,0:T(8,128)(2,1)S(1)}, bf16[512,256]{1,0:T(8,128)...) custom-call(s32[2]{0:T(128)S(1)} %pad_add_fusion.where_ref, ...), custom_call_target="tpu_custom_call" | custom-call | flops 671088640 | bytes 5505024 | tf_op jit(solution)/shard_map/kv_projection/pallas_call | solution.py:306
  43.9 1.4 %request_layout.1.meta_ref = s32[24]{0:T(128)} custom-call(s32[2]{0:T(128)} %copy-done.3, s32[8]{0:T(128)} %tiles_ref.1, s32[8]{0:T(128)} %owner_ref.1, s32[8]{0:T(128)} %text_ref.1), custom_call_target="tpu_custom_call" | custom-call | flops 1000 | bytes 4000 | tf_op jit(solution)/shard_map/request_layout/pallas_call | solution.py:140
  46.4 1.8 %collective-permute-start.8 = (bf16[512,256]{1,0:T(8,128)(2,1)S(1)}, bf16[512,256]{1,0:T(8,128)(2,1)S(1)}, u32[]{:S(2)}, u32[]{:S(2)}) collective-permute-start(bf16[512,256]{1,0:T(8,128)(2,1)S(1)} %add_convert_fusion.4), channel_id=1, source_target_pairs={{0,2},{1,3},{2,0},{3,1},{4,6},{5,7},{6,4},{7,5},{8,10},{9,11},{10,... | collective-permute-start | bytes 786440 | tf_op jit(solution)/shard_map/ppermute | solution.py:490
  48.3 6.9 %collective-permute-done.15.refs_1_ = bf16[512,256]{1,0:T(8,128)(2,1)S(1)} collective-permute-done((bf16[512,256]{1,0:T(8,128)(2,1)S(1)}, bf16[512,256]{1,0:T(8,128)(2,1)S(1)}, u32[]{:S(2)}, u32[]{:S(2)}) %collective-permute-start.15) | collective-permute-done | bytes 262176 | tf_op jit(solution)/shard_map/ppermute | solution.py:490
  55.9 3.6 %collective-permute-start.18 = (bf16[2,128,256]{2,1,0:T(8,128)(2,1)S(1)}, bf16[2,128,256]{2,1,0:T(8,128)(2,1)S(1)}, u32[]{:S(2)}, u32[]{:S(2)}) collective-permute-start(bf16[2,128,256]{2,1,0:T(8,128)(2,1)S(1)} %get-tuple-element.44), channel_id=1, source_target_pairs={{0,12},{4,8},{8,4},{12,0},{1,13},{5,9},{9,5},{13,1},{2,14},{6,10},... | collective-permute-start | bytes 393224 | tf_op jit(solution)/shard_map/ppermute | solution.py:564
  60.8 3.7 %collective-permute-start.11 = (bf16[2,128,256]{2,1,0:T(8,128)(2,1)S(1)}, bf16[2,128,256]{2,1,0:T(8,128)(2,1)S(1)}, u32[]{:S(2)}, u32[]{:S(2)}) collective-permute-start(bf16[2,128,256]{2,1,0:T(8,128)(2,1)S(1)} %get-tuple-element.36), channel_id=1, source_target_pairs={{0,12},{4,8},{8,4},{12,0},{1,13},{5,9},{9,5},{13,1},{2,14},{6,10},... | collective-permute-start | bytes 393224 | tf_op jit(solution)/shard_map/ppermute | solution.py:564
  65.3 1.3 %collective-permute-start.19 = (bf16[1,128,256]{2,1,0:T(8,128)(2,1)S(1)}, bf16[1,128,256]{2,1,0:T(8,128)(2,1)S(1)}, u32[]{:S(2)}, u32[]{:S(2)}) collective-permute-start(bf16[1,128,256]{2,1,0:T(8,128)(2,1)S(1)} %slice.9), channel_id=1, source_target_pairs={{0,4},{4,0},{8,12},{12,8},{1,5},{5,1},{9,13},{13,9},{2,6},{6,2},{1... | collective-permute-start | bytes 196616 | tf_op jit(solution)/shard_map/ppermute | solution.py:564
  66.6 1.5 %query_norm.1.query_ref = bf16[512,2048]{1,0:T(8,128)(2,1)S(1)} custom-call(f32[1,128]{1,0:T(1,128)S(1)} %bitcast.13, bf16[512,2048]{1,0:T(8,128)(2,1)S(1)} %copy-done), custom_call_target="tpu_custom_call" | custom-call | flops 8388608 | bytes 4194304 | tf_op jit(solution)/shard_map/query_norm/pallas_call | solution.py:371
  68.1 3.0 %collective-permute-start.10 = (bf16[1,128,256]{2,1,0:T(8,128)(2,1)S(1)}, bf16[1,128,256]{2,1,0:T(8,128)(2,1)S(1)}, u32[]{:S(2)}, u32[]{:S(2)}) collective-permute-start(bf16[1,128,256]{2,1,0:T(8,128)(2,1)S(1)} %get-tuple-element.35), channel_id=1, source_target_pairs={{0,8},{4,12},{8,0},{12,4},{1,9},{5,13},{9,1},{13,5},{2,10},{6,14},... | collective-permute-start | bytes 196616 | tf_op jit(solution)/shard_map/ppermute | solution.py:564
  71.8 2.0 %collective-permute-done.17.refs_2_ = bf16[1,128,256]{2,1,0:T(8,128)(2,1)S(1)} collective-permute-done((bf16[1,128,256]{2,1,0:T(8,128)(2,1)S(1)}, bf16[1,128,256]{2,1,0:T(8,128)(2,1)S(1)}, u32[]{:S(2)}, u32[]{:S(2)}) %collective-permute-start.17) | collective-permute-done | bytes 65568 | tf_op jit(solution)/shard_map/ppermute | solution.py:564
  73.9 1.7 %collective-permute-done.19.refs_4_ = bf16[1,128,256]{2,1,0:T(8,128)(2,1)S(1)} collective-permute-done((bf16[1,128,256]{2,1,0:T(8,128)(2,1)S(1)}, bf16[1,128,256]{2,1,0:T(8,128)(2,1)S(1)}, u32[]{:S(2)}, u32[]{:S(2)}) %collective-permute-start.19) | collective-permute-done | bytes 65568 | tf_op jit(solution)/shard_map/ppermute | solution.py:564
  75.6 4.2 %attend_head.2.refs_5_ = bf16[512,2048]{1,0:T(8,128)(2,1)} custom-call(s32[24]{0:T(128)S(1)} %copy-done.2, bf16[512,2048]{1,0:T(8,128)(2,1)S(1)} %query_norm.1.query_ref, bf16[2,128,256]{2,1,0:T(8,128)(2,1)S(1)} %get-tuple-element.41.refs_0_, bf16[2,128,256]{2,1,0:T(8,128)(2,1)S(1)} %collective-permute-done.16.refs_1_, ...), custom_call_target="tpu_custom_call" | custom-call | flops 2147483648 | bytes 2097152 | tf_op jit(solution)/shard_map/attend_head/pallas_call | solution.py:453
  79.8 4.2 %attend_head.3 = bf16[512,2048]{1,0:T(8,128)(2,1)} custom-call(s32[24]{0:T(128)S(1)} %copy-done.2, bf16[512,2048]{1,0:T(8,128)(2,1)S(1)} %query_norm.1.query_ref, bf16[2,128,256]{2,1,0:T(8,128)(2,1)S(1)} %get-tuple-element.33.refs_0_, bf16[2,128,256]{2,1,0:T(8,128)(2,1)S(1)} %collective-permute-done.9.refs_1_, ...), custom_call_target="tpu_custom_call", output_to_operand_aliasing={{}: (7, {})} | custom-call | flops 2147483648 | bytes 2097152 | tf_op jit(solution)/shard_map/attend_head/pallas_call | solution.py:453
  (60 shorter events, 8.2 us)
Async XLA Ops:
  1.2 12.1 %collective-permute-start.1 = (bf16[512,320]{1,0:T(8,128)(2,1)S(1)}, bf16[512,320]{1,0:T(8,128)(2,1)S(1)}, u32[]{:S(2)}, u32[]{:S(2)}) collective-permute-start(bf16[512,320]{1,0:T(8,128)(2,1)S(1)} %bitcast.7), channel_id=1, source_target_pairs={{0,2},{1,3},{2,0},{3,1},{4,6},{5,7},{6,4},{7,5},{8,10},{9,11},{10,... | collective-permute-start | bytes 983048 | tf_op jit(solution)/shard_map/ppermute | solution.py:504
  4.2 11.3 %collective-permute-start = (bf16[512,320]{1,0:T(8,128)(2,1)S(1)}, bf16[512,320]{1,0:T(8,128)(2,1)S(1)}, u32[]{:S(2)}, u32[]{:S(2)}) collective-permute-start(bf16[512,320]{1,0:T(8,128)(2,1)S(1)} %bitcast.8), channel_id=1, source_target_pairs={{0,1},{1,0},{2,3},{3,2},{4,5},{5,4},{6,7},{7,6},{8,9},{9,8},{10,11... | collective-permute-start | bytes 983048 | tf_op jit(solution)/shard_map/ppermute | solution.py:504
  13.3 2.2 %collective-permute-start.2 = (bf16[512,320]{1,0:T(8,128)(2,1)S(1)}, bf16[512,320]{1,0:T(8,128)(2,1)S(1)}, u32[]{:S(2)}, u32[]{:S(2)}) collective-permute-start(bf16[512,320]{1,0:T(8,128)(2,1)S(1)} %collective-permute-done.1.refs_2_), channel_id=1, source_target_pairs={{0,1},{1,0},{2,3},{3,2},{4,5},{5,4},{6,7},{7,6},{8,9},{9,8},{10,11... | collective-permute-start | bytes 983048 | tf_op jit(solution)/shard_map/ppermute | solution.py:504
  15.5 25.9 %copy-start.3 = (s32[2]{0:T(128)}, s32[2]{0:T(128)S(1)}, u32[]{:S(2)}) copy-start(s32[2]{0:T(128)S(1)} %pad_add_fusion.where_ref) | copy-start | bytes 28
  25.3 3.4 %collective-permute-start.4 = (bf16[640,256]{1,0:T(8,128)(2,1)S(1)}, bf16[640,256]{1,0:T(8,128)(2,1)}, u32[]{:S(2)}, u32[]{:S(2)}) collective-permute-start(bf16[640,256]{1,0:T(8,128)(2,1)S(1)} %get-tuple-element.28), channel_id=1, source_target_pairs={{0,1},{1,0},{2,3},{3,2},{4,5},{5,4},{6,7},{7,6},{8,9},{9,8},{10,11... | collective-permute-start | bytes 983048 | tf_op jit(solution)/shard_map/ppermute | solution.py:490
  28.6 12.7 %collective-permute-start.3 = (bf16[640,256]{1,0:T(8,128)(2,1)S(1)}, bf16[640,256]{1,0:T(8,128)(2,1)S(1)}, u32[]{:S(2)}, u32[]{:S(2)}) collective-permute-start(bf16[640,256]{1,0:T(8,128)(2,1)S(1)} %get-tuple-element.26), channel_id=1, source_target_pairs={{0,1},{1,0},{2,3},{3,2},{4,5},{5,4},{6,7},{7,6},{8,9},{9,8},{10,11... | collective-permute-start | bytes 983048 | tf_op jit(solution)/shard_map/ppermute | solution.py:490
  29.8 11.6 %collective-permute-start.5 = (bf16[640,256]{1,0:T(8,128)(2,1)S(1)}, bf16[640,256]{1,0:T(8,128)(2,1)S(1)}, u32[]{:S(2)}, u32[]{:S(2)}) collective-permute-start(bf16[640,256]{1,0:T(8,128)(2,1)S(1)} %add_convert_fusion), channel_id=1, source_target_pairs={{0,2},{1,3},{2,0},{3,1},{4,6},{5,7},{6,4},{7,5},{8,10},{9,11},{10,... | collective-permute-start | bytes 983048 | tf_op jit(solution)/shard_map/ppermute | solution.py:490
  43.3 11.9 %copy-start.4 = (f32[128]{0:T(128)S(1)}, f32[128]{0:T(128)}, u32[]{:S(2)}) copy-start(f32[128]{0:T(128)} %param.26) | copy-start | bytes 1540
  43.3 2.6 %collective-permute-start.14 = (bf16[512,256]{1,0:T(8,128)(2,1)S(1)}, bf16[512,256]{1,0:T(8,128)(2,1)S(1)}, u32[]{:S(2)}, u32[]{:S(2)}) collective-permute-start(bf16[512,256]{1,0:T(8,128)(2,1)S(1)} %get-tuple-element.40), channel_id=1, source_target_pairs={{0,1},{1,0},{2,3},{3,2},{4,5},{5,4},{6,7},{7,6},{8,9},{9,8},{10,11... | collective-permute-start | bytes 786440 | tf_op jit(solution)/shard_map/ppermute | solution.py:490
  43.6 2.8 %collective-permute-start.7 = (bf16[512,256]{1,0:T(8,128)(2,1)S(1)}, bf16[512,256]{1,0:T(8,128)(2,1)S(1)}, u32[]{:S(2)}, u32[]{:S(2)}) collective-permute-start(bf16[512,256]{1,0:T(8,128)(2,1)S(1)} %get-tuple-element.32), channel_id=1, source_target_pairs={{0,1},{1,0},{2,3},{3,2},{4,5},{5,4},{6,7},{7,6},{8,9},{9,8},{10,11... | collective-permute-start | bytes 786440 | tf_op jit(solution)/shard_map/ppermute | solution.py:490
  45.3 14.3 %collective-permute-start.6 = (bf16[512,256]{1,0:T(8,128)(2,1)S(1)}, bf16[512,256]{1,0:T(8,128)(2,1)S(1)}, u32[]{:S(2)}, u32[]{:S(2)}) collective-permute-start(bf16[512,256]{1,0:T(8,128)(2,1)S(1)} %get-tuple-element.30), channel_id=1, source_target_pairs={{0,1},{1,0},{2,3},{3,2},{4,5},{5,4},{6,7},{7,6},{8,9},{9,8},{10,11... | collective-permute-start | bytes 786440 | tf_op jit(solution)/shard_map/ppermute | solution.py:490
  45.6 2.6 %collective-permute-start.13 = (bf16[512,256]{1,0:T(8,128)(2,1)S(1)}, bf16[512,256]{1,0:T(8,128)(2,1)S(1)}, u32[]{:S(2)}, u32[]{:S(2)}) collective-permute-start(bf16[512,256]{1,0:T(8,128)(2,1)S(1)} %get-tuple-element.38), channel_id=1, source_target_pairs={{0,1},{1,0},{2,3},{3,2},{4,5},{5,4},{6,7},{7,6},{8,9},{9,8},{10,11... | collective-permute-start | bytes 786440 | tf_op jit(solution)/shard_map/ppermute | solution.py:490
  45.9 20.7 %copy-start = (bf16[512,2048]{1,0:T(8,128)(2,1)S(1)}, bf16[512,2048]{1,0:T(8,128)(2,1)}, u32[]{:S(2)}) copy-start(bf16[512,2048]{1,0:T(8,128)(2,1)} %query_ref.1) | copy-start | bytes 6291460
  45.9 20.7 %copy-start.5 = (f32[128]{0:T(128)S(1)}, f32[128]{0:T(128)}, u32[]{:S(2)}) copy-start(f32[128]{0:T(128)} %param.27) | copy-start | bytes 1540
  46.0 9.2 %collective-permute-start.15 = (bf16[512,256]{1,0:T(8,128)(2,1)S(1)}, bf16[512,256]{1,0:T(8,128)(2,1)S(1)}, u32[]{:S(2)}, u32[]{:S(2)}) collective-permute-start(bf16[512,256]{1,0:T(8,128)(2,1)S(1)} %add_convert_fusion.2), channel_id=1, source_target_pairs={{0,2},{1,3},{2,0},{3,1},{4,6},{5,7},{6,4},{7,5},{8,10},{9,11},{10,... | collective-permute-start | bytes 786440 | tf_op jit(solution)/shard_map/ppermute | solution.py:490
  46.4 13.7 %collective-permute-start.8 = (bf16[512,256]{1,0:T(8,128)(2,1)S(1)}, bf16[512,256]{1,0:T(8,128)(2,1)S(1)}, u32[]{:S(2)}, u32[]{:S(2)}) collective-permute-start(bf16[512,256]{1,0:T(8,128)(2,1)S(1)} %add_convert_fusion.4), channel_id=1, source_target_pairs={{0,2},{1,3},{2,0},{3,1},{4,6},{5,7},{6,4},{7,5},{8,10},{9,11},{10,... | collective-permute-start | bytes 786440 | tf_op jit(solution)/shard_map/ppermute | solution.py:490
  55.9 9.3 %collective-permute-start.18 = (bf16[2,128,256]{2,1,0:T(8,128)(2,1)S(1)}, bf16[2,128,256]{2,1,0:T(8,128)(2,1)S(1)}, u32[]{:S(2)}, u32[]{:S(2)}) collective-permute-start(bf16[2,128,256]{2,1,0:T(8,128)(2,1)S(1)} %get-tuple-element.44), channel_id=1, source_target_pairs={{0,12},{4,8},{8,4},{12,0},{1,13},{5,9},{9,5},{13,1},{2,14},{6,10},... | collective-permute-start | bytes 393224 | tf_op jit(solution)/shard_map/ppermute | solution.py:564
  60.8 10.3 %collective-permute-start.11 = (bf16[2,128,256]{2,1,0:T(8,128)(2,1)S(1)}, bf16[2,128,256]{2,1,0:T(8,128)(2,1)S(1)}, u32[]{:S(2)}, u32[]{:S(2)}) collective-permute-start(bf16[2,128,256]{2,1,0:T(8,128)(2,1)S(1)} %get-tuple-element.36), channel_id=1, source_target_pairs={{0,12},{4,8},{8,4},{12,0},{1,13},{5,9},{9,5},{13,1},{2,14},{6,10},... | collective-permute-start | bytes 393224 | tf_op jit(solution)/shard_map/ppermute | solution.py:564
  64.5 9.5 %collective-permute-start.16 = (bf16[2,128,256]{2,1,0:T(8,128)(2,1)S(1)}, bf16[2,128,256]{2,1,0:T(8,128)(2,1)S(1)}, u32[]{:S(2)}, u32[]{:S(2)}) collective-permute-start(bf16[2,128,256]{2,1,0:T(8,128)(2,1)S(1)} %get-tuple-element.42), channel_id=1, source_target_pairs={{0,4},{4,0},{8,12},{12,8},{1,5},{5,1},{9,13},{13,9},{2,6},{6,2},{1... | collective-permute-start | bytes 393224 | tf_op jit(solution)/shard_map/ppermute | solution.py:564
  64.5 9.3 %collective-permute-start.17 = (bf16[1,128,256]{2,1,0:T(8,128)(2,1)S(1)}, bf16[1,128,256]{2,1,0:T(8,128)(2,1)S(1)}, u32[]{:S(2)}, u32[]{:S(2)}) collective-permute-start(bf16[1,128,256]{2,1,0:T(8,128)(2,1)S(1)} %get-tuple-element.43), channel_id=1, source_target_pairs={{0,8},{4,12},{8,0},{12,4},{1,9},{5,13},{9,1},{13,5},{2,10},{6,14},... | collective-permute-start | bytes 196616 | tf_op jit(solution)/shard_map/ppermute | solution.py:564
  65.3 10.3 %collective-permute-start.19 = (bf16[1,128,256]{2,1,0:T(8,128)(2,1)S(1)}, bf16[1,128,256]{2,1,0:T(8,128)(2,1)S(1)}, u32[]{:S(2)}, u32[]{:S(2)}) collective-permute-start(bf16[1,128,256]{2,1,0:T(8,128)(2,1)S(1)} %slice.9), channel_id=1, source_target_pairs={{0,4},{4,0},{8,12},{12,8},{1,5},{5,1},{9,13},{13,9},{2,6},{6,2},{1... | collective-permute-start | bytes 196616 | tf_op jit(solution)/shard_map/ppermute | solution.py:564
  68.1 11.7 %collective-permute-start.10 = (bf16[1,128,256]{2,1,0:T(8,128)(2,1)S(1)}, bf16[1,128,256]{2,1,0:T(8,128)(2,1)S(1)}, u32[]{:S(2)}, u32[]{:S(2)}) collective-permute-start(bf16[1,128,256]{2,1,0:T(8,128)(2,1)S(1)} %get-tuple-element.35), channel_id=1, source_target_pairs={{0,8},{4,12},{8,0},{12,4},{1,9},{5,13},{9,1},{13,5},{2,10},{6,14},... | collective-permute-start | bytes 196616 | tf_op jit(solution)/shard_map/ppermute | solution.py:564
  71.1 8.7 %collective-permute-start.9 = (bf16[2,128,256]{2,1,0:T(8,128)(2,1)S(1)}, bf16[2,128,256]{2,1,0:T(8,128)(2,1)S(1)}, u32[]{:S(2)}, u32[]{:S(2)}) collective-permute-start(bf16[2,128,256]{2,1,0:T(8,128)(2,1)S(1)} %get-tuple-element.34), channel_id=1, source_target_pairs={{0,4},{4,0},{8,12},{12,8},{1,5},{5,1},{9,13},{13,9},{2,6},{6,2},{1... | collective-permute-start | bytes 393224 | tf_op jit(solution)/shard_map/ppermute | solution.py:564
  73.8 6.0 %collective-permute-start.12 = (bf16[1,128,256]{2,1,0:T(8,128)(2,1)S(1)}, bf16[1,128,256]{2,1,0:T(8,128)(2,1)S(1)}, u32[]{:S(2)}, u32[]{:S(2)}) collective-permute-start(bf16[1,128,256]{2,1,0:T(8,128)(2,1)S(1)} %slice.8), channel_id=1, source_target_pairs={{0,4},{4,0},{8,12},{12,8},{1,5},{5,1},{9,13},{13,9},{2,6},{6,2},{1... | collective-permute-start | bytes 196616 | tf_op jit(solution)/shard_map/ppermute | solution.py:564
  (6 other events, 30.4 us)

commit v2 on v1

--- a/solution.py
+++ b/solution.py
@@ -21,6 +21,7 @@
 F32 = jnp.float32
 BF16 = jnp.bfloat16
 VMEM = pl.BlockSpec(memory_space=pltpu.VMEM)
+HBM = pl.BlockSpec(memory_space=pl.ANY)
 SMEM = pl.BlockSpec(memory_space=pltpu.SMEM)
 MIB = 1024 * 1024
 
@@ -45,6 +46,19 @@
 
 def xor_pairs(count, mask):
     return [(i, i ^ mask) for i in range(count)]
+
+
+def lane_rows(vector):
+    return jnp.pad(vector, (0, -vector.shape[0] % LANES)).reshape(-1, LANES)
+
+
+def one_row(ref, width):
+    rows = [ref[n : n + 1, :] for n in range(ref.shape[0])]
+    return (rows[0] if len(rows) == 1 else jnp.concatenate(rows, axis=1))[:, :width]
+
+
+def column_step(width):
+    return HIDDEN_BLOCK if width % HIDDEN_BLOCK == 0 else width
 
 
 def tail_plan(rows, width):
@@ -98,6 +112,7 @@
     my_first, my_count = pick(firsts, group), pick(counts, group)
     my_offset = pick(offsets, group)
     place = meta_places(group_count)
+    meta_ref[place["tp"]] = where_ref[1]
     meta_ref[place["first"]] = my_first
     meta_ref[place["second"]] = my_count - my_first
     meta_ref[place["text_first"]] = pick(texts_first, group)
@@ -129,52 +144,46 @@
         "text_first": 2,
         "text_both": 3,
         "star": 4,
+        "tp": 5,
         "send": 8,
         "goes": 8 + table,
         "size": 8 + 2 * table,
     }
 
 
-def request_layout(group_count, tiles_local, where, tiles_per_request, owner, text_per_request):
-    size = meta_places(group_count)["size"]
-    return pl.pallas_call(
-        functools.partial(layout_kernel, group_count, tiles_local),
-        out_shape=jax.ShapeDtypeStruct((size,), jnp.int32),
-        in_specs=[SMEM] * 4,
-        out_specs=SMEM,
-        cost_estimate=pl.CostEstimate(flops=1000, bytes_accessed=4000, transcendentals=0),
-        name="request_layout",
-    )(where, tiles_per_request, owner, text_per_request)
-
-
-def mlp_kernel(piece_count, where_ref, *refs):
+def mlp_kernel(piece_count, place, meta_ref, *refs):
     pieces = refs[:piece_count]
-    gain_ref, bias_ref, up_ref, up_bias_ref, down_ref = refs[piece_count : piece_count + 5]
+    gain_ref, bias_ref, up_bias_ref, up_ref, down_ref = refs[piece_count : piece_count + 5]
     outs = refs[piece_count + 5 : 2 * piece_count + 5]
-    normed_ref, hidden_ref, total_ref = refs[2 * piece_count + 5 :]
-    index = where_ref[1]
-    rows, width = pieces[0].shape
-    channels = width * piece_count
-    for row in range(0, rows, ROW_BLOCK):
-        take = pl.ds(row, ROW_BLOCK)
-        blocks = xor_order([piece[take, :].astype(F32) for piece in pieces], index)
-        values = jnp.concatenate(blocks, axis=1)
+    cat_ref, normed_ref, hidden_ref, total_ref = refs[2 * piece_count + 5 :]
+    index = meta_ref[place]
+    tiles, width, tile_rows = pieces[0].shape
+    rows = tiles * tile_rows
+    channels, hidden_width = up_ref.shape
+    up_step = column_step(hidden_width)
+    down_step = column_step(channels)
+
+    gain, bias = one_row(gain_ref, channels), one_row(bias_ref, channels)
+    up_bias = one_row(up_bias_ref, hidden_width)
+    for tile in range(tiles):
+        for k, piece in enumerate(pieces):
+            start = pl.multiple_of((index ^ k) * width, math.gcd(width, LANES))
+            cat_ref[pl.ds(start, width), :] = piece[tile]
+        values = cat_ref[...].T.astype(F32)
         average = jnp.sum(values, axis=1, keepdims=True) * (1.0 / channels)
         centered = values - average
         variance = jnp.sum(centered * centered, axis=1, keepdims=True) * (1.0 / channels)
-        normed = centered * lax.rsqrt(variance + epsilon) * gain_ref[...] + bias_ref[...]
-        normed_ref[take, :] = normed.astype(BF16)
-    hidden_width = up_ref.shape[1]
-    step = math.gcd(hidden_width, HIDDEN_BLOCK)
-    for col in range(0, hidden_width, step):
-        take = pl.ds(col, step)
+        normed = centered * lax.rsqrt(variance + epsilon)
+        normed = normed * gain + bias
+        normed_ref[tile * tile_rows : (tile + 1) * tile_rows, :] = normed.astype(BF16)
+    for n in range(hidden_width // up_step):
+        take = slice(n * up_step, (n + 1) * up_step)
         value = jnp.dot(normed_ref[...], up_ref[:, take], preferred_element_type=F32)
-        value = value + up_bias_ref[:, take]
+        value = value + up_bias[:, take]
         value = 0.5 * value * (1.0 + lax.erf(value * (1.0 / math.sqrt(2.0))))
         hidden_ref[:, take] = value.astype(BF16)
-    step = math.gcd(channels, HIDDEN_BLOCK)
-    for col in range(0, channels, step):
-        take = pl.ds(col, step)
+    for n in range(channels // down_step):
+        take = slice(n * down_step, (n + 1) * down_step)
         total_ref[:, take] = jnp.dot(
             hidden_ref[...], down_ref[:, take], preferred_element_type=F32
         )
@@ -185,29 +194,32 @@
         for out, block in zip(outs, xor_order(blocks, index)):
             block = block.astype(BF16)
             if packed:
+                part = row // ROW_BLOCK
                 out[take, :] = block[:, :whole]
-                out[rows : rows + ROW_BLOCK, row // ROW_BLOCK * tail : (row // ROW_BLOCK + 1) * tail] = block[:, whole:]
+                out[rows : rows + ROW_BLOCK, part * tail : (part + 1) * tail] = block[:, whole:]
             else:
                 out[take, :] = block
 
 
-def encoder_mlp(where, pieces, ln_gain, ln_bias, w_up, b_up, w_down):
-    rows, width = pieces[0].shape
+def encoder_mlp(meta, place, pieces, ln_gain, ln_bias, w_up, b_up, w_down):
+    tiles, width, tile_rows = pieces[0].shape
+    rows = tiles * tile_rows
     count = len(pieces)
     channels, hidden_width = w_up.shape
     whole, _, packed = tail_plan(rows, width)
     shape = (rows + ROW_BLOCK, whole) if packed else (rows, width)
     return pl.pallas_call(
-        functools.partial(mlp_kernel, count),
+        functools.partial(mlp_kernel, count, place),
         out_shape=[jax.ShapeDtypeStruct(shape, BF16)] * count,
         in_specs=[SMEM] + [VMEM] * (count + 5),
         out_specs=[VMEM] * count,
         scratch_shapes=[
+            pltpu.VMEM((channels, tile_rows), BF16),
             pltpu.VMEM((rows, channels), BF16),
             pltpu.VMEM((rows, hidden_width), BF16),
             pltpu.VMEM((rows, channels), F32),
         ],
-        compiler_params=pltpu.CompilerParams(vmem_limit_bytes=32 * MIB),
+        compiler_params=pltpu.CompilerParams(vmem_limit_bytes=44 * MIB),
         cost_estimate=pl.CostEstimate(
             flops=4 * rows * channels * hidden_width,
             bytes_accessed=4 * channels * hidden_width + 4 * rows * channels,
@@ -215,62 +227,114 @@
         ),
         name="encoder_mlp",
     )(
-        where,
+        meta,
         *pieces,
-        ln_gain.reshape(1, channels),
-        ln_bias.reshape(1, channels),
+        lane_rows(ln_gain),
+        lane_rows(ln_bias),
+        lane_rows(b_up),
         w_up,
-        b_up.reshape(1, hidden_width),
         w_down,
     )
 
 
-def tap_kernel(where_ref, tap_ref, weight_ref, out_ref):
+def prepare_kernel(
+    group_count,
+    tiles_local,
+    where_ref,
+    tiles_ref,
+    owner_ref,
+    text_ref,
+    gain_ref,
+    tap_ref,
+    weight_ref,
+    query_ref,
+    out_ref,
+    normed_ref,
+    meta_ref,
+    row_ref,
+):
+    @pl.when(pl.program_id(0) == 0)
+    def _():
+        layout_kernel(
+            group_count, tiles_local, where_ref, tiles_ref, owner_ref, text_ref, meta_ref
+        )
+        tiles, _, tile_rows = tap_ref.shape
+        for tile in range(tiles):
+            row_ref[tile * tile_rows : (tile + 1) * tile_rows, :] = tap_ref[tile].T
+
     out_ref[...] = jnp.dot(
-        tap_ref[...], weight_ref[...], preferred_element_type=F32
+        row_ref[...], weight_ref[...], preferred_element_type=F32
     ).astype(BF16)[None, None]
-
-
-def tap_projection(where, tap_rows, weights, head_count, dest_count, dup):
-    rows, depth = tap_rows.shape
+    gain = gain_ref[...] * (math.log2(math.e) / math.sqrt(HD))
+    for col in range(0, query_ref.shape[1], HD):
+        values = query_ref[:, col : col + HD].astype(F32)
+        square = jnp.sum(values * values, axis=1, keepdims=True) * (1.0 / HD)
+        normed_ref[:, col : col + HD] = (values * lax.rsqrt(square + epsilon) * gain).astype(BF16)
+
+
+def prepare(
+    where, requests, q_gain, tap_tiles, weights, queries, group_count, head_count, dest_count, dup
+):
+    tiles, depth, tile_rows = tap_tiles.shape
+    rows = tiles * tile_rows
     block = 2 * HD
+    steps = head_count * dest_count
+    text_rows, width = queries.shape
+    query_step = text_rows // steps
+    meta_size = meta_places(group_count)["size"]
 
     def head_of(n, where_ref):
         dest = lax.div(where_ref[1], jnp.int32(dup)) ^ lax.rem(n, dest_count)
         return dest * head_count + lax.div(n, dest_count)
 
     return pl.pallas_call(
-        tap_kernel,
-        out_shape=jax.ShapeDtypeStruct((head_count, dest_count, rows, block), BF16),
+        functools.partial(prepare_kernel, group_count, tiles),
+        out_shape=[
+            jax.ShapeDtypeStruct((head_count, dest_count, rows, block), BF16),
+            jax.ShapeDtypeStruct((text_rows, width), BF16),
+            jax.ShapeDtypeStruct((meta_size,), jnp.int32),
+        ],
         grid_spec=pltpu.PrefetchScalarGridSpec(
             num_scalar_prefetch=1,
-            grid=(head_count * dest_count,),
+            grid=(steps,),
             in_specs=[
-                pl.BlockSpec((rows, depth), lambda n, w: (0, 0)),
+                SMEM,
+                SMEM,
+                SMEM,
+                pl.BlockSpec((1, HD), lambda n, w: (0, 0)),
+                pl.BlockSpec(tap_tiles.shape, lambda n, w: (0, 0, 0)),
                 pl.BlockSpec((depth, block), lambda n, w: (0, head_of(n, w))),
+                pl.BlockSpec((query_step, width), lambda n, w: (n, 0)),
             ],
-            out_specs=pl.BlockSpec(
-                (1, 1, rows, block),
-                lambda n, w: (lax.div(n, dest_count), lax.rem(n, dest_count), 0, 0),
-            ),
+            out_specs=[
+                pl.BlockSpec(
+                    (1, 1, rows, block),
+                    lambda n, w: (lax.div(n, dest_count), lax.rem(n, dest_count), 0, 0),
+                ),
+                pl.BlockSpec((query_step, width), lambda n, w: (n, 0)),
+                SMEM,
+            ],
+            scratch_shapes=[pltpu.VMEM((rows, depth), BF16)],
         ),
-        compiler_params=pltpu.CompilerParams(vmem_limit_bytes=16 * MIB),
+        compiler_params=pltpu.CompilerParams(vmem_limit_bytes=44 * MIB),
         cost_estimate=pl.CostEstimate(
             flops=2 * rows * depth * weights.shape[1],
             bytes_accessed=2 * depth * weights.shape[1],
             transcendentals=0,
         ),
-        name="tap_projection",
-    )(where, tap_rows, weights)
-
-
-def kv_kernel(head_count, dest_count, dup, term_count, where_ref, *refs):
+        name="prepare",
+    )(where, *requests, lane_rows(q_gain), tap_tiles, weights, queries)
+
+
+def kv_kernel(head_count, dest_count, dup, place, term_count, meta_ref, *refs):
     x_ref, bias_ref, weight_ref, tap_ref = refs[:4]
     terms = refs[4 : 4 + term_count]
     outs = refs[4 + term_count : -1]
     encoded_ref = refs[-1]
-    rows, width = x_ref.shape
+    tiles, width, tile_rows = x_ref.shape
+    rows = tiles * tile_rows
     whole, tail, packed = tail_plan(rows, width)
+    bias = one_row(bias_ref, width)
     for row in range(0, rows, ROW_BLOCK):
         take = pl.ds(row, ROW_BLOCK)
 
@@ -287,9 +351,11 @@
             total = jnp.concatenate([main, rest], axis=1)
         else:
             total = summed(take, slice(None))
-        encoded_ref[take, :] = (x_ref[take, :].astype(F32) + total + bias_ref[...]).astype(BF16)
+        total = total + x_ref[row // ROW_BLOCK].T.astype(F32)
+        total = total + bias
+        encoded_ref[take, :] = total.astype(BF16)
     block = 2 * HD
-    mine = lax.div(where_ref[1], jnp.int32(dup))
+    mine = lax.div(meta_ref[place], jnp.int32(dup))
     for head in range(head_count):
         for k in range(dest_count):
             column = ((mine ^ k) * head_count + head) * block
@@ -299,12 +365,13 @@
             outs[head * dest_count + k][...] = value.astype(BF16)
 
 
-def kv_projection(where, x_rows, b_down, weights, tap_part, terms, dup):
-    rows, width = x_rows.shape
+def kv_projection(meta, place, x_tiles, b_down, weights, tap_part, terms, dup):
+    tiles, width, tile_rows = x_tiles.shape
+    rows = tiles * tile_rows
     head_count, dest_count = tap_part.shape[:2]
     block = 2 * HD
     outs = pl.pallas_call(
-        functools.partial(kv_kernel, head_count, dest_count, dup, len(terms)),
+        functools.partial(kv_kernel, head_count, dest_count, dup, place, len(terms)),
         out_shape=[jax.ShapeDtypeStruct((rows, block), BF16)] * (head_count * dest_count),
         in_specs=[SMEM] + [VMEM] * (4 + len(terms)),
         out_specs=[VMEM] * (head_count * dest_count),
@@ -316,7 +383,7 @@
             transcendentals=0,
         ),
         name="kv_projection",
-    )(where, x_rows, b_down.reshape(1, width), weights, tap_part, *terms)
+    )(meta, x_tiles, lane_rows(b_down), weights, tap_part, *terms)
     return [outs[h * dest_count : (h + 1) * dest_count] for h in range(head_count)]
 
 
@@ -354,35 +421,7 @@
             flops=10 * rows * block, bytes_accessed=10 * rows * block, transcendentals=rows
         ),
         name="finish_tiles",
-    )(meta, k_gain.reshape(1, HD), *terms)
-
-
-def query_kernel(gain_ref, query_ref, out_ref):
-    gain = gain_ref[...] * (math.log2(math.e) / math.sqrt(HD))
-    for col in range(0, query_ref.shape[1], HD):
-        values = query_ref[:, col : col + HD].astype(F32)
-        square = jnp.sum(values * values, axis=1, keepdims=True) * (1.0 / HD)
-        out_ref[:, col : col + HD] = (values * lax.rsqrt(square + epsilon) * gain).astype(BF16)
-
-
-def query_norm(queries, q_gain):
-    rows, width = queries.shape
-    step = math.gcd(rows, 128)
-    return pl.pallas_call(
-        query_kernel,
-        out_shape=jax.ShapeDtypeStruct((rows, width), BF16),
-        grid=(rows // step,),
-        in_specs=[
-            pl.BlockSpec((1, HD), lambda i: (0, 0)),
-            pl.BlockSpec((step, width), lambda i: (i, 0)),
-        ],
-        out_specs=pl.BlockSpec((step, width), lambda i: (i, 0)),
-        compiler_params=pltpu.CompilerParams(vmem_limit_bytes=16 * MIB),
-        cost_estimate=pl.CostEstimate(
-            flops=8 * rows * width, bytes_accessed=4 * rows * width, transcendentals=rows * width // HD
-        ),
-        name="query_norm",
-    )(q_gain.reshape(1, HD), queries)
+    )(meta, lane_rows(k_gain), *terms)
 
 
 def attend_kernel(group_count, sources, has_base, meta_ref, query_ref, *refs):
@@ -496,13 +535,17 @@
     return [blocks[0]]
 
 
-def gather_pieces(own, count):
+def gather_pieces(own, count, ready):
+    bits = bits_of(count)
     pieces = {0: own}
-    for b in reversed(range(bits_of(count))):
+    for b in reversed(range(bits)):
         pairs = xor_pairs(count, 1 << b)
-        for k in list(pieces):
-            pieces[k | (1 << b)] = lax.ppermute(pieces[k], "tp", pairs)
-    return [pieces[k] for k in range(count)]
+        for k in sorted(pieces):
+            block = pieces[k]
+            if b == 0 and k:
+                block, ready = lax.optimization_barrier((block, ready))
+            pieces[k | (1 << b)] = lax.ppermute(block, "tp", pairs)
+    return [pieces[k] for k in range(count)], ready
 
 
 def local(
@@ -526,27 +569,35 @@
     group_count = lax.axis_size("grp")
     tp_count = lax.axis_size("tp")
     where = jnp.stack([lax.axis_index("grp"), lax.axis_index("tp")]).astype(jnp.int32)
-    tiles_local, _, tile_rows, channel_share = x_in.shape
-    local_rows = tiles_local * tile_rows
-    x_rows = x_in.reshape(local_rows, channel_share)
-    tap_rows = taps.reshape(local_rows, taps.shape[3])
-
+    tiles_local = x_in.shape[0]
+    x_tiles = jnp.swapaxes(x_in, 2, 3)[:, 0]
+    tap_tiles = jnp.swapaxes(taps, 2, 3)[:, 0]
     head_count = max(1, KVH // tp_count)
     dup = max(1, tp_count // KVH)
     dest_count = tp_count // dup
-
-    pieces = gather_pieces(x_rows, tp_count)
-    tap_part = tap_projection(where, tap_rows, kv_w_taps, head_count, dest_count, dup)
-    query_rows = query_norm(queries, q_gain)
-    meta = request_layout(
-        group_count, tiles_local, where, tiles_per_request, owner, text_per_request
+    place = meta_places(group_count)
+
+    tap_part, query_rows, meta = prepare(
+        where,
+        (tiles_per_request, owner, text_per_request),
+        q_gain,
+        tap_tiles,
+        kv_w_taps,
+        queries,
+        group_count,
+        head_count,
+        dest_count,
+        dup,
     )
-
-    mlp_blocks = encoder_mlp(where, pieces, ln_gain, ln_bias, w_up, b_up, w_down)
+    pieces, meta = gather_pieces(x_tiles, tp_count, meta)
+    mlp_blocks = encoder_mlp(
+        meta, place["tp"], pieces, ln_gain, ln_bias, w_up, b_up, w_down
+    )
     mlp_terms = scatter_sum(mlp_blocks, tp_count, 0)
-    kv_blocks = kv_projection(where, x_rows, b_down, kv_w_out, tap_part, mlp_terms, dup)
-
-    place = meta_places(group_count)
+    kv_blocks = kv_projection(
+        meta, place["tp"], x_tiles, b_down, kv_w_out, tap_part, mlp_terms, dup
+    )
+
     slots = slot_count_of(group_count)
     total_tiles = group_count * tiles_local
     most_other = total_tiles - REQ_G * MAXT - REQ_G * (group_count - 2)

time: 85.7 us -> 79.7 us (0.930); the launches traced: 84.1 us -> 79.1 us
  local copies, waits for them, and re-layouts: 12.8 us -> 5.7 us
  waiting for transfers between devices: 20.2 us -> 23.5 us
  other arithmetic: 1.48 us -> 0.53 us
    ppermute x9, waiting for transfers between devices: 7.32 us -> 18.5 us  [scatter_sum(): got[k ^ 1 << b] = lax.ppermute(blocks[k], 'tp', pairs)]
    ppermute x3, waiting for transfers between devices: 9.12 us -> 1.4 us  [gather_pieces(): pieces[k | 1 << b] = lax.ppermute(block, 'tp', pairs)]
    unnamed x22 -> x30, local copies, waits for them, and re-layouts: 10.6 us -> 5.68 us
    reshape x4 -> x1, local copies, waits for them, and re-layouts: 2.11 us -> 0.01 us  [lane_rows(): return jnp.pad(vector, (0, -vector.shape[0] % LANES)).reshape(-1, LANES)]
    ppermute x9, starting transfers between devices: 5.77 us -> 4.03 us  [scatter_sum(): got[k ^ 1 << b] = lax.ppermute(blocks[k], 'tp', pairs)]
    ppermute x8, starting transfers between devices: 13.2 us -> 14.7 us  [move(): return lax.ppermute(value, 'grp', xor_pairs(group_count, mask))]
    convert_element_type x6, other arithmetic: 1.41 us -> 0.46 us  [add_rounded(): return (a.astype(F32) + b.astype(F32)).astype(BF16)]
    pallas_call x4 -> x2, Pallas kernels: 15.7 us -> 15.4 us  [the longest x1 9.77 us: prepare(): pl.pallas_call(functools.partial(prepare_kernel, group_count, tiles), out...]
  transfers between devices with their start and end apart: 20 -> 20, of which waited for: 5 -> 9; matrix products, arithmetic and copies ran while one was open for 8% -> 1% of each run, Pallas kernels for 18% -> 19%
where the time goes in v2:
time: 79.7 us; the launch traced here: 79.1 us
  Pallas kernels  27.2 us (34%)
  waiting for transfers between devices  23.5 us (29%)
  starting transfers between devices  22 us (28%)
  local copies, waits for them, and re-layouts  5.7 us (7%)
    ppermute x9, waiting for transfers between devices, scatter_sum(): got[k ^ 1 << b] = lax.ppermute(blocks[k], 'tp', pairs)  18.5 us
    ppermute x8, starting transfers between devices, move(): return lax.ppermute(value, 'grp', xor_pairs(group_count, mask))  14.7 us
    pallas_call x1, Pallas kernels, prepare(): pl.pallas_call(functools.partial(prepare_kernel, group_count, tiles), out...  9.77 us
    pallas_call x2, Pallas kernels, attend_head(): pl.pallas_call(functools.partial(attend_kernel, group_count, sources, len...  8.4 us
    unnamed x30, local copies, waits for them, and re-layouts  5.68 us
    pallas_call x1, Pallas kernels, encoder_mlp(): pl.pallas_call(functools.partial(mlp_kernel, count, place), out_shape=[ja...  5.66 us
    ppermute x9, starting transfers between devices, scatter_sum(): got[k ^ 1 << b] = lax.ppermute(blocks[k], 'tp', pairs)  4.03 us
    ppermute x8, waiting for transfers between devices, move(): return lax.ppermute(value, 'grp', xor_pairs(group_count, mask))  3.69 us
  transfers between devices with their start and end apart: 20, of which 9 were waited for; matrix products, arithmetic and copies ran while one was open for 1% of the time, Pallas kernels for 19%

profile of v2, /device:TPU:0, one launch (start us, length us, event | category | flops | bytes accessed | tf_op | source)
XLA Modules:
  0.0 79.1 jit_solution(550346420008677780)
XLA Ops:
  0.5 2.5 %collective-permute-start = (bf16[4,320,128]{2,1,0:T(8,128)(2,1)}, bf16[4,320,128]{2,1,0:T(8,128)(2,1)S(1)}, u32[]{:S(2)}, u32[]{:S(2)}) collective-permute-start(bf16[4,320,128]{2,1,0:T(8,128)(2,1)} %bitcast.20), channel_id=1, source_target_pairs={{0,2},{1,3},{2,0},{3,1},{4,6},{5,7},{6,4},{7,5},{8,10},{9,11},{10,... | collective-permute-start | bytes 983048 | tf_op jit(solution)/shard_map/ppermute | solution.py:547
  3.0 1.6 %copy-done.5 = bf16[512,2048]{1,0:T(8,128)(2,1)S(1)} copy-done((bf16[512,2048]{1,0:T(8,128)(2,1)S(1)}, bf16[512,2048]{1,0:T(8,128)(2,1)}, u32[]{:S(2)}) %copy-start.5) | copy-done | bytes 2097176
  4.6 1.4 %copy-done.6 = bf16[4,1,128,1600]{2,3,1,0:T(8,128)(2,1)S(1)} copy-done((bf16[4,1,128,1600]{2,3,1,0:T(8,128)(2,1)S(1)}, bf16[4,1,128,1600]{2,3,1,0:T(8,128)(2,1)}, u32[]{:S(2)}) %copy-start.6) | copy-done | bytes 1638424
  6.1 0.7 copy-done.10
  8.7 9.8 %prepare.1 = (bf16[2,4,512,256]{3,2,1,0:T(8,128)(2,1)S(1)}, bf16[512,2048]{1,0:T(8,128)(2,1)S(1)}, s32[24]{0:T(128)S(1)}) custom-call(s32[2]{0:T(128)S(1)} %pad_add_fusion.where_ref, s32[8]{0:T(128)S(1)} %copy-done.10, s32[8]{0:T(128)S(1)} %copy-done.11, s32[8]{0:T(128)S(1)} %copy-done.12, f32[1,128]{1,0:T(1,128)S(1)} %bitcast.29, ...), custom_call_target="tpu_custom_call" | custom-call | flops 3355443200 | bytes 6553600 | tf_op jit(solution)/shard_map/prepare/pallas_call | solution.py:290
  18.8 1.4 %collective-permute-done.2.refs_3_ = bf16[4,320,128]{2,1,0:T(8,128)(2,1)S(1)} collective-permute-done((bf16[4,320,128]{2,1,0:T(8,128)(2,1)S(1)}, bf16[4,320,128]{2,1,0:T(8,128)(2,1)S(1)}, u32[]{:S(2)}, u32[]{:S(2)}) %collective-permute-start.2) | collective-permute-done | bytes 327712 | tf_op jit(solution)/shard_map/ppermute | solution.py:547
  20.3 5.7 %encoder_mlp.1 = (bf16[640,256]{1,0:T(8,128)(2,1)S(1)}, bf16[640,256]{1,0:T(8,128)(2,1)S(1)}, bf16[640,256]{1,0:T(8,128)(2,1)S(1)}, bf16[640,256]{1,0:T(8,128)(2,1)S(1)}) custom-call(s32[24]{0:T(128)S(1)} %get-tuple-element.31.meta_ref, bf16[4,320,128]{2,1,0:T(8,128)(2,1)S(1)} %bitcast.21, bf16[4,320,128]{2,1,0:T(8,128)(2,1)S(1)} %collective-permute-done.1.refs_1_, ...), custom_call_target="tpu_custom_call" | custom-call | flops 3355443200 | bytes 9175040 | tf_op jit(solution)/shard_map/encoder_mlp/pallas_call | solution.py:211
  26.5 1.1 %collective-permute-done.4 = bf16[640,256]{1,0:T(8,128)(2,1)S(1)} collective-permute-done((bf16[640,256]{1,0:T(8,128)(2,1)S(1)}, bf16[640,256]{1,0:T(8,128)(2,1)S(1)}, u32[]{:S(2)}, u32[]{:S(2)}) %collective-permute-start.4) | collective-permute-done | bytes 327712 | tf_op jit(solution)/shard_map/ppermute | solution.py:529
  28.2 9.5 %collective-permute-done.5.refs_5_ = bf16[640,256]{1,0:T(8,128)(2,1)S(1)} collective-permute-done((bf16[640,256]{1,0:T(8,128)(2,1)S(1)}, bf16[640,256]{1,0:T(8,128)(2,1)S(1)}, u32[]{:S(2)}, u32[]{:S(2)}) %collective-permute-start.5) | collective-permute-done | bytes 327712 | tf_op jit(solution)/shard_map/ppermute | solution.py:529
  37.6 1.9 %kv_projection.1 = (bf16[512,256]{1,0:T(8,128)(2,1)S(1)}, bf16[512,256]{1,0:T(8,128)(2,1)S(1)}, bf16[512,256]{1,0:T(8,128)(2,1)S(1)}, bf16[512,256]{1,0:T(8,128)...) custom-call(s32[24]{0:T(128)S(1)} %get-tuple-element.31.meta_ref, ...), custom_call_target="tpu_custom_call" | custom-call | flops 671088640 | bytes 5505024 | tf_op jit(solution)/shard_map/kv_projection/pallas_call | solution.py:373
  41.6 1.8 %collective-permute-start.8 = (bf16[512,256]{1,0:T(8,128)(2,1)S(1)}, bf16[512,256]{1,0:T(8,128)(2,1)S(1)}, u32[]{:S(2)}, u32[]{:S(2)}) collective-permute-start(bf16[512,256]{1,0:T(8,128)(2,1)S(1)} %add_convert_fusion.4), channel_id=1, source_target_pairs={{0,2},{1,3},{2,0},{3,1},{4,6},{5,7},{6,4},{7,5},{8,10},{9,11},{10,... | collective-permute-start | bytes 786440 | tf_op jit(solution)/shard_map/ppermute | solution.py:529
  43.5 6.9 %collective-permute-done.15.refs_1_ = bf16[512,256]{1,0:T(8,128)(2,1)S(1)} collective-permute-done((bf16[512,256]{1,0:T(8,128)(2,1)S(1)}, bf16[512,256]{1,0:T(8,128)(2,1)S(1)}, u32[]{:S(2)}, u32[]{:S(2)}) %collective-permute-start.15) | collective-permute-done | bytes 262176 | tf_op jit(solution)/shard_map/ppermute | solution.py:529
  50.4 0.7 finish_tiles.3
  51.1 3.7 %collective-permute-start.18 = (bf16[2,128,256]{2,1,0:T(8,128)(2,1)S(1)}, bf16[2,128,256]{2,1,0:T(8,128)(2,1)S(1)}, u32[]{:S(2)}, u32[]{:S(2)}) collective-permute-start(bf16[2,128,256]{2,1,0:T(8,128)(2,1)S(1)} %get-tuple-element.54), channel_id=1, source_target_pairs={{0,12},{4,8},{8,4},{12,0},{1,13},{5,9},{9,5},{13,1},{2,14},{6,10},... | collective-permute-start | bytes 393224 | tf_op jit(solution)/shard_map/ppermute | solution.py:615
  55.2 0.7 finish_tiles.2
  55.9 3.7 %collective-permute-start.11 = (bf16[2,128,256]{2,1,0:T(8,128)(2,1)S(1)}, bf16[2,128,256]{2,1,0:T(8,128)(2,1)S(1)}, u32[]{:S(2)}, u32[]{:S(2)}) collective-permute-start(bf16[2,128,256]{2,1,0:T(8,128)(2,1)S(1)} %get-tuple-element.46), channel_id=1, source_target_pairs={{0,12},{4,8},{8,4},{12,0},{1,13},{5,9},{9,5},{13,1},{2,14},{6,10},... | collective-permute-start | bytes 393224 | tf_op jit(solution)/shard_map/ppermute | solution.py:615
  59.6 0.8 collective-permute-start.17
  60.4 1.3 %collective-permute-start.19 = (bf16[1,128,256]{2,1,0:T(8,128)(2,1)S(1)}, bf16[1,128,256]{2,1,0:T(8,128)(2,1)S(1)}, u32[]{:S(2)}, u32[]{:S(2)}) collective-permute-start(bf16[1,128,256]{2,1,0:T(8,128)(2,1)S(1)} %slice.9), channel_id=1, source_target_pairs={{0,4},{4,0},{8,12},{12,8},{1,5},{5,1},{9,13},{13,9},{2,6},{6,2},{1... | collective-permute-start | bytes 196616 | tf_op jit(solution)/shard_map/ppermute | solution.py:615
  61.7 2.9 %collective-permute-start.10 = (bf16[1,128,256]{2,1,0:T(8,128)(2,1)S(1)}, bf16[1,128,256]{2,1,0:T(8,128)(2,1)S(1)}, u32[]{:S(2)}, u32[]{:S(2)}) collective-permute-start(bf16[1,128,256]{2,1,0:T(8,128)(2,1)S(1)} %get-tuple-element.45), channel_id=1, source_target_pairs={{0,8},{4,12},{8,0},{12,4},{1,9},{5,13},{9,1},{13,5},{2,10},{6,14},... | collective-permute-start | bytes 196616 | tf_op jit(solution)/shard_map/ppermute | solution.py:615
  64.6 2.2 %collective-permute-start.9 = (bf16[2,128,256]{2,1,0:T(8,128)(2,1)S(1)}, bf16[2,128,256]{2,1,0:T(8,128)(2,1)S(1)}, u32[]{:S(2)}, u32[]{:S(2)}) collective-permute-start(bf16[2,128,256]{2,1,0:T(8,128)(2,1)S(1)} %get-tuple-element.44), channel_id=1, source_target_pairs={{0,4},{4,0},{8,12},{12,8},{1,5},{5,1},{9,13},{13,9},{2,6},{6,2},{1... | collective-permute-start | bytes 393224 | tf_op jit(solution)/shard_map/ppermute | solution.py:615
  66.8 2.0 %collective-permute-done.17.refs_2_ = bf16[1,128,256]{2,1,0:T(8,128)(2,1)S(1)} collective-permute-done((bf16[1,128,256]{2,1,0:T(8,128)(2,1)S(1)}, bf16[1,128,256]{2,1,0:T(8,128)(2,1)S(1)}, u32[]{:S(2)}, u32[]{:S(2)}) %collective-permute-start.17) | collective-permute-done | bytes 65568 | tf_op jit(solution)/shard_map/ppermute | solution.py:615
  69.1 1.6 %collective-permute-done.19.refs_4_ = bf16[1,128,256]{2,1,0:T(8,128)(2,1)S(1)} collective-permute-done((bf16[1,128,256]{2,1,0:T(8,128)(2,1)S(1)}, bf16[1,128,256]{2,1,0:T(8,128)(2,1)S(1)}, u32[]{:S(2)}, u32[]{:S(2)}) %collective-permute-start.19) | collective-permute-done | bytes 65568 | tf_op jit(solution)/shard_map/ppermute | solution.py:615
  70.7 4.2 %attend_head.2.refs_5_ = bf16[512,2048]{1,0:T(8,128)(2,1)} custom-call(s32[24]{0:T(128)S(1)} %get-tuple-element.31.meta_ref, bf16[512,2048]{1,0:T(8,128)(2,1)S(1)} %get-tuple-element.32.query_ref, bf16[2,128,256]{2,1,0:T(8,128)(2,1)S(1)} %get-tuple-element.51.refs_0_, bf16[2,128,256]{2,1,0:T(8,128)(2,1)S(1)} %collective-permute-done.16.refs_1_, ...), custom_call_target="tpu_custom_call" | custom-call | flops 2147483648 | bytes 2097152 | tf_op jit(solution)/shard_map/attend_head/pallas_call | solution.py:492
  74.9 4.2 %attend_head.3 = bf16[512,2048]{1,0:T(8,128)(2,1)} custom-call(s32[24]{0:T(128)S(1)} %get-tuple-element.31.meta_ref, bf16[512,2048]{1,0:T(8,128)(2,1)S(1)} %get-tuple-element.32.query_ref, bf16[2,128,256]{2,1,0:T(8,128)(2,1)S(1)} %get-tuple-element.43.refs_0_, ...), custom_call_target="tpu_custom_call", output_to_operand_aliasing={{}: (7, {})} | custom-call | flops 2147483648 | bytes 2097152 | tf_op jit(solution)/shard_map/attend_head/pallas_call | solution.py:492
  (63 shorter events, 6.8 us)
Async XLA Ops:
  0.0 18.8 %collective-permute-start.1 = (bf16[4,320,128]{2,1,0:T(8,128)(2,1)}, bf16[4,320,128]{2,1,0:T(8,128)(2,1)S(1)}, u32[]{:S(2)}, u32[]{:S(2)}) collective-permute-start(bf16[4,320,128]{2,1,0:T(8,128)(2,1)} %bitcast.19), channel_id=1, source_target_pairs={{0,1},{1,0},{2,3},{3,2},{4,5},{5,4},{6,7},{7,6},{8,9},{9,8},{10,11... | collective-permute-start | bytes 983048 | tf_op jit(solution)/shard_map/ppermute | solution.py:547
  0.5 18.1 %collective-permute-start = (bf16[4,320,128]{2,1,0:T(8,128)(2,1)}, bf16[4,320,128]{2,1,0:T(8,128)(2,1)S(1)}, u32[]{:S(2)}, u32[]{:S(2)}) collective-permute-start(bf16[4,320,128]{2,1,0:T(8,128)(2,1)} %bitcast.20), channel_id=1, source_target_pairs={{0,2},{1,3},{2,0},{3,1},{4,6},{5,7},{6,4},{7,5},{8,10},{9,11},{10,... | collective-permute-start | bytes 983048 | tf_op jit(solution)/shard_map/ppermute | solution.py:547
  8.7 11.5 %copy-start.7 = (f32[1280]{0:T(1024)S(1)}, f32[1280]{0:T(1024)}, u32[]{:S(2)}) copy-start(f32[1280]{0:T(1024)} %param.18) | copy-start | bytes 15364
  8.7 11.5 %copy-start.8 = (f32[1280]{0:T(1024)S(1)}, f32[1280]{0:T(1024)}, u32[]{:S(2)}) copy-start(f32[1280]{0:T(1024)} %param.19) | copy-start | bytes 15364
  8.7 11.5 %copy-start.9 = (f32[1280]{0:T(1024)S(1)}, f32[1280]{0:T(1024)}, u32[]{:S(2)}) copy-start(f32[1280]{0:T(1024)} %param.21) | copy-start | bytes 15364
  18.5 1.7 %collective-permute-start.2 = (bf16[4,320,128]{2,1,0:T(8,128)(2,1)S(1)}, bf16[4,320,128]{2,1,0:T(8,128)(2,1)S(1)}, u32[]{:S(2)}, u32[]{:S(2)}) collective-permute-start(bf16[4,320,128]{2,1,0:T(8,128)(2,1)S(1)} %collective-permute-done.refs_2_), channel_id=1, source_target_pairs={{0,1},{1,0},{2,3},{3,2},{4,5},{5,4},{6,7},{7,6},{8,9},{9,8},{10,11... | collective-permute-start | bytes 983048 | tf_op jit(solution)/shard_map/ppermute | solution.py:547
  25.9 11.7 %copy-start = (bf16[320,2048]{1,0:T(8,128)(2,1)S(1)}, bf16[320,2048]{1,0:T(8,128)(2,1)}, u32[]{:S(2)}) copy-start(bf16[320,2048]{1,0:T(8,128)(2,1)} %refs_2_.1) | copy-start | bytes 3932164
  25.9 1.7 %collective-permute-start.4 = (bf16[640,256]{1,0:T(8,128)(2,1)S(1)}, bf16[640,256]{1,0:T(8,128)(2,1)S(1)}, u32[]{:S(2)}, u32[]{:S(2)}) collective-permute-start(bf16[640,256]{1,0:T(8,128)(2,1)S(1)} %get-tuple-element.38), channel_id=1, source_target_pairs={{0,1},{1,0},{2,3},{3,2},{4,5},{5,4},{6,7},{7,6},{8,9},{9,8},{10,11... | collective-permute-start | bytes 983048 | tf_op jit(solution)/shard_map/ppermute | solution.py:529
  26.2 1.9 %collective-permute-start.3 = (bf16[640,256]{1,0:T(8,128)(2,1)S(1)}, bf16[640,256]{1,0:T(8,128)(2,1)S(1)}, u32[]{:S(2)}, u32[]{:S(2)}) collective-permute-start(bf16[640,256]{1,0:T(8,128)(2,1)S(1)} %get-tuple-element.36), channel_id=1, source_target_pairs={{0,1},{1,0},{2,3},{3,2},{4,5},{5,4},{6,7},{7,6},{8,9},{9,8},{10,11... | collective-permute-start | bytes 983048 | tf_op jit(solution)/shard_map/ppermute | solution.py:529
  27.7 9.9 %collective-permute-start.5 = (bf16[640,256]{1,0:T(8,128)(2,1)S(1)}, bf16[640,256]{1,0:T(8,128)(2,1)S(1)}, u32[]{:S(2)}, u32[]{:S(2)}) collective-permute-start(bf16[640,256]{1,0:T(8,128)(2,1)S(1)} %add_convert_fusion), channel_id=1, source_target_pairs={{0,2},{1,3},{2,0},{3,1},{4,6},{5,7},{6,4},{7,5},{8,10},{9,11},{10,... | collective-permute-start | bytes 983048 | tf_op jit(solution)/shard_map/ppermute | solution.py:529
  39.5 1.6 %collective-permute-start.14 = (bf16[512,256]{1,0:T(8,128)(2,1)S(1)}, bf16[512,256]{1,0:T(8,128)(2,1)S(1)}, u32[]{:S(2)}, u32[]{:S(2)}) collective-permute-start(bf16[512,256]{1,0:T(8,128)(2,1)S(1)} %get-tuple-element.50), channel_id=1, source_target_pairs={{0,1},{1,0},{2,3},{3,2},{4,5},{5,4},{6,7},{7,6},{8,9},{9,8},{10,11... | collective-permute-start | bytes 786440 | tf_op jit(solution)/shard_map/ppermute | solution.py:529
  39.6 1.9 %collective-permute-start.7 = (bf16[512,256]{1,0:T(8,128)(2,1)S(1)}, bf16[512,256]{1,0:T(8,128)(2,1)S(1)}, u32[]{:S(2)}, u32[]{:S(2)}) collective-permute-start(bf16[512,256]{1,0:T(8,128)(2,1)S(1)} %get-tuple-element.42), channel_id=1, source_target_pairs={{0,1},{1,0},{2,3},{3,2},{4,5},{5,4},{6,7},{7,6},{8,9},{9,8},{10,11... | collective-permute-start | bytes 786440 | tf_op jit(solution)/shard_map/ppermute | solution.py:529
  40.1 14.7 %collective-permute-start.6 = (bf16[512,256]{1,0:T(8,128)(2,1)S(1)}, bf16[512,256]{1,0:T(8,128)(2,1)S(1)}, u32[]{:S(2)}, u32[]{:S(2)}) collective-permute-start(bf16[512,256]{1,0:T(8,128)(2,1)S(1)} %get-tuple-element.40), channel_id=1, source_target_pairs={{0,1},{1,0},{2,3},{3,2},{4,5},{5,4},{6,7},{7,6},{8,9},{9,8},{10,11... | collective-permute-start | bytes 786440 | tf_op jit(solution)/shard_map/ppermute | solution.py:529
  40.2 3.3 %collective-permute-start.13 = (bf16[512,256]{1,0:T(8,128)(2,1)S(1)}, bf16[512,256]{1,0:T(8,128)(2,1)S(1)}, u32[]{:S(2)}, u32[]{:S(2)}) collective-permute-start(bf16[512,256]{1,0:T(8,128)(2,1)S(1)} %get-tuple-element.48), channel_id=1, source_target_pairs={{0,1},{1,0},{2,3},{3,2},{4,5},{5,4},{6,7},{7,6},{8,9},{9,8},{10,11... | collective-permute-start | bytes 786440 | tf_op jit(solution)/shard_map/ppermute | solution.py:529
  41.2 9.2 %collective-permute-start.15 = (bf16[512,256]{1,0:T(8,128)(2,1)S(1)}, bf16[512,256]{1,0:T(8,128)(2,1)S(1)}, u32[]{:S(2)}, u32[]{:S(2)}) collective-permute-start(bf16[512,256]{1,0:T(8,128)(2,1)S(1)} %add_convert_fusion.2), channel_id=1, source_target_pairs={{0,2},{1,3},{2,0},{3,1},{4,6},{5,7},{6,4},{7,5},{8,10},{9,11},{10,... | collective-permute-start | bytes 786440 | tf_op jit(solution)/shard_map/ppermute | solution.py:529
  41.6 13.6 %collective-permute-start.8 = (bf16[512,256]{1,0:T(8,128)(2,1)S(1)}, bf16[512,256]{1,0:T(8,128)(2,1)S(1)}, u32[]{:S(2)}, u32[]{:S(2)}) collective-permute-start(bf16[512,256]{1,0:T(8,128)(2,1)S(1)} %add_convert_fusion.4), channel_id=1, source_target_pairs={{0,2},{1,3},{2,0},{3,1},{4,6},{5,7},{6,4},{7,5},{8,10},{9,11},{10,... | collective-permute-start | bytes 786440 | tf_op jit(solution)/shard_map/ppermute | solution.py:529
  51.1 9.3 %collective-permute-start.18 = (bf16[2,128,256]{2,1,0:T(8,128)(2,1)S(1)}, bf16[2,128,256]{2,1,0:T(8,128)(2,1)S(1)}, u32[]{:S(2)}, u32[]{:S(2)}) collective-permute-start(bf16[2,128,256]{2,1,0:T(8,128)(2,1)S(1)} %get-tuple-element.54), channel_id=1, source_target_pairs={{0,12},{4,8},{8,4},{12,0},{1,13},{5,9},{9,5},{13,1},{2,14},{6,10},... | collective-permute-start | bytes 393224 | tf_op jit(solution)/shard_map/ppermute | solution.py:615
  55.9 8.7 %collective-permute-start.11 = (bf16[2,128,256]{2,1,0:T(8,128)(2,1)S(1)}, bf16[2,128,256]{2,1,0:T(8,128)(2,1)S(1)}, u32[]{:S(2)}, u32[]{:S(2)}) collective-permute-start(bf16[2,128,256]{2,1,0:T(8,128)(2,1)S(1)} %get-tuple-element.46), channel_id=1, source_target_pairs={{0,12},{4,8},{8,4},{12,0},{1,13},{5,9},{9,5},{13,1},{2,14},{6,10},... | collective-permute-start | bytes 393224 | tf_op jit(solution)/shard_map/ppermute | solution.py:615
  59.6 9.5 %collective-permute-start.16 = (bf16[2,128,256]{2,1,0:T(8,128)(2,1)S(1)}, bf16[2,128,256]{2,1,0:T(8,128)(2,1)S(1)}, u32[]{:S(2)}, u32[]{:S(2)}) collective-permute-start(bf16[2,128,256]{2,1,0:T(8,128)(2,1)S(1)} %get-tuple-element.52), channel_id=1, source_target_pairs={{0,4},{4,0},{8,12},{12,8},{1,5},{5,1},{9,13},{13,9},{2,6},{6,2},{1... | collective-permute-start | bytes 393224 | tf_op jit(solution)/shard_map/ppermute | solution.py:615
  59.6 9.2 %collective-permute-start.17 = (bf16[1,128,256]{2,1,0:T(8,128)(2,1)S(1)}, bf16[1,128,256]{2,1,0:T(8,128)(2,1)S(1)}, u32[]{:S(2)}, u32[]{:S(2)}) collective-permute-start(bf16[1,128,256]{2,1,0:T(8,128)(2,1)S(1)} %get-tuple-element.53), channel_id=1, source_target_pairs={{0,8},{4,12},{8,0},{12,4},{1,9},{5,13},{9,1},{13,5},{2,10},{6,14},... | collective-permute-start | bytes 196616 | tf_op jit(solution)/shard_map/ppermute | solution.py:615
  60.4 10.3 %collective-permute-start.19 = (bf16[1,128,256]{2,1,0:T(8,128)(2,1)S(1)}, bf16[1,128,256]{2,1,0:T(8,128)(2,1)S(1)}, u32[]{:S(2)}, u32[]{:S(2)}) collective-permute-start(bf16[1,128,256]{2,1,0:T(8,128)(2,1)S(1)} %slice.9), channel_id=1, source_target_pairs={{0,4},{4,0},{8,12},{12,8},{1,5},{5,1},{9,13},{13,9},{2,6},{6,2},{1... | collective-permute-start | bytes 196616 | tf_op jit(solution)/shard_map/ppermute | solution.py:615
  61.7 13.2 %collective-permute-start.10 = (bf16[1,128,256]{2,1,0:T(8,128)(2,1)S(1)}, bf16[1,128,256]{2,1,0:T(8,128)(2,1)S(1)}, u32[]{:S(2)}, u32[]{:S(2)}) collective-permute-start(bf16[1,128,256]{2,1,0:T(8,128)(2,1)S(1)} %get-tuple-element.45), channel_id=1, source_target_pairs={{0,8},{4,12},{8,0},{12,4},{1,9},{5,13},{9,1},{13,5},{2,10},{6,14},... | collective-permute-start | bytes 196616 | tf_op jit(solution)/shard_map/ppermute | solution.py:615
  64.6 10.3 %collective-permute-start.9 = (bf16[2,128,256]{2,1,0:T(8,128)(2,1)S(1)}, bf16[2,128,256]{2,1,0:T(8,128)(2,1)S(1)}, u32[]{:S(2)}, u32[]{:S(2)}) collective-permute-start(bf16[2,128,256]{2,1,0:T(8,128)(2,1)S(1)} %get-tuple-element.44), channel_id=1, source_target_pairs={{0,4},{4,0},{8,12},{12,8},{1,5},{5,1},{9,13},{13,9},{2,6},{6,2},{1... | collective-permute-start | bytes 393224 | tf_op jit(solution)/shard_map/ppermute | solution.py:615
  68.9 6.0 %collective-permute-start.12 = (bf16[1,128,256]{2,1,0:T(8,128)(2,1)S(1)}, bf16[1,128,256]{2,1,0:T(8,128)(2,1)S(1)}, u32[]{:S(2)}, u32[]{:S(2)}) collective-permute-start(bf16[1,128,256]{2,1,0:T(8,128)(2,1)S(1)} %slice.8), channel_id=1, source_target_pairs={{0,4},{4,0},{8,12},{12,8},{1,5},{5,1},{9,13},{13,9},{2,6},{6,2},{1... | collective-permute-start | bytes 196616 | tf_op jit(solution)/shard_map/ppermute | solution.py:615
  (11 other events, 58.8 us)

commit v3 on v2

--- a/solution.py
+++ b/solution.py
@@ -24,6 +24,7 @@
 HBM = pl.BlockSpec(memory_space=pl.ANY)
 SMEM = pl.BlockSpec(memory_space=pltpu.SMEM)
 MIB = 1024 * 1024
+LIGHT = pl.CostEstimate(flops=1024, bytes_accessed=1024, transcendentals=0)
 
 
 def bits_of(count):
@@ -64,8 +65,15 @@
 def tail_plan(rows, width):
     whole = width // LANES * LANES
     tail = width - whole
-    packed = tail > 0 and rows // ROW_BLOCK * tail == whole
-    return whole, tail, packed
+    packed = tail > 0 and whole > 0 and whole % tail == 0 and rows * tail % whole == 0
+    extra = rows * tail // whole if packed else 0
+    packed = packed and extra % 16 == 0 and ROW_BLOCK % extra == 0
+    return whole, tail, extra if packed else 0
+
+
+def sent_shape(rows, width):
+    whole, _, extra = tail_plan(rows, width)
+    return (rows + extra, whole) if extra else (rows, width)
 
 
 def layout_kernel(group_count, tiles_local, where_ref, tiles_ref, owner_ref, text_ref, meta_ref):
@@ -151,13 +159,13 @@
     }
 
 
-def mlp_kernel(piece_count, place, meta_ref, *refs):
+def mlp_kernel(piece_count, bases, tiles, place, meta_ref, *refs):
     pieces = refs[:piece_count]
     gain_ref, bias_ref, up_bias_ref, up_ref, down_ref = refs[piece_count : piece_count + 5]
     outs = refs[piece_count + 5 : 2 * piece_count + 5]
     cat_ref, normed_ref, hidden_ref, total_ref = refs[2 * piece_count + 5 :]
     index = meta_ref[place]
-    tiles, width, tile_rows = pieces[0].shape
+    _, width, tile_rows = pieces[0].shape
     rows = tiles * tile_rows
     channels, hidden_width = up_ref.shape
     up_step = column_step(hidden_width)
@@ -168,7 +176,7 @@
     for tile in range(tiles):
         for k, piece in enumerate(pieces):
             start = pl.multiple_of((index ^ k) * width, math.gcd(width, LANES))
-            cat_ref[pl.ds(start, width), :] = piece[tile]
+            cat_ref[pl.ds(start, width), :] = piece[bases[k] + tile]
         values = cat_ref[...].T.astype(F32)
         average = jnp.sum(values, axis=1, keepdims=True) * (1.0 / channels)
         centered = values - average
@@ -187,29 +195,28 @@
         total_ref[:, take] = jnp.dot(
             hidden_ref[...], down_ref[:, take], preferred_element_type=F32
         )
-    whole, tail, packed = tail_plan(rows, width)
-    for row in range(0, rows, ROW_BLOCK):
-        take = pl.ds(row, ROW_BLOCK)
+    whole, tail, extra = tail_plan(rows, width)
+    step = extra or ROW_BLOCK
+    for part in range(rows // step):
+        take = pl.ds(part * step, step)
         blocks = [total_ref[take, j * width : (j + 1) * width] for j in range(piece_count)]
         for out, block in zip(outs, xor_order(blocks, index)):
             block = block.astype(BF16)
-            if packed:
-                part = row // ROW_BLOCK
+            if extra:
                 out[take, :] = block[:, :whole]
-                out[rows : rows + ROW_BLOCK, part * tail : (part + 1) * tail] = block[:, whole:]
+                out[rows : rows + extra, part * tail : (part + 1) * tail] = block[:, whole:]
             else:
                 out[take, :] = block
 
 
-def encoder_mlp(meta, place, pieces, ln_gain, ln_bias, w_up, b_up, w_down):
-    tiles, width, tile_rows = pieces[0].shape
+def encoder_mlp(meta, place, pieces, bases, tiles, ln_gain, ln_bias, w_up, b_up, w_down):
+    _, width, tile_rows = pieces[0].shape
     rows = tiles * tile_rows
     count = len(pieces)
     channels, hidden_width = w_up.shape
-    whole, _, packed = tail_plan(rows, width)
-    shape = (rows + ROW_BLOCK, whole) if packed else (rows, width)
+    shape = sent_shape(rows, width)
     return pl.pallas_call(
-        functools.partial(mlp_kernel, count, place),
+        functools.partial(mlp_kernel, count, bases, tiles, place),
         out_shape=[jax.ShapeDtypeStruct(shape, BF16)] * count,
         in_specs=[SMEM] + [VMEM] * (count + 5),
         out_specs=[VMEM] * count,
@@ -220,11 +227,7 @@
             pltpu.VMEM((rows, channels), F32),
         ],
         compiler_params=pltpu.CompilerParams(vmem_limit_bytes=44 * MIB),
-        cost_estimate=pl.CostEstimate(
-            flops=4 * rows * channels * hidden_width,
-            bytes_accessed=4 * channels * hidden_width + 4 * rows * channels,
-            transcendentals=rows * hidden_width,
-        ),
+        cost_estimate=LIGHT,
         name="encoder_mlp",
     )(
         meta,
@@ -245,26 +248,16 @@
     owner_ref,
     text_ref,
     gain_ref,
-    tap_ref,
-    weight_ref,
     query_ref,
-    out_ref,
     normed_ref,
     meta_ref,
-    row_ref,
 ):
     @pl.when(pl.program_id(0) == 0)
     def _():
         layout_kernel(
             group_count, tiles_local, where_ref, tiles_ref, owner_ref, text_ref, meta_ref
         )
-        tiles, _, tile_rows = tap_ref.shape
-        for tile in range(tiles):
-            row_ref[tile * tile_rows : (tile + 1) * tile_rows, :] = tap_ref[tile].T
-
-    out_ref[...] = jnp.dot(
-        row_ref[...], weight_ref[...], preferred_element_type=F32
-    ).astype(BF16)[None, None]
+
     gain = gain_ref[...] * (math.log2(math.e) / math.sqrt(HD))
     for col in range(0, query_ref.shape[1], HD):
         values = query_ref[:, col : col + HD].astype(F32)
@@ -272,88 +265,104 @@
         normed_ref[:, col : col + HD] = (values * lax.rsqrt(square + epsilon) * gain).astype(BF16)
 
 
-def prepare(
-    where, requests, q_gain, tap_tiles, weights, queries, group_count, head_count, dest_count, dup
-):
+def prepare(where, requests, q_gain, queries, group_count, tiles_local):
+    text_rows, width = queries.shape
+    step = ROW_BLOCK
+    return pl.pallas_call(
+        functools.partial(prepare_kernel, group_count, tiles_local),
+        out_shape=[
+            jax.ShapeDtypeStruct((text_rows, width), BF16),
+            jax.ShapeDtypeStruct((meta_places(group_count)["size"],), jnp.int32),
+        ],
+        grid=(text_rows // step,),
+        in_specs=[
+            SMEM,
+            SMEM,
+            SMEM,
+            SMEM,
+            pl.BlockSpec((1, HD), lambda n: (0, 0)),
+            pl.BlockSpec((step, width), lambda n: (n, 0)),
+        ],
+        out_specs=[pl.BlockSpec((step, width), lambda n: (n, 0)), SMEM],
+        compiler_params=pltpu.CompilerParams(vmem_limit_bytes=16 * MIB),
+        cost_estimate=LIGHT,
+        name="prepare",
+    )(where, *requests, lane_rows(q_gain), queries)
+
+
+def tap_kernel(meta_ref, tap_ref, weight_ref, out_ref, row_ref):
+    @pl.when(pl.program_id(0) == 0)
+    def _():
+        tiles, _, tile_rows = tap_ref.shape
+        for tile in range(tiles):
+            row_ref[tile * tile_rows : (tile + 1) * tile_rows, :] = tap_ref[tile].T
+
+    out_ref[...] = jnp.dot(
+        row_ref[...], weight_ref[...], preferred_element_type=F32
+    ).astype(BF16)[None, None]
+
+
+def tap_projection(meta, place, tap_tiles, weights, head_count, dest_count, dup):
     tiles, depth, tile_rows = tap_tiles.shape
     rows = tiles * tile_rows
     block = 2 * HD
-    steps = head_count * dest_count
-    text_rows, width = queries.shape
-    query_step = text_rows // steps
-    meta_size = meta_places(group_count)["size"]
-
-    def head_of(n, where_ref):
-        dest = lax.div(where_ref[1], jnp.int32(dup)) ^ lax.rem(n, dest_count)
+
+    def head_of(n, meta_ref):
+        dest = lax.div(meta_ref[place], jnp.int32(dup)) ^ lax.rem(n, dest_count)
         return dest * head_count + lax.div(n, dest_count)
 
     return pl.pallas_call(
-        functools.partial(prepare_kernel, group_count, tiles),
-        out_shape=[
-            jax.ShapeDtypeStruct((head_count, dest_count, rows, block), BF16),
-            jax.ShapeDtypeStruct((text_rows, width), BF16),
-            jax.ShapeDtypeStruct((meta_size,), jnp.int32),
-        ],
+        tap_kernel,
+        out_shape=jax.ShapeDtypeStruct((head_count, dest_count, rows, block), BF16),
         grid_spec=pltpu.PrefetchScalarGridSpec(
             num_scalar_prefetch=1,
-            grid=(steps,),
+            grid=(head_count * dest_count,),
             in_specs=[
-                SMEM,
-                SMEM,
-                SMEM,
-                pl.BlockSpec((1, HD), lambda n, w: (0, 0)),
                 pl.BlockSpec(tap_tiles.shape, lambda n, w: (0, 0, 0)),
                 pl.BlockSpec((depth, block), lambda n, w: (0, head_of(n, w))),
-                pl.BlockSpec((query_step, width), lambda n, w: (n, 0)),
             ],
-            out_specs=[
-                pl.BlockSpec(
-                    (1, 1, rows, block),
-                    lambda n, w: (lax.div(n, dest_count), lax.rem(n, dest_count), 0, 0),
-                ),
-                pl.BlockSpec((query_step, width), lambda n, w: (n, 0)),
-                SMEM,
-            ],
+            out_specs=pl.BlockSpec(
+                (1, 1, rows, block),
+                lambda n, w: (lax.div(n, dest_count), lax.rem(n, dest_count), 0, 0),
+            ),
             scratch_shapes=[pltpu.VMEM((rows, depth), BF16)],
         ),
-        compiler_params=pltpu.CompilerParams(vmem_limit_bytes=44 * MIB),
-        cost_estimate=pl.CostEstimate(
-            flops=2 * rows * depth * weights.shape[1],
-            bytes_accessed=2 * depth * weights.shape[1],
-            transcendentals=0,
-        ),
-        name="prepare",
-    )(where, *requests, lane_rows(q_gain), tap_tiles, weights, queries)
-
-
-def kv_kernel(head_count, dest_count, dup, place, term_count, meta_ref, *refs):
+        compiler_params=pltpu.CompilerParams(vmem_limit_bytes=16 * MIB),
+        cost_estimate=LIGHT,
+        name="tap_projection",
+    )(meta, tap_tiles, weights)
+
+
+def kv_kernel(head_count, dest_count, dup, place, term_counts, meta_ref, *refs):
     x_ref, bias_ref, weight_ref, tap_ref = refs[:4]
-    terms = refs[4 : 4 + term_count]
-    outs = refs[4 + term_count : -1]
+    terms = refs[4 : 4 + sum(term_counts)]
+    outs = refs[4 + sum(term_counts) : -1]
     encoded_ref = refs[-1]
     tiles, width, tile_rows = x_ref.shape
-    rows = tiles * tile_rows
-    whole, tail, packed = tail_plan(rows, width)
+    half_tiles = tiles // len(term_counts)
+    whole, tail, extra = tail_plan(half_tiles * tile_rows, width)
     bias = one_row(bias_ref, width)
-    for row in range(0, rows, ROW_BLOCK):
-        take = pl.ds(row, ROW_BLOCK)
+    for tile in range(tiles):
+        half, row = tile // half_tiles, tile % half_tiles * tile_rows
+        mine = terms[sum(term_counts[:half]) : sum(term_counts[: half + 1])]
 
         def summed(part, lanes):
-            out = terms[0][part, lanes].astype(F32)
-            for term in terms[1:]:
+            out = mine[0][part, lanes].astype(F32)
+            for term in mine[1:]:
                 out = out + term[part, lanes].astype(F32)
             return out
 
-        if packed:
-            start = row // ROW_BLOCK * tail
-            main = summed(take, slice(None))
-            rest = summed(pl.ds(rows, ROW_BLOCK), slice(start, start + tail))
-            total = jnp.concatenate([main, rest], axis=1)
-        else:
-            total = summed(take, slice(None))
-        total = total + x_ref[row // ROW_BLOCK].T.astype(F32)
-        total = total + bias
-        encoded_ref[take, :] = total.astype(BF16)
+        total = summed(pl.ds(row, tile_rows), slice(None))
+        if extra:
+            chunks = range(row // extra, (row + tile_rows) // extra)
+            rest = [
+                summed(pl.ds(half_tiles * tile_rows, extra), slice(c * tail, (c + 1) * tail))
+                for c in chunks
+            ]
+            rest = rest[0] if len(rest) == 1 else jnp.concatenate(rest, axis=0)
+            total = jnp.concatenate([total, rest], axis=1)
+        total = total + x_ref[tile].T.astype(F32) + bias
+        encoded_ref[tile * tile_rows : (tile + 1) * tile_rows, :] = total.astype(BF16)
     block = 2 * HD
     mine = lax.div(meta_ref[place], jnp.int32(dup))
     for head in range(head_count):
@@ -365,23 +374,22 @@
             outs[head * dest_count + k][...] = value.astype(BF16)
 
 
-def kv_projection(meta, place, x_tiles, b_down, weights, tap_part, terms, dup):
+def kv_projection(meta, place, x_tiles, b_down, weights, tap_part, halves, dup):
+    terms = [term for half in halves for term in half]
     tiles, width, tile_rows = x_tiles.shape
     rows = tiles * tile_rows
     head_count, dest_count = tap_part.shape[:2]
     block = 2 * HD
     outs = pl.pallas_call(
-        functools.partial(kv_kernel, head_count, dest_count, dup, place, len(terms)),
+        functools.partial(
+            kv_kernel, head_count, dest_count, dup, place, tuple(len(half) for half in halves)
+        ),
         out_shape=[jax.ShapeDtypeStruct((rows, block), BF16)] * (head_count * dest_count),
         in_specs=[SMEM] + [VMEM] * (4 + len(terms)),
         out_specs=[VMEM] * (head_count * dest_count),
         scratch_shapes=[pltpu.VMEM((rows, width), BF16)],
         compiler_params=pltpu.CompilerParams(vmem_limit_bytes=24 * MIB),
-        cost_estimate=pl.CostEstimate(
-            flops=2 * rows * width * weights.shape[1],
-            bytes_accessed=2 * width * weights.shape[1] + 4 * rows * weights.shape[1],
-            transcendentals=0,
-        ),
+        cost_estimate=LIGHT,
         name="kv_projection",
     )(meta, x_tiles, lane_rows(b_down), weights, tap_part, *terms)
     return [outs[h * dest_count : (h + 1) * dest_count] for h in range(head_count)]
@@ -417,9 +425,7 @@
         out_specs=[VMEM] * len(picks),
         scratch_shapes=[pltpu.VMEM((rows, block), BF16)],
         compiler_params=pltpu.CompilerParams(vmem_limit_bytes=8 * MIB),
-        cost_estimate=pl.CostEstimate(
-            flops=10 * rows * block, bytes_accessed=10 * rows * block, transcendentals=rows
-        ),
+        cost_estimate=LIGHT,
         name="finish_tiles",
     )(meta, lane_rows(k_gain), *terms)
 
@@ -506,11 +512,7 @@
         ],
         input_output_aliases={2 + len(tiles): 0} if extra else {},
         compiler_params=pltpu.CompilerParams(vmem_limit_bytes=24 * MIB),
-        cost_estimate=pl.CostEstimate(
-            flops=4 * rows * head_width * group_rows,
-            bytes_accessed=4 * rows * head_width,
-            transcendentals=rows * head_width // HD * group_rows // 2,
-        ),
+        cost_estimate=LIGHT,
         name="attend_head",
     )(meta, queries, *tiles, *extra)
 
@@ -524,28 +526,32 @@
     bits = bits_of(len(blocks))
     for b in range(bits):
         pairs = xor_pairs(count, 1 << (b + first_bit))
-        got = {}
+        got, sent = {}, None
         for k in sorted((k for k in blocks if (k >> b) & 1), reverse=True):
-            got[k ^ (1 << b)] = lax.ppermute(blocks[k], "tp", pairs)
+            sent = blocks[k]
+            got[k ^ (1 << b)] = lax.ppermute(sent, "tp", pairs)
         if b == bits - 1:
-            return [blocks[0], got[0]]
-        blocks = {
-            k: add_rounded(blocks[k], got[k]) for k in got
-        }
-    return [blocks[0]]
-
-
-def gather_pieces(own, count, ready):
+            return [blocks[0], got[0]], sent
+        blocks = {k: add_rounded(blocks[k], got[k]) for k in got}
+    return [blocks[0]], blocks[0]
+
+
+def gather_half(whole, tiles, half, count, ready):
     bits = bits_of(count)
-    pieces = {0: own}
-    for b in reversed(range(bits)):
+    first = half * tiles
+    pieces = {0: whole[0][first : first + tiles]}
+    for b in reversed(range(1, bits)):
         pairs = xor_pairs(count, 1 << b)
         for k in sorted(pieces):
-            block = pieces[k]
-            if b == 0 and k:
-                block, ready = lax.optimization_barrier((block, ready))
-            pieces[k | (1 << b)] = lax.ppermute(block, "tp", pairs)
-    return [pieces[k] for k in range(count)], ready
+            pieces[k | (1 << b)] = lax.ppermute(pieces[k], "tp", pairs)
+    pairs = xor_pairs(count, 1)
+    for k in sorted(pieces):
+        if k:
+            block, ready = lax.optimization_barrier((pieces[k], ready))
+            pieces[k | 1] = lax.ppermute(block, "tp", pairs)
+    pieces[0], pieces[1] = whole
+    bases = tuple(first if k < 2 else 0 for k in range(count))
+    return [pieces[k] for k in range(count)], bases, ready
 
 
 def local(
@@ -577,23 +583,33 @@
     dest_count = tp_count // dup
     place = meta_places(group_count)
 
-    tap_part, query_rows, meta = prepare(
+    query_rows, meta = prepare(
         where,
         (tiles_per_request, owner, text_per_request),
         q_gain,
-        tap_tiles,
-        kv_w_taps,
         queries,
         group_count,
-        head_count,
-        dest_count,
-        dup,
+        tiles_local,
     )
-    pieces, meta = gather_pieces(x_tiles, tp_count, meta)
-    mlp_blocks = encoder_mlp(
-        meta, place["tp"], pieces, ln_gain, ln_bias, w_up, b_up, w_down
+    halves = 2 if tiles_local % 2 == 0 else 1
+    tiles = tiles_local // halves
+    whole = [x_tiles, lax.ppermute(x_tiles, "tp", xor_pairs(tp_count, 1))]
+    mlp_terms = []
+    ready = meta
+    for half in range(halves):
+        pieces, bases, ready = gather_half(whole, tiles, half, tp_count, ready)
+        if half == 0:
+            meta = ready
+        mlp_blocks = encoder_mlp(
+            meta, place["tp"], pieces, bases, tiles, ln_gain, ln_bias, w_up, b_up, w_down
+        )
+        terms, sent = scatter_sum(mlp_blocks, tp_count, 0)
+        mlp_terms.append(terms)
+        ready, _ = lax.optimization_barrier((meta, mlp_blocks[0]))
+        meta, _ = lax.optimization_barrier((meta, sent))
+    tap_part = tap_projection(
+        meta, place["tp"], tap_tiles, kv_w_taps, head_count, dest_count, dup
     )
-    mlp_terms = scatter_sum(mlp_blocks, tp_count, 0)
     kv_blocks = kv_projection(
         meta, place["tp"], x_tiles, b_down, kv_w_out, tap_part, mlp_terms, dup
     )
@@ -603,25 +619,33 @@
     most_other = total_tiles - REQ_G * MAXT - REQ_G * (group_count - 2)
     one_large = group_count == 4 and slots == 2 and most_other <= group_count
     out = None
+    before = {}
     for head in range(head_count):
         blocks = kv_blocks[head]
         for b in range(bits_of(dup)):
             pairs = xor_pairs(tp_count, 1 << b)
             blocks = [add_rounded(v, lax.ppermute(v, "tp", pairs)) for v in blocks]
-        terms = scatter_sum(blocks, tp_count, bits_of(dup))
+        terms, _ = scatter_sum(blocks, tp_count, bits_of(dup))
         send = place["send"]
 
-        def move(value, mask):
-            return lax.ppermute(value, "grp", xor_pairs(group_count, mask))
+        def move(value, mask, name):
+            if name in before:
+                value, _ = lax.optimization_barrier((value, before[name]))
+            got = lax.ppermute(value, "grp", xor_pairs(group_count, mask))
+            if name is not None:
+                before[name] = got
+            return got
 
         if one_large:
             star = place["star"]
             picks = ((send, star), (send + 1, star), (send + 2,), (send + 3, star))
             own, near, middle, far = finish_tiles(meta, k_gain, terms, picks)
-            far_got = move(far, 3)
-            middle_got = move(middle, 2)
-            near_got = move(near, 1)
-            passed = move(far_got[1:], 1)
+            far_got = move(far, 3, None)
+            middle_got = move(middle, 2, "middle")
+            near_got = move(near, 1, "near")
+            after = middle_got if out is None else out
+            far_got, _ = lax.optimization_barrier((far_got, after))
+            passed = move(far_got[1:], 1, None)
             tiles = (own, near_got, middle_got, far_got, passed)
             sources = ((0, 4), (1, 5), (2,), (3, 7), (6,))
         else:
@@ -629,7 +653,7 @@
                 tuple(send + s * group_count + d for s in range(slots)) for d in range(group_count)
             )
             made = finish_tiles(meta, k_gain, terms, picks)
-            tiles = tuple(made[:1]) + tuple(move(made[d], d) for d in range(1, group_count))
+            tiles = tuple(made[:1]) + tuple(move(made[d], d, d) for d in range(1, group_count))
             sources = tuple(
                 tuple(s * group_count + d for s in range(slots)) for d in range(group_count)
             )

time: 79.7 us -> 84.3 us (1.058); the launches traced: 79.1 us -> 82.8 us
  waiting for transfers between devices: 23.5 us -> 15.7 us
  starting transfers between devices: 22 us -> 28.6 us
  local copies, waits for them, and re-layouts: 5.7 us -> 9.18 us
  Pallas kernels: 27.2 us -> 28.6 us
    ppermute x20 -> x25, waiting for transfers between devices: 23.5 us -> 15.7 us  [the longest x12 8.71 us: scatter_sum(): got[k ^ 1 << b] = lax.ppermute(sent, 'tp', pairs)]
    ppermute x20 -> x25, starting transfers between devices: 22 us -> 28.6 us  [the longest x8 18 us: move(): got = lax.ppermute(value, 'grp', xor_pairs(group_count, mask))]
    unnamed x30 -> x36, local copies, waits for them, and re-layouts: 5.68 us -> 8.11 us
    pallas_call x2 -> x4, Pallas kernels: 15.4 us -> 16.8 us  [the longest x1 7.33 us: tap_projection(): pl.pallas_call(tap_kernel, out_shape=jax.ShapeDtypeStruct((head_count, de...]
    slice x2 -> x3, local copies, waits for them, and re-layouts: 0.01 us -> 1.07 us  [the longest x1 1.06 us: gather_half(): pieces = {0: whole[0][first:first + tiles]}]
  transfers between devices with their start and end apart: 20 -> 25, of which waited for: 9 -> 7; matrix products, arithmetic and copies ran while one was open for 1% -> 1% of each run, Pallas kernels for 19% -> 27%
where the time goes in v3:
time: 84.3 us; the launch traced here: 82.8 us
  starting transfers between devices  28.6 us (34%)
  Pallas kernels  28.6 us (34%)
  waiting for transfers between devices  15.7 us (19%)
  local copies, waits for them, and re-layouts  9.18 us (11%)
    ppermute x8, starting transfers between devices, move(): got = lax.ppermute(value, 'grp', xor_pairs(group_count, mask))  18 us
    ppermute x12, waiting for transfers between devices, scatter_sum(): got[k ^ 1 << b] = lax.ppermute(sent, 'tp', pairs)  8.71 us
    pallas_call x2, Pallas kernels, attend_head(): pl.pallas_call(functools.partial(attend_kernel, group_count, sources, len...  8.4 us
    unnamed x36, local copies, waits for them, and re-layouts  8.11 us
    pallas_call x1, Pallas kernels, tap_projection(): pl.pallas_call(tap_kernel, out_shape=jax.ShapeDtypeStruct((head_count, de...  7.33 us
    pallas_call x2, Pallas kernels, encoder_mlp(): pl.pallas_call(functools.partial(mlp_kernel, count, bases, tiles, place),...  6.85 us
    ppermute x12, starting transfers between devices, scatter_sum(): got[k ^ 1 << b] = lax.ppermute(sent, 'tp', pairs)  6.73 us
    ppermute x8, waiting for transfers between devices, move(): got = lax.ppermute(value, 'grp', xor_pairs(group_count, mask))  6.01 us
  transfers between devices with their start and end apart: 25, of which 7 were waited for; matrix products, arithmetic and copies ran while one was open for 1% of the time, Pallas kernels for 27%

profile of v3, /device:TPU:0, one launch (start us, length us, event | category | flops | bytes accessed | tf_op | source)
XLA Modules:
  0.0 82.8 jit_solution(480195029541896126)
XLA Ops:
  0.0 1.1 %slice_bitcast_fusion = (bf16[2,320,128]{2,1,0:T(8,128)(2,1)S(1)}, bf16[2,320,128]{2,1,0:T(8,128)(2,1)S(1)}) fusion(bf16[4,1,320,128]{3,2,0,1:T(8,128)(2,1)} %bitcast.23), kind=kLoop, calls=%fused_computation.8 | loop fusion | bytes 655360 | tf_op jit(solution)/shard_map/slice | solution.py:542
  1.1 3.0 %collective-permute-start = (bf16[2,320,128]{2,1,0:T(8,128)(2,1)S(1)}, bf16[2,320,128]{2,1,0:T(8,128)(2,1)S(1)}, u32[]{:S(2)}, u32[]{:S(2)}) collective-permute-start(bf16[2,320,128]{2,1,0:T(8,128)(2,1)S(1)} %get-tuple-element.74), channel_id=1, source_target_pairs={{0,2},{1,3},{2,0},{3,1},{4,6},{5,7},{6,4},{7,5},{8,10},{9,11},{10,... | collective-permute-start | bytes 491528 | tf_op jit(solution)/shard_map/ppermute | solution.py:546
  4.2 1.6 %copy-done.6 = bf16[512,2048]{1,0:T(8,128)(2,1)S(1)} copy-done((bf16[512,2048]{1,0:T(8,128)(2,1)S(1)}, bf16[512,2048]{1,0:T(8,128)(2,1)}, u32[]{:S(2)}) %copy-start.6) | copy-done | bytes 2097176
  8.4 2.6 %prepare.1 = (bf16[512,2048]{1,0:T(8,128)(2,1)S(1)}, s32[24]{0:T(128)S(1)}) custom-call(s32[2]{0:T(128)S(1)} %pad_add_fusion.where_ref, s32[8]{0:T(128)S(1)} %copy-done.13, s32[8]{0:T(128)S(1)} %copy-done.14, s32[8]{0:T(128)S(1)} %copy-done.15, f32[1,128]{1,0:T(1,128)S(1)} %bitcast.37, bf16[512,2048]{1,0:T(8,128)(2,1)S(1)} %copy-done.6), custom_call_target="tpu_custom_call" | custom-call | flops 1024 | bytes 1024 | tf_op jit(solution)/shard_map/prepare/pallas_call | solution.py:271
  12.7 1.9 %copy-done = bf16[1280,1280]{1,0:T(8,128)(2,1)S(1)} copy-done((bf16[1280,1280]{1,0:T(8,128)(2,1)S(1)}, bf16[1280,1280]{1,0:T(8,128)(2,1)}, u32[]{:S(2)}) %copy-start) | copy-done | bytes 3276824
  14.6 1.9 %copy-done.2 = bf16[1280,1280]{1,0:T(8,128)(2,1)S(1)} copy-done((bf16[1280,1280]{1,0:T(8,128)(2,1)S(1)}, bf16[1280,1280]{1,0:T(8,128)(2,1)}, u32[]{:S(2)}) %copy-start.2) | copy-done | bytes 3276824
  16.5 3.4 %encoder_mlp.2 = (bf16[320,256]{1,0:T(8,128)(2,1)S(1)}, bf16[320,256]{1,0:T(8,128)(2,1)S(1)}, bf16[320,256]{1,0:T(8,128)(2,1)S(1)}, bf16[320,256]{1,0:T(8,128)(2,1)S(1)}) custom-call(s32[24]{0:T(128)S(1)} %get-tuple-element.47.meta_ref, bf16[4,320,128]{2,1,0:T(8,128)(2,1)S(1)} %bitcast.25, bf16[4,320,128]{2,1,0:T(8,128)(2,1)S(1)} %collective-permute-done.1.refs_1_, ...), custom_call_target="tpu_custom_call" | custom-call | flops 1024 | bytes 1024 | tf_op jit(solution)/shard_map/encoder_mlp/pallas_call | solution.py:218
  21.4 1.1 %collective-permute-start.8 = (bf16[320,256]{1,0:T(8,128)(2,1)S(1)}, bf16[320,256]{1,0:T(8,128)(2,1)S(1)}, u32[]{:S(2)}, u32[]{:S(2)}) collective-permute-start(bf16[320,256]{1,0:T(8,128)(2,1)S(1)} %add_convert_fusion.7), channel_id=1, source_target_pairs={{0,2},{1,3},{2,0},{3,1},{4,6},{5,7},{6,4},{7,5},{8,10},{9,11},{10,... | collective-permute-start | bytes 491528 | tf_op jit(solution)/shard_map/ppermute | solution.py:532
  22.6 3.4 %encoder_mlp.3 = (bf16[320,256]{1,0:T(8,128)(2,1)S(1)}, bf16[320,256]{1,0:T(8,128)(2,1)S(1)}, bf16[320,256]{1,0:T(8,128)(2,1)S(1)}, bf16[320,256]{1,0:T(8,128)(2,1)S(1)}) custom-call(s32[24]{0:T(128)S(1)} %get-tuple-element.47.meta_ref, bf16[4,320,128]{2,1,0:T(8,128)(2,1)S(1)} %bitcast.26, bf16[4,320,128]{2,1,0:T(8,128)(2,1)S(1)} %collective-permute-done.1.refs_1_, ...), custom_call_target="tpu_custom_call" | custom-call | flops 1024 | bytes 1024 | tf_op jit(solution)/shard_map/encoder_mlp/pallas_call | solution.py:218
  28.6 7.3 %tap_projection.1.refs_3_ = bf16[2,4,512,256]{3,2,1,0:T(8,128)(2,1)S(1)} custom-call(s32[24]{0:T(128)S(1)} %get-tuple-element.47.meta_ref, bf16[4,1600,128]{2,1,0:T(8,128)(2,1)S(1)} %bitcast.28, bf16[1600,2048]{1,0:T(8,128)(2,1)S(1)} %copy-done.4), custom_call_target="tpu_custom_call" | custom-call | flops 1024 | bytes 1024 | tf_op jit(solution)/shard_map/tap_projection/pallas_call | solution.py:314
  36.0 1.9 %kv_projection.1 = (bf16[512,256]{1,0:T(8,128)(2,1)S(1)}, bf16[512,256]{1,0:T(8,128)(2,1)S(1)}, bf16[512,256]{1,0:T(8,128)(2,1)S(1)}, bf16[512,256]{1,0:T(8,128)...) custom-call(s32[24]{0:T(128)S(1)} %get-tuple-element.47.meta_ref, ...), custom_call_target="tpu_custom_call" | custom-call | flops 1024 | bytes 1024 | tf_op jit(solution)/shard_map/kv_projection/pallas_call | solution.py:383
  39.6 1.1 %collective-permute-start.16 = (bf16[512,256]{1,0:T(8,128)(2,1)S(1)}, bf16[512,256]{1,0:T(8,128)(2,1)S(1)}, u32[]{:S(2)}, u32[]{:S(2)}) collective-permute-start(bf16[512,256]{1,0:T(8,128)(2,1)S(1)} %add_convert_fusion), channel_id=1, source_target_pairs={{0,2},{1,3},{2,0},{3,1},{4,6},{5,7},{6,4},{7,5},{8,10},{9,11},{10,... | collective-permute-start | bytes 786440 | tf_op jit(solution)/shard_map/ppermute | solution.py:532
  40.7 1.1 %collective-permute-start.13 = (bf16[512,256]{1,0:T(8,128)(2,1)S(1)}, bf16[512,256]{1,0:T(8,128)(2,1)S(1)}, u32[]{:S(2)}, u32[]{:S(2)}) collective-permute-start(bf16[512,256]{1,0:T(8,128)(2,1)S(1)} %add_convert_fusion.2), channel_id=1, source_target_pairs={{0,2},{1,3},{2,0},{3,1},{4,6},{5,7},{6,4},{7,5},{8,10},{9,11},{10,... | collective-permute-start | bytes 786440 | tf_op jit(solution)/shard_map/ppermute | solution.py:532
  41.9 6.9 %collective-permute-done.16.refs_1_ = bf16[512,256]{1,0:T(8,128)(2,1)S(1)} collective-permute-done((bf16[512,256]{1,0:T(8,128)(2,1)S(1)}, bf16[512,256]{1,0:T(8,128)(2,1)S(1)}, u32[]{:S(2)}, u32[]{:S(2)}) %collective-permute-start.16) | collective-permute-done | bytes 262176 | tf_op jit(solution)/shard_map/ppermute | solution.py:532
  49.5 2.7 %collective-permute-start.19 = (bf16[1,128,256]{2,1,0:T(8,128)(2,1)S(1)}, bf16[1,128,256]{2,1,0:T(8,128)(2,1)S(1)}, u32[]{:S(2)}, u32[]{:S(2)}) collective-permute-start(bf16[1,128,256]{2,1,0:T(8,128)(2,1)S(1)} %get-tuple-element.66), channel_id=1, source_target_pairs={{0,8},{4,12},{8,0},{12,4},{1,9},{5,13},{9,1},{13,5},{2,10},{6,14},... | collective-permute-start | bytes 196616 | tf_op jit(solution)/shard_map/ppermute | solution.py:634
  52.2 1.6 %collective-permute-start.17 = (bf16[2,128,256]{2,1,0:T(8,128)(2,1)S(1)}, bf16[2,128,256]{2,1,0:T(8,128)(2,1)S(1)}, u32[]{:S(2)}, u32[]{:S(2)}) collective-permute-start(bf16[2,128,256]{2,1,0:T(8,128)(2,1)S(1)} %get-tuple-element.63), channel_id=1, source_target_pairs={{0,4},{4,0},{8,12},{12,8},{1,5},{5,1},{9,13},{13,9},{2,6},{6,2},{1... | collective-permute-start | bytes 393224 | tf_op jit(solution)/shard_map/ppermute | solution.py:634
  54.8 3.7 %collective-permute-start.21 = (bf16[2,128,256]{2,1,0:T(8,128)(2,1)S(1)}, bf16[2,128,256]{2,1,0:T(8,128)(2,1)S(1)}, u32[]{:S(2)}, u32[]{:S(2)}) collective-permute-start(bf16[2,128,256]{2,1,0:T(8,128)(2,1)S(1)} %get-tuple-element.68), channel_id=1, source_target_pairs={{0,12},{4,8},{8,4},{12,0},{1,13},{5,9},{9,5},{13,1},{2,14},{6,10},... | collective-permute-start | bytes 393224 | tf_op jit(solution)/shard_map/ppermute | solution.py:634
  58.5 3.0 %collective-permute-done.22.refs_3_ = bf16[2,128,256]{2,1,0:T(8,128)(2,1)S(1)} collective-permute-done((bf16[2,128,256]{2,1,0:T(8,128)(2,1)S(1)}, bf16[2,128,256]{2,1,0:T(8,128)(2,1)S(1)}, u32[]{:S(2)}, u32[]{:S(2)}) %collective-permute-start.22) | collective-permute-done | bytes 131104 | tf_op jit(solution)/shard_map/ppermute | solution.py:634
  61.5 4.9 %collective-permute-start.23 = (bf16[1,128,256]{2,1,0:T(8,128)(2,1)S(1)}, bf16[1,128,256]{2,1,0:T(8,128)(2,1)S(1)}, u32[]{:S(2)}, u32[]{:S(2)}) collective-permute-start(bf16[1,128,256]{2,1,0:T(8,128)(2,1)S(1)} %slice.22), channel_id=1, source_target_pairs={{0,4},{4,0},{8,12},{12,8},{1,5},{5,1},{9,13},{13,9},{2,6},{6,2},{1... | collective-permute-start | bytes 196616 | tf_op jit(solution)/shard_map/ppermute | solution.py:634
  66.5 3.5 %collective-permute-start.20 = (bf16[1,128,256]{2,1,0:T(8,128)(2,1)S(1)}, bf16[1,128,256]{2,1,0:T(8,128)(2,1)S(1)}, u32[]{:S(2)}, u32[]{:S(2)}) collective-permute-start(bf16[1,128,256]{2,1,0:T(8,128)(2,1)S(1)} %get-tuple-element.67), channel_id=1, source_target_pairs={{0,8},{4,12},{8,0},{12,4},{1,9},{5,13},{9,1},{13,5},{2,10},{6,14},... | collective-permute-start | bytes 196616 | tf_op jit(solution)/shard_map/ppermute | solution.py:634
  70.0 4.2 %attend_head.2.refs_5_ = bf16[512,2048]{1,0:T(8,128)(2,1)} custom-call(s32[24]{0:T(128)S(1)} %get-tuple-element.47.meta_ref, bf16[512,2048]{1,0:T(8,128)(2,1)S(1)} %get-tuple-element.48.query_ref, bf16[2,128,256]{2,1,0:T(8,128)(2,1)S(1)} %get-tuple-element.69.refs_0_, bf16[2,128,256]{2,1,0:T(8,128)(2,1)S(1)} %collective-permute-done.17.refs_1_, ...), custom_call_target="tpu_custom_call" | custom-call | flops 1024 | bytes 1024 | tf_op jit(solution)/shard_map/attend_head/pallas_call | solution.py:498
  74.2 1.3 %collective-permute-start.24 = (bf16[1,128,256]{2,1,0:T(8,128)(2,1)S(1)}, bf16[1,128,256]{2,1,0:T(8,128)(2,1)S(1)}, u32[]{:S(2)}, u32[]{:S(2)}) collective-permute-start(bf16[1,128,256]{2,1,0:T(8,128)(2,1)S(1)} %slice.23), channel_id=1, source_target_pairs={{0,4},{4,0},{8,12},{12,8},{1,5},{5,1},{9,13},{13,9},{2,6},{6,2},{1... | collective-permute-start | bytes 196616 | tf_op jit(solution)/shard_map/ppermute | solution.py:634
  75.5 3.0 %collective-permute-done.24.refs_4_ = bf16[1,128,256]{2,1,0:T(8,128)(2,1)S(1)} collective-permute-done((bf16[1,128,256]{2,1,0:T(8,128)(2,1)S(1)}, bf16[1,128,256]{2,1,0:T(8,128)(2,1)S(1)}, u32[]{:S(2)}, u32[]{:S(2)}) %collective-permute-start.24) | collective-permute-done | bytes 65568 | tf_op jit(solution)/shard_map/ppermute | solution.py:634
  78.5 4.2 %attend_head.3 = bf16[512,2048]{1,0:T(8,128)(2,1)} custom-call(s32[24]{0:T(128)S(1)} %get-tuple-element.47.meta_ref, bf16[512,2048]{1,0:T(8,128)(2,1)S(1)} %get-tuple-element.48.query_ref, bf16[2,128,256]{2,1,0:T(8,128)(2,1)S(1)} %get-tuple-element.57.refs_0_, ...), custom_call_target="tpu_custom_call", output_to_operand_aliasing={{}: (7, {})} | custom-call | flops 1024 | bytes 1024 | tf_op jit(solution)/shard_map/attend_head/pallas_call | solution.py:498
  (84 shorter events, 12.1 us)
Async XLA Ops:
  1.1 10.0 %collective-permute-start = (bf16[2,320,128]{2,1,0:T(8,128)(2,1)S(1)}, bf16[2,320,128]{2,1,0:T(8,128)(2,1)S(1)}, u32[]{:S(2)}, u32[]{:S(2)}) collective-permute-start(bf16[2,320,128]{2,1,0:T(8,128)(2,1)S(1)} %get-tuple-element.74), channel_id=1, source_target_pairs={{0,2},{1,3},{2,0},{3,1},{4,6},{5,7},{6,4},{7,5},{8,10},{9,11},{10,... | collective-permute-start | bytes 491528 | tf_op jit(solution)/shard_map/ppermute | solution.py:546
  4.1 7.6 %collective-permute-start.1 = (bf16[4,320,128]{2,1,0:T(8,128)(2,1)}, bf16[4,320,128]{2,1,0:T(8,128)(2,1)S(1)}, u32[]{:S(2)}, u32[]{:S(2)}) collective-permute-start(bf16[4,320,128]{2,1,0:T(8,128)(2,1)} %bitcast.24), channel_id=1, source_target_pairs={{0,1},{1,0},{2,3},{3,2},{4,5},{5,4},{6,7},{7,6},{8,9},{9,8},{10,11... | collective-permute-start | bytes 983048 | tf_op jit(solution)/shard_map/ppermute | solution.py:596
  11.1 1.6 %collective-permute-start.2 = (bf16[2,320,128]{2,1,0:T(8,128)(2,1)S(1)}, bf16[2,320,128]{2,1,0:T(8,128)(2,1)S(1)}, u32[]{:S(2)}, u32[]{:S(2)}) collective-permute-start(bf16[2,320,128]{2,1,0:T(8,128)(2,1)S(1)} %collective-permute-done.refs_2_), channel_id=1, source_target_pairs={{0,1},{1,0},{2,3},{3,2},{4,5},{5,4},{6,7},{7,6},{8,9},{9,8},{10,11... | collective-permute-start | bytes 491528 | tf_op jit(solution)/shard_map/ppermute | solution.py:551
  11.6 8.7 %collective-permute-start.4 = (bf16[2,320,128]{2,1,0:T(8,128)(2,1)S(1)}, bf16[2,320,128]{2,1,0:T(8,128)(2,1)S(1)}, u32[]{:S(2)}, u32[]{:S(2)}) collective-permute-start(bf16[2,320,128]{2,1,0:T(8,128)(2,1)S(1)} %get-tuple-element.73), channel_id=1, source_target_pairs={{0,2},{1,3},{2,0},{3,1},{4,6},{5,7},{6,4},{7,5},{8,10},{9,11},{10,... | collective-permute-start | bytes 491528 | tf_op jit(solution)/shard_map/ppermute | solution.py:546
  20.0 1.4 %collective-permute-start.3 = (bf16[320,256]{1,0:T(8,128)(2,1)S(1)}, bf16[320,256]{1,0:T(8,128)(2,1)S(1)}, u32[]{:S(2)}, u32[]{:S(2)}) collective-permute-start(bf16[320,256]{1,0:T(8,128)(2,1)S(1)} %get-tuple-element.43), channel_id=1, source_target_pairs={{0,1},{1,0},{2,3},{3,2},{4,5},{5,4},{6,7},{7,6},{8,9},{9,8},{10,11... | collective-permute-start | bytes 491528 | tf_op jit(solution)/shard_map/ppermute | solution.py:532
  20.4 2.2 %collective-permute-start.5 = (bf16[2,320,128]{2,1,0:T(8,128)(2,1)S(1)}, bf16[2,320,128]{2,1,0:T(8,128)(2,1)S(1)}, u32[]{:S(2)}, u32[]{:S(2)}) collective-permute-start(bf16[2,320,128]{2,1,0:T(8,128)(2,1)S(1)} %collective-permute-done.4.refs_2_), channel_id=1, source_target_pairs={{0,1},{1,0},{2,3},{3,2},{4,5},{5,4},{6,7},{7,6},{8,9},{9,8},{10,11... | collective-permute-start | bytes 491528 | tf_op jit(solution)/shard_map/ppermute | solution.py:551
  20.6 6.0 %collective-permute-start.7 = (bf16[320,256]{1,0:T(8,128)(2,1)S(1)}, bf16[320,256]{1,0:T(8,128)(2,1)S(1)}, u32[]{:S(2)}, u32[]{:S(2)}) collective-permute-start(bf16[320,256]{1,0:T(8,128)(2,1)S(1)} %get-tuple-element.50), channel_id=1, source_target_pairs={{0,1},{1,0},{2,3},{3,2},{4,5},{5,4},{6,7},{7,6},{8,9},{9,8},{10,11... | collective-permute-start | bytes 491528 | tf_op jit(solution)/shard_map/ppermute | solution.py:532
  21.4 14.5 %collective-permute-start.8 = (bf16[320,256]{1,0:T(8,128)(2,1)S(1)}, bf16[320,256]{1,0:T(8,128)(2,1)S(1)}, u32[]{:S(2)}, u32[]{:S(2)}) collective-permute-start(bf16[320,256]{1,0:T(8,128)(2,1)S(1)} %add_convert_fusion.7), channel_id=1, source_target_pairs={{0,2},{1,3},{2,0},{3,1},{4,6},{5,7},{6,4},{7,5},{8,10},{9,11},{10,... | collective-permute-start | bytes 491528 | tf_op jit(solution)/shard_map/ppermute | solution.py:532
  26.1 9.8 %collective-permute-start.9 = (bf16[320,256]{1,0:T(8,128)(2,1)S(1)}, bf16[320,256]{1,0:T(8,128)(2,1)S(1)}, u32[]{:S(2)}, u32[]{:S(2)}) collective-permute-start(bf16[320,256]{1,0:T(8,128)(2,1)S(1)} %get-tuple-element.52), channel_id=1, source_target_pairs={{0,1},{1,0},{2,3},{3,2},{4,5},{5,4},{6,7},{7,6},{8,9},{9,8},{10,11... | collective-permute-start | bytes 491528 | tf_op jit(solution)/shard_map/ppermute | solution.py:532
  27.5 8.5 %collective-permute-start.10 = (bf16[320,256]{1,0:T(8,128)(2,1)S(1)}, bf16[320,256]{1,0:T(8,128)(2,1)S(1)}, u32[]{:S(2)}, u32[]{:S(2)}) collective-permute-start(bf16[320,256]{1,0:T(8,128)(2,1)S(1)} %add_convert_fusion.6), channel_id=1, source_target_pairs={{0,2},{1,3},{2,0},{3,1},{4,6},{5,7},{6,4},{7,5},{8,10},{9,11},{10,... | collective-permute-start | bytes 491528 | tf_op jit(solution)/shard_map/ppermute | solution.py:532
  37.9 1.6 %collective-permute-start.15 = (bf16[512,256]{1,0:T(8,128)(2,1)S(1)}, bf16[512,256]{1,0:T(8,128)(2,1)S(1)}, u32[]{:S(2)}, u32[]{:S(2)}) collective-permute-start(bf16[512,256]{1,0:T(8,128)(2,1)S(1)} %get-tuple-element.62), channel_id=1, source_target_pairs={{0,1},{1,0},{2,3},{3,2},{4,5},{5,4},{6,7},{7,6},{8,9},{9,8},{10,11... | collective-permute-start | bytes 786440 | tf_op jit(solution)/shard_map/ppermute | solution.py:532
  38.0 2.7 %collective-permute-start.12 = (bf16[512,256]{1,0:T(8,128)(2,1)S(1)}, bf16[512,256]{1,0:T(8,128)(2,1)S(1)}, u32[]{:S(2)}, u32[]{:S(2)}) collective-permute-start(bf16[512,256]{1,0:T(8,128)(2,1)S(1)} %get-tuple-element.56), channel_id=1, source_target_pairs={{0,1},{1,0},{2,3},{3,2},{4,5},{5,4},{6,7},{7,6},{8,9},{9,8},{10,11... | collective-permute-start | bytes 786440 | tf_op jit(solution)/shard_map/ppermute | solution.py:532
  38.5 15.5 %collective-permute-start.11 = (bf16[512,256]{1,0:T(8,128)(2,1)S(1)}, bf16[512,256]{1,0:T(8,128)(2,1)S(1)}, u32[]{:S(2)}, u32[]{:S(2)}) collective-permute-start(bf16[512,256]{1,0:T(8,128)(2,1)S(1)} %get-tuple-element.54), channel_id=1, source_target_pairs={{0,1},{1,0},{2,3},{3,2},{4,5},{5,4},{6,7},{7,6},{8,9},{9,8},{10,11... | collective-permute-start | bytes 786440 | tf_op jit(solution)/shard_map/ppermute | solution.py:532
  38.6 3.2 %collective-permute-start.14 = (bf16[512,256]{1,0:T(8,128)(2,1)S(1)}, bf16[512,256]{1,0:T(8,128)(2,1)S(1)}, u32[]{:S(2)}, u32[]{:S(2)}) collective-permute-start(bf16[512,256]{1,0:T(8,128)(2,1)S(1)} %get-tuple-element.60), channel_id=1, source_target_pairs={{0,1},{1,0},{2,3},{3,2},{4,5},{5,4},{6,7},{7,6},{8,9},{9,8},{10,11... | collective-permute-start | bytes 786440 | tf_op jit(solution)/shard_map/ppermute | solution.py:532
  39.6 9.2 %collective-permute-start.16 = (bf16[512,256]{1,0:T(8,128)(2,1)S(1)}, bf16[512,256]{1,0:T(8,128)(2,1)S(1)}, u32[]{:S(2)}, u32[]{:S(2)}) collective-permute-start(bf16[512,256]{1,0:T(8,128)(2,1)S(1)} %add_convert_fusion), channel_id=1, source_target_pairs={{0,2},{1,3},{2,0},{3,1},{4,6},{5,7},{6,4},{7,5},{8,10},{9,11},{10,... | collective-permute-start | bytes 786440 | tf_op jit(solution)/shard_map/ppermute | solution.py:532
  40.7 13.3 %collective-permute-start.13 = (bf16[512,256]{1,0:T(8,128)(2,1)S(1)}, bf16[512,256]{1,0:T(8,128)(2,1)S(1)}, u32[]{:S(2)}, u32[]{:S(2)}) collective-permute-start(bf16[512,256]{1,0:T(8,128)(2,1)S(1)} %add_convert_fusion.2), channel_id=1, source_target_pairs={{0,2},{1,3},{2,0},{3,1},{4,6},{5,7},{6,4},{7,5},{8,10},{9,11},{10,... | collective-permute-start | bytes 786440 | tf_op jit(solution)/shard_map/ppermute | solution.py:532
  49.5 9.0 %collective-permute-start.19 = (bf16[1,128,256]{2,1,0:T(8,128)(2,1)S(1)}, bf16[1,128,256]{2,1,0:T(8,128)(2,1)S(1)}, u32[]{:S(2)}, u32[]{:S(2)}) collective-permute-start(bf16[1,128,256]{2,1,0:T(8,128)(2,1)S(1)} %get-tuple-element.66), channel_id=1, source_target_pairs={{0,8},{4,12},{8,0},{12,4},{1,9},{5,13},{9,1},{13,5},{2,10},{6,14},... | collective-permute-start | bytes 196616 | tf_op jit(solution)/shard_map/ppermute | solution.py:634
  52.2 14.2 %collective-permute-start.17 = (bf16[2,128,256]{2,1,0:T(8,128)(2,1)S(1)}, bf16[2,128,256]{2,1,0:T(8,128)(2,1)S(1)}, u32[]{:S(2)}, u32[]{:S(2)}) collective-permute-start(bf16[2,128,256]{2,1,0:T(8,128)(2,1)S(1)} %get-tuple-element.63), channel_id=1, source_target_pairs={{0,4},{4,0},{8,12},{12,8},{1,5},{5,1},{9,13},{13,9},{2,6},{6,2},{1... | collective-permute-start | bytes 393224 | tf_op jit(solution)/shard_map/ppermute | solution.py:634
  53.8 7.7 %collective-permute-start.22 = (bf16[2,128,256]{2,1,0:T(8,128)(2,1)S(1)}, bf16[2,128,256]{2,1,0:T(8,128)(2,1)S(1)}, u32[]{:S(2)}, u32[]{:S(2)}) collective-permute-start(bf16[2,128,256]{2,1,0:T(8,128)(2,1)S(1)} %get-tuple-element.70), channel_id=1, source_target_pairs={{0,12},{4,8},{8,4},{12,0},{1,13},{5,9},{9,5},{13,1},{2,14},{6,10},... | collective-permute-start | bytes 393224 | tf_op jit(solution)/shard_map/ppermute | solution.py:634
  54.8 19.4 %collective-permute-start.21 = (bf16[2,128,256]{2,1,0:T(8,128)(2,1)S(1)}, bf16[2,128,256]{2,1,0:T(8,128)(2,1)S(1)}, u32[]{:S(2)}, u32[]{:S(2)}) collective-permute-start(bf16[2,128,256]{2,1,0:T(8,128)(2,1)S(1)} %get-tuple-element.68), channel_id=1, source_target_pairs={{0,12},{4,8},{8,4},{12,0},{1,13},{5,9},{9,5},{13,1},{2,14},{6,10},... | collective-permute-start | bytes 393224 | tf_op jit(solution)/shard_map/ppermute | solution.py:634
  61.5 8.5 %collective-permute-start.23 = (bf16[1,128,256]{2,1,0:T(8,128)(2,1)S(1)}, bf16[1,128,256]{2,1,0:T(8,128)(2,1)S(1)}, u32[]{:S(2)}, u32[]{:S(2)}) collective-permute-start(bf16[1,128,256]{2,1,0:T(8,128)(2,1)S(1)} %slice.22), channel_id=1, source_target_pairs={{0,4},{4,0},{8,12},{12,8},{1,5},{5,1},{9,13},{13,9},{2,6},{6,2},{1... | collective-permute-start | bytes 196616 | tf_op jit(solution)/shard_map/ppermute | solution.py:634
  66.4 9.1 %collective-permute-start.18 = (bf16[2,128,256]{2,1,0:T(8,128)(2,1)S(1)}, bf16[2,128,256]{2,1,0:T(8,128)(2,1)S(1)}, u32[]{:S(2)}, u32[]{:S(2)}) collective-permute-start(bf16[2,128,256]{2,1,0:T(8,128)(2,1)S(1)} %get-tuple-element.64), channel_id=1, source_target_pairs={{0,4},{4,0},{8,12},{12,8},{1,5},{5,1},{9,13},{13,9},{2,6},{6,2},{1... | collective-permute-start | bytes 393224 | tf_op jit(solution)/shard_map/ppermute | solution.py:634
  66.5 9.0 %collective-permute-start.20 = (bf16[1,128,256]{2,1,0:T(8,128)(2,1)S(1)}, bf16[1,128,256]{2,1,0:T(8,128)(2,1)S(1)}, u32[]{:S(2)}, u32[]{:S(2)}) collective-permute-start(bf16[1,128,256]{2,1,0:T(8,128)(2,1)S(1)} %get-tuple-element.67), channel_id=1, source_target_pairs={{0,8},{4,12},{8,0},{12,4},{1,9},{5,13},{9,1},{13,5},{2,10},{6,14},... | collective-permute-start | bytes 196616 | tf_op jit(solution)/shard_map/ppermute | solution.py:634
  74.2 4.3 %collective-permute-start.24 = (bf16[1,128,256]{2,1,0:T(8,128)(2,1)S(1)}, bf16[1,128,256]{2,1,0:T(8,128)(2,1)S(1)}, u32[]{:S(2)}, u32[]{:S(2)}) collective-permute-start(bf16[1,128,256]{2,1,0:T(8,128)(2,1)S(1)} %slice.23), channel_id=1, source_target_pairs={{0,4},{4,0},{8,12},{12,8},{1,5},{5,1},{9,13},{13,9},{2,6},{6,2},{1... | collective-permute-start | bytes 196616 | tf_op jit(solution)/shard_map/ppermute | solution.py:634
  (19 other events, 106.3 us)

commit v4 on v3

--- a/solution.py
+++ b/solution.py
@@ -15,6 +15,7 @@
 LANES = 128
 ROW_BLOCK = 128
 HIDDEN_BLOCK = 256
+HEAD_GROUP = 8
 VALUE_SHIFT = 2.0**-24
 epsilon = 1e-05
 
@@ -76,17 +77,19 @@
     return (rows + extra, whole) if extra else (rows, width)
 
 
-def layout_kernel(group_count, tiles_local, where_ref, tiles_ref, owner_ref, text_ref, meta_ref):
+def layout_kernel(group_count, tiles_local, where_ref, meta_ref):
     group = where_ref[0]
+    requests = (where_ref.shape[0] - 2) // 3
+    tiles_of, owner_of, text_of = ([where_ref[2 + n * requests + r] for r in range(requests)] for n in range(3))
     zero = jnp.int32(0)
     firsts, counts, offsets, texts_first, texts_both = [], [], [], [], []
     offset = zero
     for p in range(group_count):
         first, count, text_first, text_both, seen = zero, zero, zero, zero, zero
-        for r in range(owner_ref.shape[0]):
-            mine = owner_ref[r] == p
-            tiles = jnp.where(mine, tiles_ref[r], 0)
-            text = jnp.where(mine, text_ref[r], 0)
+        for r in range(requests):
+            mine = owner_of[r] == p
+            tiles = jnp.where(mine, tiles_of[r], 0)
+            text = jnp.where(mine, text_of[r], 0)
             first = first + jnp.where(seen == 0, tiles, 0)
             text_first = text_first + jnp.where(seen == 0, text, 0)
             count = count + tiles
@@ -120,7 +123,6 @@
     my_first, my_count = pick(firsts, group), pick(counts, group)
     my_offset = pick(offsets, group)
     place = meta_places(group_count)
-    meta_ref[place["tp"]] = where_ref[1]
     meta_ref[place["first"]] = my_first
     meta_ref[place["second"]] = my_count - my_first
     meta_ref[place["text_first"]] = pick(texts_first, group)
@@ -152,19 +154,18 @@
         "text_first": 2,
         "text_both": 3,
         "star": 4,
-        "tp": 5,
         "send": 8,
         "goes": 8 + table,
         "size": 8 + 2 * table,
     }
 
 
-def mlp_kernel(piece_count, bases, tiles, place, meta_ref, *refs):
+def mlp_kernel(piece_count, bases, tiles, where_ref, *refs):
     pieces = refs[:piece_count]
     gain_ref, bias_ref, up_bias_ref, up_ref, down_ref = refs[piece_count : piece_count + 5]
     outs = refs[piece_count + 5 : 2 * piece_count + 5]
     cat_ref, normed_ref, hidden_ref, total_ref = refs[2 * piece_count + 5 :]
-    index = meta_ref[place]
+    index = where_ref[1]
     _, width, tile_rows = pieces[0].shape
     rows = tiles * tile_rows
     channels, hidden_width = up_ref.shape
@@ -209,14 +210,14 @@
                 out[take, :] = block
 
 
-def encoder_mlp(meta, place, pieces, bases, tiles, ln_gain, ln_bias, w_up, b_up, w_down):
+def encoder_mlp(where, pieces, bases, tiles, ln_gain, ln_bias, w_up, b_up, w_down):
     _, width, tile_rows = pieces[0].shape
     rows = tiles * tile_rows
     count = len(pieces)
     channels, hidden_width = w_up.shape
     shape = sent_shape(rows, width)
     return pl.pallas_call(
-        functools.partial(mlp_kernel, count, bases, tiles, place),
+        functools.partial(mlp_kernel, count, bases, tiles),
         out_shape=[jax.ShapeDtypeStruct(shape, BF16)] * count,
         in_specs=[SMEM] + [VMEM] * (count + 5),
         out_specs=[VMEM] * count,
@@ -230,7 +231,7 @@
         cost_estimate=LIGHT,
         name="encoder_mlp",
     )(
-        meta,
+        where,
         *pieces,
         lane_rows(ln_gain),
         lane_rows(ln_bias),
@@ -244,9 +245,6 @@
     group_count,
     tiles_local,
     where_ref,
-    tiles_ref,
-    owner_ref,
-    text_ref,
     gain_ref,
     query_ref,
     normed_ref,
@@ -254,9 +252,7 @@
 ):
     @pl.when(pl.program_id(0) == 0)
     def _():
-        layout_kernel(
-            group_count, tiles_local, where_ref, tiles_ref, owner_ref, text_ref, meta_ref
-        )
+        layout_kernel(group_count, tiles_local, where_ref, meta_ref)
 
     gain = gain_ref[...] * (math.log2(math.e) / math.sqrt(HD))
     for col in range(0, query_ref.shape[1], HD):
@@ -265,7 +261,7 @@
         normed_ref[:, col : col + HD] = (values * lax.rsqrt(square + epsilon) * gain).astype(BF16)
 
 
-def prepare(where, requests, q_gain, queries, group_count, tiles_local):
+def prepare(where, q_gain, queries, group_count, tiles_local):
     text_rows, width = queries.shape
     step = ROW_BLOCK
     return pl.pallas_call(
@@ -277,9 +273,6 @@
         grid=(text_rows // step,),
         in_specs=[
             SMEM,
-            SMEM,
-            SMEM,
-            SMEM,
             pl.BlockSpec((1, HD), lambda n: (0, 0)),
             pl.BlockSpec((step, width), lambda n: (n, 0)),
         ],
@@ -287,56 +280,85 @@
         compiler_params=pltpu.CompilerParams(vmem_limit_bytes=16 * MIB),
         cost_estimate=LIGHT,
         name="prepare",
-    )(where, *requests, lane_rows(q_gain), queries)
-
-
-def tap_kernel(meta_ref, tap_ref, weight_ref, out_ref, row_ref):
-    @pl.when(pl.program_id(0) == 0)
-    def _():
-        tiles, _, tile_rows = tap_ref.shape
-        for tile in range(tiles):
-            row_ref[tile * tile_rows : (tile + 1) * tile_rows, :] = tap_ref[tile].T
-
+    )(where, lane_rows(q_gain), queries)
+
+
+def tap_kernel(staged, first, where_ref, tap_ref, weight_ref, *refs):
+    sources, out_ref = refs[:staged], refs[staged]
+    targets, scratch = refs[staged + 1 : 2 * staged + 1], refs[2 * staged + 1 :]
+    step, last = pl.program_id(0), pl.num_programs(0) - 1
+
+    def copies():
+        return [
+            pltpu.make_async_copy(source, target, scratch[1].at[n])
+            for n, (source, target) in enumerate(zip(sources, targets))
+        ]
+
+    if first:
+        row_ref = scratch[0]
+
+        @pl.when(step == 0)
+        def _():
+            for copy in copies():
+                copy.start()
+            tiles, _, tile_rows = tap_ref.shape
+            for tile in range(tiles):
+                row_ref[tile * tile_rows : (tile + 1) * tile_rows, :] = tap_ref[tile].T
+
+    else:
+        row_ref = tap_ref
     out_ref[...] = jnp.dot(
         row_ref[...], weight_ref[...], preferred_element_type=F32
-    ).astype(BF16)[None, None]
-
-
-def tap_projection(meta, place, tap_tiles, weights, head_count, dest_count, dup):
-    tiles, depth, tile_rows = tap_tiles.shape
-    rows = tiles * tile_rows
+    ).astype(BF16)[None]
+    if first:
+
+        @pl.when(step == last)
+        def _():
+            for copy in copies():
+                copy.wait()
+
+
+def tap_projection(where, taps, weights, head, head_count, dest_count, dup, staged):
+    first = head == 0
+    if first:
+        tiles, depth, tile_rows = taps.shape
+        rows = tiles * tile_rows
+    else:
+        rows, depth = taps.shape
     block = 2 * HD
 
-    def head_of(n, meta_ref):
-        dest = lax.div(meta_ref[place], jnp.int32(dup)) ^ lax.rem(n, dest_count)
-        return dest * head_count + lax.div(n, dest_count)
-
+    def head_of(n, where_ref):
+        return (lax.div(where_ref[1], jnp.int32(dup)) ^ n) * head_count + head
+
+    row_shape = jax.ShapeDtypeStruct((rows, depth), BF16)
     return pl.pallas_call(
-        tap_kernel,
-        out_shape=jax.ShapeDtypeStruct((head_count, dest_count, rows, block), BF16),
+        functools.partial(tap_kernel, len(staged), first),
+        out_shape=[jax.ShapeDtypeStruct((dest_count, rows, block), BF16)]
+        + [jax.ShapeDtypeStruct(w.shape, w.dtype) for w in staged]
+        + ([row_shape] if first else []),
         grid_spec=pltpu.PrefetchScalarGridSpec(
             num_scalar_prefetch=1,
-            grid=(head_count * dest_count,),
+            grid=(dest_count,),
             in_specs=[
-                pl.BlockSpec(tap_tiles.shape, lambda n, w: (0, 0, 0)),
+                VMEM,
                 pl.BlockSpec((depth, block), lambda n, w: (0, head_of(n, w))),
-            ],
-            out_specs=pl.BlockSpec(
-                (1, 1, rows, block),
-                lambda n, w: (lax.div(n, dest_count), lax.rem(n, dest_count), 0, 0),
-            ),
-            scratch_shapes=[pltpu.VMEM((rows, depth), BF16)],
+            ]
+            + [HBM] * len(staged),
+            out_specs=[pl.BlockSpec((1, rows, block), lambda n, w: (n, 0, 0))]
+            + [VMEM] * (len(staged) + first),
+            scratch_shapes=[pltpu.SemaphoreType.DMA((max(1, len(staged)),))] if first else [],
         ),
-        compiler_params=pltpu.CompilerParams(vmem_limit_bytes=16 * MIB),
+        compiler_params=pltpu.CompilerParams(vmem_limit_bytes=(42 if first else 50) * MIB),
         cost_estimate=LIGHT,
         name="tap_projection",
-    )(meta, tap_tiles, weights)
-
-
-def kv_kernel(head_count, dest_count, dup, place, term_counts, meta_ref, *refs):
-    x_ref, bias_ref, weight_ref, tap_ref = refs[:4]
-    terms = refs[4 : 4 + sum(term_counts)]
-    outs = refs[4 + sum(term_counts) : -1]
+    )(where, taps, weights, *staged)
+
+
+def kv_kernel(head_count, dest_count, dup, term_counts, where_ref, *refs):
+    x_ref, bias_ref, weight_ref = refs[:3]
+    tap_refs = refs[3 : 3 + head_count]
+    terms = refs[3 + head_count : 3 + head_count + sum(term_counts)]
+    outs = refs[3 + head_count + sum(term_counts) : -1]
     encoded_ref = refs[-1]
     tiles, width, tile_rows = x_ref.shape
     half_tiles = tiles // len(term_counts)
@@ -364,34 +386,34 @@
         total = total + x_ref[tile].T.astype(F32) + bias
         encoded_ref[tile * tile_rows : (tile + 1) * tile_rows, :] = total.astype(BF16)
     block = 2 * HD
-    mine = lax.div(meta_ref[place], jnp.int32(dup))
+    mine = lax.div(where_ref[1], jnp.int32(dup))
     for head in range(head_count):
         for k in range(dest_count):
             column = ((mine ^ k) * head_count + head) * block
             weights = weight_ref[:, pl.ds(pl.multiple_of(column, block), block)]
             value = jnp.dot(encoded_ref[...], weights, preferred_element_type=F32)
-            value = value + tap_ref[head, k].astype(F32)
+            value = value + tap_refs[head][k].astype(F32)
             outs[head * dest_count + k][...] = value.astype(BF16)
 
 
-def kv_projection(meta, place, x_tiles, b_down, weights, tap_part, halves, dup):
+def kv_projection(where, x_tiles, b_down, weights, tap_parts, halves, dup):
     terms = [term for half in halves for term in half]
     tiles, width, tile_rows = x_tiles.shape
     rows = tiles * tile_rows
-    head_count, dest_count = tap_part.shape[:2]
+    head_count, dest_count = len(tap_parts), tap_parts[0].shape[0]
     block = 2 * HD
     outs = pl.pallas_call(
         functools.partial(
-            kv_kernel, head_count, dest_count, dup, place, tuple(len(half) for half in halves)
+            kv_kernel, head_count, dest_count, dup, tuple(len(half) for half in halves)
         ),
         out_shape=[jax.ShapeDtypeStruct((rows, block), BF16)] * (head_count * dest_count),
-        in_specs=[SMEM] + [VMEM] * (4 + len(terms)),
+        in_specs=[SMEM] + [VMEM] * (3 + head_count + len(terms)),
         out_specs=[VMEM] * (head_count * dest_count),
         scratch_shapes=[pltpu.VMEM((rows, width), BF16)],
         compiler_params=pltpu.CompilerParams(vmem_limit_bytes=24 * MIB),
         cost_estimate=LIGHT,
         name="kv_projection",
-    )(meta, x_tiles, lane_rows(b_down), weights, tap_part, *terms)
+    )(where, x_tiles, lane_rows(b_down), weights, *tap_parts, *terms)
     return [outs[h * dest_count : (h + 1) * dest_count] for h in range(head_count)]
 
 
@@ -463,10 +485,13 @@
                 part = pl.ds(label * span, key_rows)
                 slots = start + lax.broadcasted_iota(jnp.int32, (ROW_BLOCK, HD), 0)
                 owned = (slots >= low) & (slots < high)
-                for head in range(heads):
-                    lanes = slice(head * HD, (head + 1) * HD)
+                for first in range(0, heads, HEAD_GROUP):
+                    group = range(first, min(first + HEAD_GROUP, heads))
+                    stacked = jnp.concatenate(
+                        [query_ref[take, h * HD : (h + 1) * HD] for h in group], axis=0
+                    )
                     scores = lax.dot_general(
-                        query_ref[take, lanes],
+                        stacked,
                         key_ref[part, :],
                         (((1,), (1,)), ((), ())),
                         preferred_element_type=F32,
@@ -474,8 +499,11 @@
                     weights = jnp.exp2(scores).astype(BF16)
                     sums = jnp.dot(weights, value_ref[part, :], preferred_element_type=F32)
                     result = sums[:, :HD] / sums[:, HD:] * (1.0 / VALUE_SHIFT)
-                    kept = out_ref[take, lanes].astype(F32)
-                    out_ref[take, lanes] = jnp.where(owned, result, kept).astype(BF16)
+                    for n, h in enumerate(group):
+                        lanes = slice(h * HD, (h + 1) * HD)
+                        own = result[n * ROW_BLOCK : (n + 1) * ROW_BLOCK]
+                        kept = out_ref[take, lanes].astype(F32)
+                        out_ref[take, lanes] = jnp.where(owned, own, kept).astype(BF16)
 
             half = span // 2
             few = counts[label] * ROW_BLOCK <= half
@@ -521,7 +549,12 @@
     return (a.astype(F32) + b.astype(F32)).astype(BF16)
 
 
-def scatter_sum(blocks, count, first_bit):
+def after(value, *others):
+    others = [v for v in others if v is not None]
+    return lax.optimization_barrier((value, others))[0]
+
+
+def scatter_sum(blocks, count, first_bit, earlier=None):
     blocks = dict(enumerate(blocks))
     bits = bits_of(len(blocks))
     for b in range(bits):
@@ -529,6 +562,8 @@
         got, sent = {}, None
         for k in sorted((k for k in blocks if (k >> b) & 1), reverse=True):
             sent = blocks[k]
+            if b == bits - 1 and earlier is not None:
+                sent = after(sent, earlier)
             got[k ^ (1 << b)] = lax.ppermute(sent, "tp", pairs)
         if b == bits - 1:
             return [blocks[0], got[0]], sent
@@ -536,10 +571,9 @@
     return [blocks[0]], blocks[0]
 
 
-def gather_half(whole, tiles, half, count, ready):
+def gather_half(whole, own, first, count, ready):
     bits = bits_of(count)
-    first = half * tiles
-    pieces = {0: whole[0][first : first + tiles]}
+    pieces = {0: own}
     for b in reversed(range(1, bits)):
         pairs = xor_pairs(count, 1 << b)
         for k in sorted(pieces):
@@ -547,11 +581,10 @@
     pairs = xor_pairs(count, 1)
     for k in sorted(pieces):
         if k:
-            block, ready = lax.optimization_barrier((pieces[k], ready))
-            pieces[k | 1] = lax.ppermute(block, "tp", pairs)
+            pieces[k | 1] = lax.ppermute(after(pieces[k], ready), "tp", pairs)
     pieces[0], pieces[1] = whole
     bases = tuple(first if k < 2 else 0 for k in range(count))
-    return [pieces[k] for k in range(count)], bases, ready
+    return [pieces[k] for k in range(count)], bases
 
 
 def local(
@@ -574,7 +607,8 @@
 ):
     group_count = lax.axis_size("grp")
     tp_count = lax.axis_size("tp")
-    where = jnp.stack([lax.axis_index("grp"), lax.axis_index("tp")]).astype(jnp.int32)
+    position = jnp.stack([lax.axis_index("grp"), lax.axis_index("tp")]).astype(jnp.int32)
+    where = jnp.concatenate([position, tiles_per_request, owner, text_per_request])
     tiles_local = x_in.shape[0]
     x_tiles = jnp.swapaxes(x_in, 2, 3)[:, 0]
     tap_tiles = jnp.swapaxes(taps, 2, 3)[:, 0]
@@ -583,69 +617,69 @@
     dest_count = tp_count // dup
     place = meta_places(group_count)
 
-    query_rows, meta = prepare(
-        where,
-        (tiles_per_request, owner, text_per_request),
-        q_gain,
-        queries,
-        group_count,
-        tiles_local,
-    )
     halves = 2 if tiles_local % 2 == 0 else 1
     tiles = tiles_local // halves
+    own_halves = [x_tiles[:tiles]] + [
+        after(x_tiles, where)[h * tiles : (h + 1) * tiles] for h in range(1, halves)
+    ]
     whole = [x_tiles, lax.ppermute(x_tiles, "tp", xor_pairs(tp_count, 1))]
+
+    first_taps, w_up, w_down, tap_rows = tap_projection(
+        where, tap_tiles, kv_w_taps, 0, head_count, dest_count, dup, (w_up, w_down)
+    )
+    tap_parts = [first_taps]
     mlp_terms = []
-    ready = meta
+    ready, begun = first_taps, where
     for half in range(halves):
-        pieces, bases, ready = gather_half(whole, tiles, half, tp_count, ready)
-        if half == 0:
-            meta = ready
+        pieces, bases = gather_half(whole, own_halves[half], half * tiles, tp_count, ready)
         mlp_blocks = encoder_mlp(
-            meta, place["tp"], pieces, bases, tiles, ln_gain, ln_bias, w_up, b_up, w_down
+            begun, pieces, bases, tiles, ln_gain, ln_bias, w_up, b_up, w_down
         )
         terms, sent = scatter_sum(mlp_blocks, tp_count, 0)
         mlp_terms.append(terms)
-        ready, _ = lax.optimization_barrier((meta, mlp_blocks[0]))
-        meta, _ = lax.optimization_barrier((meta, sent))
-    tap_part = tap_projection(
-        meta, place["tp"], tap_tiles, kv_w_taps, head_count, dest_count, dup
+        ready, begun = mlp_blocks[0], after(where, sent)
+    for head in range(1, head_count):
+        tap_parts += tap_projection(
+            begun, tap_rows, kv_w_taps, head, head_count, dest_count, dup, ()
+        )
+    kv_blocks = kv_projection(
+        where, x_tiles, b_down, kv_w_out, tap_parts, mlp_terms, dup
     )
-    kv_blocks = kv_projection(
-        meta, place["tp"], x_tiles, b_down, kv_w_out, tap_part, mlp_terms, dup
-    )
-
-    slots = slot_count_of(group_count)
-    total_tiles = group_count * tiles_local
-    most_other = total_tiles - REQ_G * MAXT - REQ_G * (group_count - 2)
-    one_large = group_count == 4 and slots == 2 and most_other <= group_count
-    out = None
-    before = {}
+    kv_terms, arrived = [], None
     for head in range(head_count):
         blocks = kv_blocks[head]
         for b in range(bits_of(dup)):
             pairs = xor_pairs(tp_count, 1 << b)
             blocks = [add_rounded(v, lax.ppermute(v, "tp", pairs)) for v in blocks]
-        terms, _ = scatter_sum(blocks, tp_count, bits_of(dup))
-        send = place["send"]
-
-        def move(value, mask, name):
-            if name in before:
-                value, _ = lax.optimization_barrier((value, before[name]))
-            got = lax.ppermute(value, "grp", xor_pairs(group_count, mask))
-            if name is not None:
-                before[name] = got
-            return got
-
+        terms, sent = scatter_sum(blocks, tp_count, bits_of(dup), arrived)
+        kv_terms.append(terms)
+        if head == 0:
+            query_rows, meta = prepare(
+                after(where, sent), q_gain, queries, group_count, tiles_local
+            )
+        arrived = (terms[-1], meta)
+
+    slots = slot_count_of(group_count)
+    total_tiles = group_count * tiles_local
+    most_other = total_tiles - REQ_G * MAXT - REQ_G * (group_count - 2)
+    one_large = group_count == 4 and slots == 2 and most_other <= group_count
+    send = place["send"]
+    out, before = None, ()
+
+    def move(value, mask):
+        return lax.ppermute(value, "grp", xor_pairs(group_count, mask))
+
+    for head in range(head_count):
+        terms = kv_terms[head]
         if one_large:
             star = place["star"]
             picks = ((send, star), (send + 1, star), (send + 2,), (send + 3, star))
             own, near, middle, far = finish_tiles(meta, k_gain, terms, picks)
-            far_got = move(far, 3, None)
-            middle_got = move(middle, 2, "middle")
-            near_got = move(near, 1, "near")
-            after = middle_got if out is None else out
-            far_got, _ = lax.optimization_barrier((far_got, after))
-            passed = move(far_got[1:], 1, None)
+            if before:
+                near, middle, far = (after(v, w) for v, w in zip((near, middle, far), before))
+            far_got, middle_got, near_got = move(far, 3), move(middle, 2), move(near, 1)
+            before = (near_got, far_got, middle_got)
+            passed = move(after(far_got[1:], middle_got, out), 1)
             tiles = (own, near_got, middle_got, far_got, passed)
             sources = ((0, 4), (1, 5), (2,), (3, 7), (6,))
         else:
@@ -653,7 +687,7 @@
                 tuple(send + s * group_count + d for s in range(slots)) for d in range(group_count)
             )
             made = finish_tiles(meta, k_gain, terms, picks)
-            tiles = tuple(made[:1]) + tuple(move(made[d], d, d) for d in range(1, group_count))
+            tiles = tuple(made[:1]) + tuple(move(made[d], d) for d in range(1, group_count))
             sources = tuple(
                 tuple(s * group_count + d for s in range(slots)) for d in range(group_count)
             )

time: 84.3 us -> 80.2 us (0.951); the launches traced: 82.8 us -> 80 us
  starting transfers between devices: 28.6 us -> 19.8 us
  waiting for transfers between devices: 15.7 us -> 23.9 us
  local copies, waits for them, and re-layouts: 9.18 us -> 3.19 us
  Pallas kernels: 28.6 us -> 32.4 us
    ppermute x10, starting transfers between devices: 18.7 us -> 9.73 us  [the longest x8 9.16 us: move(): return lax.ppermute(value, 'grp', xor_pairs(group_count, mask))]
    ppermute x10, waiting for transfers between devices: 6.96 us -> 15.7 us  [the longest x8 14.3 us: move(): return lax.ppermute(value, 'grp', xor_pairs(group_count, mask))]
    unnamed x36 -> x20, local copies, waits for them, and re-layouts: 8.11 us -> 1.47 us
    pallas_call x3 -> x4, Pallas kernels: 14.2 us -> 18.1 us  [the longest x2 11.2 us: tap_projection(): pl.pallas_call(functools.partial(tap_kernel, len(staged), first), out_sha...]
    ppermute x12, waiting for transfers between devices: 8.71 us -> 6.96 us  [scatter_sum(): got[k ^ 1 << b] = lax.ppermute(sent, 'tp', pairs)]
    ppermute x2, waiting for transfers between devices: 0.01 us -> 1.31 us  [gather_half(): pieces[k | 1 << b] = lax.ppermute(pieces[k], 'tp', pairs)]
  transfers between devices with their start and end apart: 25 -> 25, of which waited for: 7 -> 11; matrix products, arithmetic and copies ran while one was open for 1% -> 2% of each run, Pallas kernels for 27% -> 33%
where the time goes in v4:
time: 80.2 us; the launch traced here: 80 us
  Pallas kernels  32.4 us (40%)
  waiting for transfers between devices  23.9 us (30%)
  starting transfers between devices  19.8 us (25%)
  local copies, waits for them, and re-layouts  3.19 us (4%)
    ppermute x8, waiting for transfers between devices, move(): return lax.ppermute(value, 'grp', xor_pairs(group_count, mask))  14.3 us
    pallas_call x2, Pallas kernels, tap_projection(): pl.pallas_call(functools.partial(tap_kernel, len(staged), first), out_sha...  11.2 us
    ppermute x8, starting transfers between devices, move(): return lax.ppermute(value, 'grp', xor_pairs(group_count, mask))  9.16 us
    pallas_call x2, Pallas kernels, attend_head(): pl.pallas_call(functools.partial(attend_kernel, group_count, sources, len...  8.4 us
    ppermute x12, waiting for transfers between devices, scatter_sum(): got[k ^ 1 << b] = lax.ppermute(sent, 'tp', pairs)  6.96 us
    pallas_call x2, Pallas kernels, encoder_mlp(): pl.pallas_call(functools.partial(mlp_kernel, count, bases, tiles), out_sh...  6.86 us
    ppermute x12, starting transfers between devices, scatter_sum(): got[k ^ 1 << b] = lax.ppermute(sent, 'tp', pairs)  6.85 us
    ppermute x2, starting transfers between devices, gather_half(): pieces[k | 1 << b] = lax.ppermute(pieces[k], 'tp', pairs)  3.18 us
  transfers between devices with their start and end apart: 25, of which 11 were waited for; matrix products, arithmetic and copies ran while one was open for 2% of the time, Pallas kernels for 33%

profile of v4, /device:TPU:0, one launch (start us, length us, event | category | flops | bytes accessed | tf_op | source)
XLA Modules:
  0.0 80.0 jit_solution(16831912599053506548)
XLA Ops:
  0.0 0.9 %slice_bitcast_fusion = bf16[2,320,128]{2,1,0:T(8,128)(2,1)S(1)} fusion(bf16[4,1,320,128]{3,2,0,1:T(8,128)(2,1)} %bitcast.21), kind=kLoop, calls=%fused_computation.8 | loop fusion | bytes 327680 | tf_op jit(solution)/shard_map/slice | solution.py:622
  0.9 3.0 %collective-permute-start.1 = (bf16[2,320,128]{2,1,0:T(8,128)(2,1)S(1)}, bf16[2,320,128]{2,1,0:T(8,128)(2,1)S(1)}, u32[]{:S(2)}, u32[]{:S(2)}) collective-permute-start(bf16[2,320,128]{2,1,0:T(8,128)(2,1)S(1)} %slice_bitcast_fusion), channel_id=1, source_target_pairs={{0,2},{1,3},{2,0},{3,1},{4,6},{5,7},{6,4},{7,5},{8,10},{9,11},{10,... | collective-permute-start | bytes 491528 | tf_op jit(solution)/shard_map/ppermute | solution.py:580
  4.7 1.4 %copy-done.2 = bf16[4,1,128,1600]{2,3,1,0:T(8,128)(2,1)S(1)} copy-done((bf16[4,1,128,1600]{2,3,1,0:T(8,128)(2,1)S(1)}, bf16[4,1,128,1600]{2,3,1,0:T(8,128)(2,1)}, u32[]{:S(2)}) %copy-start.2) | copy-done | bytes 1638424
  6.2 6.3 %tap_projection.2 = (bf16[4,512,256]{2,1,0:T(8,128)(2,1)S(1)}, bf16[1280,1280]{1,0:T(8,128)(2,1)S(1)}, bf16[1280,1280]{1,0:T(8,128)(2,1)S(1)}, bf16[512,1600]{1,0:T(8,128)(2,1)S(1)}) custom-call(s32[26]{0:T(128)S(1)} %concatenate.3.where_ref, bf16[4,1600,128]{2,1,0:T(8,128)(2,1)S(1)} %bitcast.27, bf16[1600,2048]{1,0:T(8,128)(2,1)} %weight_ref.3, ...), custom_call_target="tpu_custom_call" | custom-call | flops 1024 | bytes 1024 | tf_op jit(solution)/shard_map/tap_projection/pallas_call | solution.py:334
  14.2 3.4 %encoder_mlp.2 = (bf16[320,256]{1,0:T(8,128)(2,1)S(1)}, bf16[320,256]{1,0:T(8,128)(2,1)S(1)}, bf16[320,256]{1,0:T(8,128)(2,1)S(1)}, bf16[320,256]{1,0:T(8,128)(2,1)S(1)}) custom-call(s32[26]{0:T(128)S(1)} %concatenate.3.where_ref, bf16[4,320,128]{2,1,0:T(8,128)(2,1)S(1)} %bitcast.24, bf16[4,320,128]{2,1,0:T(8,128)(2,1)S(1)} %collective-permute-done.refs_1_, ...), custom_call_target="tpu_custom_call" | custom-call | flops 1024 | bytes 1024 | tf_op jit(solution)/shard_map/encoder_mlp/pallas_call | solution.py:219
  18.0 1.3 %collective-permute-done.4.refs_2_ = bf16[2,320,128]{2,1,0:T(8,128)(2,1)S(1)} collective-permute-done((bf16[2,320,128]{2,1,0:T(8,128)(2,1)S(1)}, bf16[2,320,128]{2,1,0:T(8,128)(2,1)S(1)}, u32[]{:S(2)}, u32[]{:S(2)}) %collective-permute-start.4) | collective-permute-done | bytes 163872 | tf_op jit(solution)/shard_map/ppermute | solution.py:580
  20.7 3.4 %encoder_mlp.3 = (bf16[320,256]{1,0:T(8,128)(2,1)S(1)}, bf16[320,256]{1,0:T(8,128)(2,1)S(1)}, bf16[320,256]{1,0:T(8,128)(2,1)S(1)}, bf16[320,256]{1,0:T(8,128)(2,1)S(1)}) custom-call(s32[26]{0:T(128)S(1)} %concatenate.3.where_ref, bf16[4,320,128]{2,1,0:T(8,128)(2,1)S(1)} %bitcast.25, bf16[4,320,128]{2,1,0:T(8,128)(2,1)S(1)} %collective-permute-done.refs_1_, ...), custom_call_target="tpu_custom_call" | custom-call | flops 1024 | bytes 1024 | tf_op jit(solution)/shard_map/encoder_mlp/pallas_call | solution.py:219
  24.7 1.1 %collective-permute-done.6 = bf16[320,256]{1,0:T(8,128)(2,1)S(1)} collective-permute-done((bf16[320,256]{1,0:T(8,128)(2,1)S(1)}, bf16[320,256]{1,0:T(8,128)(2,1)S(1)}, u32[]{:S(2)}, u32[]{:S(2)}) %collective-permute-start.6) | collective-permute-done | bytes 163872 | tf_op jit(solution)/shard_map/ppermute | solution.py:567
  25.8 1.3 %collective-permute-start.10 = (bf16[320,256]{1,0:T(8,128)(2,1)S(1)}, bf16[320,256]{1,0:T(8,128)(2,1)S(1)}, u32[]{:S(2)}, u32[]{:S(2)}) collective-permute-start(bf16[320,256]{1,0:T(8,128)(2,1)S(1)} %add_convert_fusion.6), channel_id=1, source_target_pairs={{0,2},{1,3},{2,0},{3,1},{4,6},{5,7},{6,4},{7,5},{8,10},{9,11},{10,... | collective-permute-start | bytes 491528 | tf_op jit(solution)/shard_map/ppermute | solution.py:567
  27.2 4.9 %tap_projection.3.refs_4_ = bf16[4,512,256]{2,1,0:T(8,128)(2,1)S(1)} custom-call(s32[26]{0:T(128)S(1)} %concatenate.3.where_ref, bf16[512,1600]{1,0:T(8,128)(2,1)S(1)} %get-tuple-element.60.tap_ref, bf16[1600,2048]{1,0:T(8,128)(2,1)} %weight_ref.3), custom_call_target="tpu_custom_call" | custom-call | flops 1024 | bytes 1024 | tf_op jit(solution)/shard_map/tap_projection/pallas_call | solution.py:334
  32.3 1.9 %kv_projection.1 = (bf16[512,256]{1,0:T(8,128)(2,1)S(1)}, bf16[512,256]{1,0:T(8,128)(2,1)S(1)}, bf16[512,256]{1,0:T(8,128)(2,1)S(1)}, bf16[512,256]{1,0:T(8,128)...) custom-call(s32[26]{0:T(128)S(1)} %concatenate.3.where_ref, ...), custom_call_target="tpu_custom_call" | custom-call | flops 1024 | bytes 1024 | tf_op jit(solution)/shard_map/kv_projection/pallas_call | solution.py:405
  34.8 1.0 %collective-permute-done.11 = bf16[512,256]{1,0:T(8,128)(2,1)S(1)} collective-permute-done((bf16[512,256]{1,0:T(8,128)(2,1)S(1)}, bf16[512,256]{1,0:T(8,128)(2,1)S(1)}, u32[]{:S(2)}, u32[]{:S(2)}) %collective-permute-start.11) | collective-permute-done | bytes 262176 | tf_op jit(solution)/shard_map/ppermute | solution.py:567
  35.9 1.4 %collective-permute-start.14 = (bf16[512,256]{1,0:T(8,128)(2,1)S(1)}, bf16[512,256]{1,0:T(8,128)(2,1)S(1)}, u32[]{:S(2)}, u32[]{:S(2)}) collective-permute-start(bf16[512,256]{1,0:T(8,128)(2,1)S(1)} %add_convert_fusion.3), channel_id=1, source_target_pairs={{0,2},{1,3},{2,0},{3,1},{4,6},{5,7},{6,4},{7,5},{8,10},{9,11},{10,... | collective-permute-start | bytes 786440 | tf_op jit(solution)/shard_map/ppermute | solution.py:567
  37.8 2.6 %prepare.1 = (bf16[512,2048]{1,0:T(8,128)(2,1)S(1)}, s32[24]{0:T(128)S(1)}) custom-call(s32[26]{0:T(128)S(1)} %concatenate.3.where_ref, f32[1,128]{1,0:T(1,128)S(1)} %bitcast.36, bf16[512,2048]{1,0:T(8,128)(2,1)S(1)} %copy-done.1), custom_call_target="tpu_custom_call" | custom-call | flops 1024 | bytes 1024 | tf_op jit(solution)/shard_map/prepare/pallas_call | solution.py:267
  40.4 3.8 %collective-permute-done.14.refs_1_ = bf16[512,256]{1,0:T(8,128)(2,1)S(1)} collective-permute-done((bf16[512,256]{1,0:T(8,128)(2,1)S(1)}, bf16[512,256]{1,0:T(8,128)(2,1)S(1)}, u32[]{:S(2)}, u32[]{:S(2)}) %collective-permute-start.14) | collective-permute-done | bytes 262176 | tf_op jit(solution)/shard_map/ppermute | solution.py:567
  44.3 1.3 %collective-permute-start.15 = (bf16[512,256]{1,0:T(8,128)(2,1)S(1)}, bf16[512,256]{1,0:T(8,128)(2,1)S(1)}, u32[]{:S(2)}, u32[]{:S(2)}) collective-permute-start(bf16[512,256]{1,0:T(8,128)(2,1)S(1)} %add_convert_fusion.1), channel_id=1, source_target_pairs={{0,2},{1,3},{2,0},{3,1},{4,6},{5,7},{6,4},{7,5},{8,10},{9,11},{10,... | collective-permute-start | bytes 786440 | tf_op jit(solution)/shard_map/ppermute | solution.py:567
  46.4 3.6 %collective-permute-start.19 = (bf16[2,128,256]{2,1,0:T(8,128)(2,1)S(1)}, bf16[2,128,256]{2,1,0:T(8,128)(2,1)S(1)}, u32[]{:S(2)}, u32[]{:S(2)}) collective-permute-start(bf16[2,128,256]{2,1,0:T(8,128)(2,1)S(1)} %get-tuple-element.81), channel_id=1, source_target_pairs={{0,12},{4,8},{8,4},{12,0},{1,13},{5,9},{9,5},{13,1},{2,14},{6,10},... | collective-permute-start | bytes 393224 | tf_op jit(solution)/shard_map/ppermute | solution.py:670
  52.5 5.4 %collective-permute-done.21.refs_2_ = bf16[1,128,256]{2,1,0:T(8,128)(2,1)S(1)} collective-permute-done((bf16[1,128,256]{2,1,0:T(8,128)(2,1)S(1)}, bf16[1,128,256]{2,1,0:T(8,128)(2,1)S(1)}, u32[]{:S(2)}, u32[]{:S(2)}) %collective-permute-start.21) | collective-permute-done | bytes 65568 | tf_op jit(solution)/shard_map/ppermute | solution.py:670
  57.9 2.3 %collective-permute-start.22 = (bf16[2,128,256]{2,1,0:T(8,128)(2,1)S(1)}, bf16[2,128,256]{2,1,0:T(8,128)(2,1)S(1)}, u32[]{:S(2)}, u32[]{:S(2)}) collective-permute-start(bf16[2,128,256]{2,1,0:T(8,128)(2,1)S(1)} %get-tuple-element.85), channel_id=1, source_target_pairs={{0,12},{4,8},{8,4},{12,0},{1,13},{5,9},{9,5},{13,1},{2,14},{6,10},... | collective-permute-start | bytes 393224 | tf_op jit(solution)/shard_map/ppermute | solution.py:670
  60.3 2.1 %collective-permute-start.20 = (bf16[1,128,256]{2,1,0:T(8,128)(2,1)S(1)}, bf16[1,128,256]{2,1,0:T(8,128)(2,1)S(1)}, u32[]{:S(2)}, u32[]{:S(2)}) collective-permute-start(bf16[1,128,256]{2,1,0:T(8,128)(2,1)S(1)} %get-tuple-element.82), channel_id=1, source_target_pairs={{0,8},{4,12},{8,0},{12,4},{1,9},{5,13},{9,1},{13,5},{2,10},{6,14},... | collective-permute-start | bytes 196616 | tf_op jit(solution)/shard_map/ppermute | solution.py:670
  62.5 4.8 %collective-permute-done.23.refs_4_ = bf16[1,128,256]{2,1,0:T(8,128)(2,1)S(1)} collective-permute-done((bf16[1,128,256]{2,1,0:T(8,128)(2,1)S(1)}, bf16[1,128,256]{2,1,0:T(8,128)(2,1)S(1)}, u32[]{:S(2)}, u32[]{:S(2)}) %collective-permute-start.23) | collective-permute-done | bytes 65568 | tf_op jit(solution)/shard_map/ppermute | solution.py:670
  67.2 4.2 %attend_head.2.refs_5_ = bf16[512,2048]{1,0:T(8,128)(2,1)} custom-call(s32[24]{0:T(128)S(1)} %get-tuple-element.67.meta_ref, bf16[512,2048]{1,0:T(8,128)(2,1)S(1)} %get-tuple-element.68.query_ref, bf16[2,128,256]{2,1,0:T(8,128)(2,1)S(1)} %get-tuple-element.86.refs_0_, bf16[2,128,256]{2,1,0:T(8,128)(2,1)S(1)} %collective-permute-done.17.refs_1_, ...), custom_call_target="tpu_custom_call" | custom-call | flops 1024 | bytes 1024 | tf_op jit(solution)/shard_map/attend_head/pallas_call | solution.py:526
  71.6 4.1 %collective-permute-done.24.refs_4_ = bf16[1,128,256]{2,1,0:T(8,128)(2,1)S(1)} collective-permute-done((bf16[1,128,256]{2,1,0:T(8,128)(2,1)S(1)}, bf16[1,128,256]{2,1,0:T(8,128)(2,1)S(1)}, u32[]{:S(2)}, u32[]{:S(2)}) %collective-permute-start.24) | collective-permute-done | bytes 65568 | tf_op jit(solution)/shard_map/ppermute | solution.py:670
  75.8 4.2 %attend_head.3 = bf16[512,2048]{1,0:T(8,128)(2,1)} custom-call(s32[24]{0:T(128)S(1)} %get-tuple-element.67.meta_ref, bf16[512,2048]{1,0:T(8,128)(2,1)S(1)} %get-tuple-element.68.query_ref, bf16[2,128,256]{2,1,0:T(8,128)(2,1)S(1)} %get-tuple-element.74.refs_0_, ...), custom_call_target="tpu_custom_call", output_to_operand_aliasing={{}: (7, {})} | custom-call | flops 1024 | bytes 1024 | tf_op jit(solution)/shard_map/attend_head/pallas_call | solution.py:526
  (70 shorter events, 9.9 us)
Async XLA Ops:
  0.9 11.6 %collective-permute-start.1 = (bf16[2,320,128]{2,1,0:T(8,128)(2,1)S(1)}, bf16[2,320,128]{2,1,0:T(8,128)(2,1)S(1)}, u32[]{:S(2)}, u32[]{:S(2)}) collective-permute-start(bf16[2,320,128]{2,1,0:T(8,128)(2,1)S(1)} %slice_bitcast_fusion), channel_id=1, source_target_pairs={{0,2},{1,3},{2,0},{3,1},{4,6},{5,7},{6,4},{7,5},{8,10},{9,11},{10,... | collective-permute-start | bytes 491528 | tf_op jit(solution)/shard_map/ppermute | solution.py:580
  4.0 10.2 %collective-permute-start = (bf16[4,320,128]{2,1,0:T(8,128)(2,1)}, bf16[4,320,128]{2,1,0:T(8,128)(2,1)S(1)}, u32[]{:S(2)}, u32[]{:S(2)}) collective-permute-start(bf16[4,320,128]{2,1,0:T(8,128)(2,1)} %bitcast.22), channel_id=1, source_target_pairs={{0,1},{1,0},{2,3},{3,2},{4,5},{5,4},{6,7},{7,6},{8,9},{9,8},{10,11... | collective-permute-start | bytes 983048 | tf_op jit(solution)/shard_map/ppermute | solution.py:625
  12.5 1.6 %collective-permute-start.2 = (bf16[2,320,128]{2,1,0:T(8,128)(2,1)S(1)}, bf16[2,320,128]{2,1,0:T(8,128)(2,1)S(1)}, u32[]{:S(2)}, u32[]{:S(2)}) collective-permute-start(bf16[2,320,128]{2,1,0:T(8,128)(2,1)S(1)} %collective-permute-done.1.refs_2_), channel_id=1, source_target_pairs={{0,1},{1,0},{2,3},{3,2},{4,5},{5,4},{6,7},{7,6},{8,9},{9,8},{10,11... | collective-permute-start | bytes 491528 | tf_op jit(solution)/shard_map/ppermute | solution.py:584
  13.1 6.2 %collective-permute-start.4 = (bf16[2,320,128]{2,1,0:T(8,128)(2,1)S(1)}, bf16[2,320,128]{2,1,0:T(8,128)(2,1)S(1)}, u32[]{:S(2)}, u32[]{:S(2)}) collective-permute-start(bf16[2,320,128]{2,1,0:T(8,128)(2,1)S(1)} %slice.17), channel_id=1, source_target_pairs={{0,2},{1,3},{2,0},{3,1},{4,6},{5,7},{6,4},{7,5},{8,10},{9,11},{10,... | collective-permute-start | bytes 491528 | tf_op jit(solution)/shard_map/ppermute | solution.py:580
  17.6 2.2 %collective-permute-start.3 = (bf16[320,256]{1,0:T(8,128)(2,1)S(1)}, bf16[320,256]{1,0:T(8,128)(2,1)S(1)}, u32[]{:S(2)}, u32[]{:S(2)}) collective-permute-start(bf16[320,256]{1,0:T(8,128)(2,1)S(1)} %get-tuple-element.52), channel_id=1, source_target_pairs={{0,1},{1,0},{2,3},{3,2},{4,5},{5,4},{6,7},{7,6},{8,9},{9,8},{10,11... | collective-permute-start | bytes 491528 | tf_op jit(solution)/shard_map/ppermute | solution.py:567
  19.3 5.4 %collective-permute-start.7 = (bf16[320,256]{1,0:T(8,128)(2,1)S(1)}, bf16[320,256]{1,0:T(8,128)(2,1)S(1)}, u32[]{:S(2)}, u32[]{:S(2)}) collective-permute-start(bf16[320,256]{1,0:T(8,128)(2,1)S(1)} %get-tuple-element.61), channel_id=1, source_target_pairs={{0,1},{1,0},{2,3},{3,2},{4,5},{5,4},{6,7},{7,6},{8,9},{9,8},{10,11... | collective-permute-start | bytes 491528 | tf_op jit(solution)/shard_map/ppermute | solution.py:567
  19.9 12.3 %collective-permute-start.8 = (bf16[320,256]{1,0:T(8,128)(2,1)S(1)}, bf16[320,256]{1,0:T(8,128)(2,1)S(1)}, u32[]{:S(2)}, u32[]{:S(2)}) collective-permute-start(bf16[320,256]{1,0:T(8,128)(2,1)S(1)} %add_convert_fusion.7), channel_id=1, source_target_pairs={{0,2},{1,3},{2,0},{3,1},{4,6},{5,7},{6,4},{7,5},{8,10},{9,11},{10,... | collective-permute-start | bytes 491528 | tf_op jit(solution)/shard_map/ppermute | solution.py:567
  24.1 7.9 %collective-permute-start.9 = (bf16[320,256]{1,0:T(8,128)(2,1)S(1)}, bf16[320,256]{1,0:T(8,128)(2,1)S(1)}, u32[]{:S(2)}, u32[]{:S(2)}) collective-permute-start(bf16[320,256]{1,0:T(8,128)(2,1)S(1)} %get-tuple-element.63), channel_id=1, source_target_pairs={{0,1},{1,0},{2,3},{3,2},{4,5},{5,4},{6,7},{7,6},{8,9},{9,8},{10,11... | collective-permute-start | bytes 491528 | tf_op jit(solution)/shard_map/ppermute | solution.py:567
  24.3 1.5 %collective-permute-start.6 = (bf16[320,256]{1,0:T(8,128)(2,1)S(1)}, bf16[320,256]{1,0:T(8,128)(2,1)S(1)}, u32[]{:S(2)}, u32[]{:S(2)}) collective-permute-start(bf16[320,256]{1,0:T(8,128)(2,1)S(1)} %get-tuple-element.58), channel_id=1, source_target_pairs={{0,1},{1,0},{2,3},{3,2},{4,5},{5,4},{6,7},{7,6},{8,9},{9,8},{10,11... | collective-permute-start | bytes 491528 | tf_op jit(solution)/shard_map/ppermute | solution.py:567
  25.8 6.4 %collective-permute-start.10 = (bf16[320,256]{1,0:T(8,128)(2,1)S(1)}, bf16[320,256]{1,0:T(8,128)(2,1)S(1)}, u32[]{:S(2)}, u32[]{:S(2)}) collective-permute-start(bf16[320,256]{1,0:T(8,128)(2,1)S(1)} %add_convert_fusion.6), channel_id=1, source_target_pairs={{0,2},{1,3},{2,0},{3,1},{4,6},{5,7},{6,4},{7,5},{8,10},{9,11},{10,... | collective-permute-start | bytes 491528 | tf_op jit(solution)/shard_map/ppermute | solution.py:567
  34.2 1.6 %collective-permute-start.11 = (bf16[512,256]{1,0:T(8,128)(2,1)S(1)}, bf16[512,256]{1,0:T(8,128)(2,1)S(1)}, u32[]{:S(2)}, u32[]{:S(2)}) collective-permute-start(bf16[512,256]{1,0:T(8,128)(2,1)S(1)} %get-tuple-element.65), channel_id=1, source_target_pairs={{0,1},{1,0},{2,3},{3,2},{4,5},{5,4},{6,7},{7,6},{8,9},{9,8},{10,11... | collective-permute-start | bytes 786440 | tf_op jit(solution)/shard_map/ppermute | solution.py:567
  34.3 3.5 %collective-permute-start.13 = (bf16[512,256]{1,0:T(8,128)(2,1)S(1)}, bf16[512,256]{1,0:T(8,128)(2,1)S(1)}, u32[]{:S(2)}, u32[]{:S(2)}) collective-permute-start(bf16[512,256]{1,0:T(8,128)(2,1)S(1)} %get-tuple-element.72), channel_id=1, source_target_pairs={{0,1},{1,0},{2,3},{3,2},{4,5},{5,4},{6,7},{7,6},{8,9},{9,8},{10,11... | collective-permute-start | bytes 786440 | tf_op jit(solution)/shard_map/ppermute | solution.py:567
  35.9 8.4 %collective-permute-start.14 = (bf16[512,256]{1,0:T(8,128)(2,1)S(1)}, bf16[512,256]{1,0:T(8,128)(2,1)S(1)}, u32[]{:S(2)}, u32[]{:S(2)}) collective-permute-start(bf16[512,256]{1,0:T(8,128)(2,1)S(1)} %add_convert_fusion.3), channel_id=1, source_target_pairs={{0,2},{1,3},{2,0},{3,1},{4,6},{5,7},{6,4},{7,5},{8,10},{9,11},{10,... | collective-permute-start | bytes 786440 | tf_op jit(solution)/shard_map/ppermute | solution.py:567
  37.2 8.4 %collective-permute-start.16 = (bf16[512,256]{1,0:T(8,128)(2,1)S(1)}, bf16[512,256]{1,0:T(8,128)(2,1)S(1)}, u32[]{:S(2)}, u32[]{:S(2)}) collective-permute-start(bf16[512,256]{1,0:T(8,128)(2,1)S(1)} %get-tuple-element.77), channel_id=1, source_target_pairs={{0,1},{1,0},{2,3},{3,2},{4,5},{5,4},{6,7},{7,6},{8,9},{9,8},{10,11... | collective-permute-start | bytes 786440 | tf_op jit(solution)/shard_map/ppermute | solution.py:567
  37.2 13.6 %collective-permute-start.12 = (bf16[512,256]{1,0:T(8,128)(2,1)S(1)}, bf16[512,256]{1,0:T(8,128)(2,1)S(1)}, u32[]{:S(2)}, u32[]{:S(2)}) collective-permute-start(bf16[512,256]{1,0:T(8,128)(2,1)S(1)} %get-tuple-element.70), channel_id=1, source_target_pairs={{0,1},{1,0},{2,3},{3,2},{4,5},{5,4},{6,7},{7,6},{8,9},{9,8},{10,11... | collective-permute-start | bytes 786440 | tf_op jit(solution)/shard_map/ppermute | solution.py:567
  44.3 7.5 %collective-permute-start.15 = (bf16[512,256]{1,0:T(8,128)(2,1)S(1)}, bf16[512,256]{1,0:T(8,128)(2,1)S(1)}, u32[]{:S(2)}, u32[]{:S(2)}) collective-permute-start(bf16[512,256]{1,0:T(8,128)(2,1)S(1)} %add_convert_fusion.1), channel_id=1, source_target_pairs={{0,2},{1,3},{2,0},{3,1},{4,6},{5,7},{6,4},{7,5},{8,10},{9,11},{10,... | collective-permute-start | bytes 786440 | tf_op jit(solution)/shard_map/ppermute | solution.py:567
  46.4 13.9 %collective-permute-start.19 = (bf16[2,128,256]{2,1,0:T(8,128)(2,1)S(1)}, bf16[2,128,256]{2,1,0:T(8,128)(2,1)S(1)}, u32[]{:S(2)}, u32[]{:S(2)}) collective-permute-start(bf16[2,128,256]{2,1,0:T(8,128)(2,1)S(1)} %get-tuple-element.81), channel_id=1, source_target_pairs={{0,12},{4,8},{8,4},{12,0},{1,13},{5,9},{9,5},{13,1},{2,14},{6,10},... | collective-permute-start | bytes 393224 | tf_op jit(solution)/shard_map/ppermute | solution.py:670
  50.0 7.9 %collective-permute-start.21 = (bf16[1,128,256]{2,1,0:T(8,128)(2,1)S(1)}, bf16[1,128,256]{2,1,0:T(8,128)(2,1)S(1)}, u32[]{:S(2)}, u32[]{:S(2)}) collective-permute-start(bf16[1,128,256]{2,1,0:T(8,128)(2,1)S(1)} %get-tuple-element.84), channel_id=1, source_target_pairs={{0,8},{4,12},{8,0},{12,4},{1,9},{5,13},{9,1},{13,5},{2,10},{6,14},... | collective-permute-start | bytes 196616 | tf_op jit(solution)/shard_map/ppermute | solution.py:670
  50.0 12.4 %collective-permute-start.17 = (bf16[2,128,256]{2,1,0:T(8,128)(2,1)S(1)}, bf16[2,128,256]{2,1,0:T(8,128)(2,1)S(1)}, u32[]{:S(2)}, u32[]{:S(2)}) collective-permute-start(bf16[2,128,256]{2,1,0:T(8,128)(2,1)S(1)} %get-tuple-element.78), channel_id=1, source_target_pairs={{0,4},{4,0},{8,12},{12,8},{1,5},{5,1},{9,13},{13,9},{2,6},{6,2},{1... | collective-permute-start | bytes 393224 | tf_op jit(solution)/shard_map/ppermute | solution.py:670
  57.9 13.5 %collective-permute-start.22 = (bf16[2,128,256]{2,1,0:T(8,128)(2,1)S(1)}, bf16[2,128,256]{2,1,0:T(8,128)(2,1)S(1)}, u32[]{:S(2)}, u32[]{:S(2)}) collective-permute-start(bf16[2,128,256]{2,1,0:T(8,128)(2,1)S(1)} %get-tuple-element.85), channel_id=1, source_target_pairs={{0,12},{4,8},{8,4},{12,0},{1,13},{5,9},{9,5},{13,1},{2,14},{6,10},... | collective-permute-start | bytes 393224 | tf_op jit(solution)/shard_map/ppermute | solution.py:670
  60.2 7.0 %collective-permute-start.23 = (bf16[1,128,256]{2,1,0:T(8,128)(2,1)S(1)}, bf16[1,128,256]{2,1,0:T(8,128)(2,1)S(1)}, u32[]{:S(2)}, u32[]{:S(2)}) collective-permute-start(bf16[1,128,256]{2,1,0:T(8,128)(2,1)S(1)} %slice.22), channel_id=1, source_target_pairs={{0,4},{4,0},{8,12},{12,8},{1,5},{5,1},{9,13},{13,9},{2,6},{6,2},{1... | collective-permute-start | bytes 196616 | tf_op jit(solution)/shard_map/ppermute | solution.py:670
  60.3 11.1 %collective-permute-start.20 = (bf16[1,128,256]{2,1,0:T(8,128)(2,1)S(1)}, bf16[1,128,256]{2,1,0:T(8,128)(2,1)S(1)}, u32[]{:S(2)}, u32[]{:S(2)}) collective-permute-start(bf16[1,128,256]{2,1,0:T(8,128)(2,1)S(1)} %get-tuple-element.82), channel_id=1, source_target_pairs={{0,8},{4,12},{8,0},{12,4},{1,9},{5,13},{9,1},{13,5},{2,10},{6,14},... | collective-permute-start | bytes 196616 | tf_op jit(solution)/shard_map/ppermute | solution.py:670
  62.4 9.2 %collective-permute-start.18 = (bf16[2,128,256]{2,1,0:T(8,128)(2,1)S(1)}, bf16[2,128,256]{2,1,0:T(8,128)(2,1)S(1)}, u32[]{:S(2)}, u32[]{:S(2)}) collective-permute-start(bf16[2,128,256]{2,1,0:T(8,128)(2,1)S(1)} %get-tuple-element.79), channel_id=1, source_target_pairs={{0,4},{4,0},{8,12},{12,8},{1,5},{5,1},{9,13},{13,9},{2,6},{6,2},{1... | collective-permute-start | bytes 393224 | tf_op jit(solution)/shard_map/ppermute | solution.py:670
  71.4 4.3 %collective-permute-start.24 = (bf16[1,128,256]{2,1,0:T(8,128)(2,1)S(1)}, bf16[1,128,256]{2,1,0:T(8,128)(2,1)S(1)}, u32[]{:S(2)}, u32[]{:S(2)}) collective-permute-start(bf16[1,128,256]{2,1,0:T(8,128)(2,1)S(1)} %slice.21), channel_id=1, source_target_pairs={{0,4},{4,0},{8,12},{12,8},{1,5},{5,1},{9,13},{13,9},{2,6},{6,2},{1... | collective-permute-start | bytes 196616 | tf_op jit(solution)/shard_map/ppermute | solution.py:670
  (11 other events, 63.9 us)
